TPU v7x, 256 devices: a whole 4x4x8 slice. The times are simulated.
256 devices in a mesh: clip: 8 (over x, z_lo), fp: 32 (over y, z_hi, core).
Axes of the slice: x: 4, y: 4, z: 8 (z_hi: 4, z_lo: 2; z = z_hi * 2 + z_lo), core: 2. Of those that a mesh axis runs over, the one named last changes fastest.
Arguments:
- tokens: bfloat16 [8, 64, 128, 768], P('clip', 'fp'), may hold values from -6 to 6
- block_cotangent: bfloat16 [8, 64, 128, 768], P('clip', 'fp'), may hold values from -6 to 6
- time_qkv: bfloat16 [768, 2304], replicated, may hold values from -8 to 8
- time_out: bfloat16 [768, 768], replicated, may hold values from -0.21875 to 0.21875
- space_qkv: bfloat16 [768, 2304], replicated, may hold values from -8 to 8
- space_out: bfloat16 [768, 768], replicated, may hold values from -0.21875 to 0.21875
Outputs:
- block_out: bfloat16 [8, 64, 128, 768], P('clip', 'fp')
- tokens_grad: bfloat16 [8, 64, 128, 768], P('clip', 'fp')
- time_qkv_grad: float32 [768, 2304], P('fp')
- time_out_grad: float32 [768, 768], P('fp')
- space_qkv_grad: float32 [768, 2304], P('fp')
- space_out_grad: float32 [768, 768], P('fp')
All inputs are finite; a program needn't handle non-finite values.
Results may differ from a plain program's by a relative error of at most 0.029.
Values may be sent and summed in bfloat16 or wider, within the bound.
No kernel may reach another device: no remote copies, remote signals or barrier semaphores. Data moves between devices by JAX's collectives and lax.ppermute only.
A program may use at most 128 MiB of HBM per device.

v0:
```python
import jax
import jax.numpy as jnp
from jax import lax
from jax.sharding import PartitionSpec as P

HEAD = 64


TIME_SPECS = ("cqphe,ckphe->cphqk", "cphqk,ckphe->cqphe", "cphqk,cqphe->ckphe")
SPACE_SPECS = ("cfqhe,cfkhe->cfhqk", "cfhqk,cfkhe->cfqhe", "cfhqk,cfqhe->cfkhe")
EPSILON = 1e-06


def product(formula, lhs_rows, rhs_rows):
    return jnp.einsum(formula, lhs_rows, rhs_rows, preferred_element_type=jnp.float32)


def project(matrix_rows, weight):
    flat_rows = matrix_rows.reshape(-1, matrix_rows.shape[-1])
    result = jnp.dot(flat_rows, weight, preferred_element_type=jnp.float32)
    return result.reshape(matrix_rows.shape[:-1] + (weight.shape[1],))


def project_back(matrix_rows, weight):
    flat_rows = matrix_rows.reshape(-1, matrix_rows.shape[-1])
    result = lax.dot_general(
        flat_rows, weight, (((1,), (1,)), ((), ())), preferred_element_type=jnp.float32
    )
    return result.reshape(matrix_rows.shape[:-1] + (weight.shape[0],))


def weight_grad(inputs, cotangent):
    lhs_rows = inputs.reshape(-1, inputs.shape[-1])
    rhs_rows = cotangent.reshape(-1, cotangent.shape[-1])
    return lax.dot_general(
        lhs_rows, rhs_rows, (((0,), (0,)), ((), ())), preferred_element_type=jnp.float32
    )


def normalize(values):
    widened = values.astype(jnp.float32)
    centred = widened - jnp.mean(widened, axis=-1, keepdims=True)
    inverse = lax.rsqrt(jnp.mean(centred * centred, axis=-1, keepdims=True) + EPSILON)
    return (centred * inverse, inverse)


def normalize_back(normed, inverse, grad_normed):
    first_mean = jnp.mean(grad_normed, axis=-1, keepdims=True)
    second_mean = jnp.mean(grad_normed * normed, axis=-1, keepdims=True)
    return inverse * (grad_normed - first_mean - normed * second_mean)


def split_heads(packed):
    leading = packed.shape[:-1]
    model_width = packed.shape[-1] // 3
    heads_view = packed.reshape(leading + (3, model_width // HEAD, HEAD))
    return (heads_view[..., 0, :, :], heads_view[..., 1, :, :], heads_view[..., 2, :, :])


def attend(packed, formulas):
    queries, key_heads, value_heads = split_heads(packed)
    scores = product(formulas[0], queries, key_heads) * HEAD ** (-0.5)
    probabilities = jax.nn.softmax(scores, axis=-1)
    weights = probabilities.astype(jnp.bfloat16)
    mixture = product(formulas[1], weights, value_heads).astype(jnp.bfloat16)
    return (mixture.reshape(packed.shape[:-1] + (packed.shape[-1] // 3,)), probabilities, weights)


def attend_back(packed, probabilities, weights, grad_mixture, formulas):
    queries, key_heads, value_heads = split_heads(packed)
    grad_heads = grad_mixture.reshape(value_heads.shape)
    grad_probs = product(formulas[0], grad_heads, value_heads)
    centred = grad_probs - jnp.sum(grad_probs * probabilities, axis=-1, keepdims=True)
    grad_scores = (probabilities * centred * HEAD ** (-0.5)).astype(jnp.bfloat16)
    grad_queries = product(formulas[1], grad_scores, key_heads)
    grad_keys = product(formulas[2], grad_scores, queries)
    grad_values = product(formulas[2], weights, grad_heads)
    stacked = jnp.stack([grad_queries, grad_keys, grad_values], axis=-3)
    return stacked.reshape(packed.shape).astype(jnp.bfloat16)


def sublayer(stream, qkv_weight, out_weight, formulas):
    normed, inverse = normalize(stream)
    normed_low = normed.astype(jnp.bfloat16)
    packed = project(normed_low, qkv_weight).astype(jnp.bfloat16)
    mixture, probabilities, weights = attend(packed, formulas)
    result = (stream.astype(jnp.float32) + project(mixture, out_weight)).astype(jnp.bfloat16)
    return (result, (normed, inverse, normed_low, packed, probabilities, weights, mixture))


def sublayer_back(grad_result, saved, qkv_weight, out_weight, formulas):
    normed, inverse, normed_low, packed, probabilities, weights, mixture = saved
    out_weight_grad = weight_grad(mixture, grad_result)
    grad_mixture = project_back(grad_result, out_weight).astype(jnp.bfloat16)
    grad_packed = attend_back(packed, probabilities, weights, grad_mixture, formulas)
    qkv_weight_grad = weight_grad(normed_low, grad_packed)
    grad_normed = project_back(grad_packed, qkv_weight)
    grad_stream = grad_result.astype(jnp.float32) + normalize_back(normed, inverse, grad_normed)
    return (grad_stream.astype(jnp.bfloat16), qkv_weight_grad, out_weight_grad)


def to_patches(stream):
    return lax.all_to_all(stream, "fp", split_axis=2, concat_axis=1, tiled=True)


def to_frames(stream):
    return lax.all_to_all(stream, "fp", split_axis=1, concat_axis=2, tiled=True)


def reduce_grads(qkv_part, out_part):
    shares = (
        lax.psum_scatter(
            qkv_part.astype(jnp.bfloat16), "fp", scatter_dimension=0, tiled=True
        ).astype(jnp.float32),
        lax.psum_scatter(
            out_part.astype(jnp.bfloat16), "fp", scatter_dimension=0, tiled=True
        ).astype(jnp.float32),
    )
    return (
        lax.psum(shares[0].astype(jnp.bfloat16), "clip").astype(jnp.float32),
        lax.psum(shares[1].astype(jnp.bfloat16), "clip").astype(jnp.float32),
    )


def on_device(tokens, block_cotangent, time_qkv, time_out, space_qkv, space_out):
    by_patch = to_patches(tokens)
    middle_patch, time_saved = sublayer(by_patch, time_qkv, time_out, TIME_SPECS)
    middle = to_frames(middle_patch)
    block_result, space_saved = sublayer(middle, space_qkv, space_out, SPACE_SPECS)
    grad_middle, space_qkv_part, space_out_part = sublayer_back(
        block_cotangent, space_saved, space_qkv, space_out, SPACE_SPECS
    )
    space_sums = reduce_grads(space_qkv_part, space_out_part)
    grad_patch, time_qkv_part, time_out_part = sublayer_back(
        to_patches(grad_middle), time_saved, time_qkv, time_out, TIME_SPECS
    )
    time_sums = reduce_grads(time_qkv_part, time_out_part)
    tokens_grad = to_frames(grad_patch)
    return (block_result, tokens_grad, time_sums[0], time_sums[1], space_sums[0], space_sums[1])


def solution(mesh):
    return jax.shard_map(
        on_device,
        mesh=mesh,
        in_specs=(P("clip", "fp", None, None), P("clip", "fp", None, None), P(), P(), P(), P()),
        out_specs=(
            P("clip", "fp", None, None),
            P("clip", "fp", None, None),
            P("fp", None),
            P("fp", None),
            P("fp", None),
            P("fp", None),
        ),
        check_vma=False,
    )
```

profile of v0, /device:TPU:8, one launch (start us, length us, event | category | flops | bytes accessed | tf_op | source)
XLA Modules:
  0.0 681.4 jit_solution(8731712124064843324)
XLA Ops:
  8.7 25.3 %all_to_all.51 = bf16[1,2,128,768]{3,1,0,2:T(2,128)(2,1)S(1)} all-to-all(bf16[1,2,128,768]{3,1,0,2:T(2,128)(2,1)S(1)} %copy.212), channel_id=1, replica_groups=mesh['clip'=8,'fp'=32] {'fp'}, dimensions={2} | all-to-all | bytes 786432 | tf_op jit(solution)/shard_map/all_to_all | solution.py:103
  48.1 4.4 convolution_convert_fusion.1
  52.5 4.7 reshape.685
  57.2 3.8 fusion.96
  63.5 4.1 fusion.97
  71.6 7.0 %all-to-all-start.1 = ((bf16[1,64,4,768]{3,2,0,1:T(4,128)(2,1)}), bf16[1,64,4,768]{3,2,0,1:T(4,128)(2,1)}, u32[]{:S(2)}, u32[]{:S(2)}) async-start(bf16[1,64,4,768]{3,2,0,1:T(4,128)(2,1)} %copy.226), calls=%async_computation.1 | async-start | bytes 786432 | tf_op jit(solution)/shard_map/all_to_all | solution.py:107
  83.5 8.9 %all-to-all-done.1 = bf16[1,64,4,768]{3,2,0,1:T(4,128)(2,1)} async-done(((bf16[1,64,4,768]{3,2,0,1:T(4,128)(2,1)}), bf16[1,64,4,768]{3,2,0,1:T(4,128)(2,1)}, u32[]{:S(2)}, u32[]{:S(2)}) %all-to-all-start.1) | async-done | bytes 393248 | tf_op jit(solution)/shard_map/all_to_all | solution.py:107
  105.7 3.3 convolution_convert_fusion
  111.3 3.6 fusion.98
  117.6 4.4 fusion.34
  121.9 4.3 fusion.37
  126.3 2.9 convolution_bitcast_fusion.1
  146.3 2.9 fusion.95
  150.6 6.5 all-to-all-start.2
  159.4 11.4 %all-to-all-done.2 = bf16[1,2,128,768]{3,1,0,2:T(2,128)(2,1)S(1)} async-done(((bf16[1,2,128,768]{3,1,0,2:T(2,128)(2,1)}), bf16[1,2,128,768]{3,1,0,2:T(2,128)(2,1)S(1)}, u32[]{:S(2)}, u32[]{:S(2)}) %all-to-all-start.2) | async-done | bytes 393248 | tf_op jit(solution)/shard_map/all_to_all | solution.py:103
  175.7 2.9 bitcast_convert_fusion
  178.7 8.9 %reduce-scatter.5.cloned.1.call-start = ((), (), s32[]{:S(2)}) async-start(), calls=%async_computation.8 | async-start | bytes 3649536 | tf_op jit(solution)/shard_map/reduce_scatter | solution.py:112
  190.6 3.9 fusion.26
  194.5 3.9 fusion.29
  201.1 3.6 copy.268
  204.7 4.8 convert_element_type.339
  209.6 4.2 bitcast_convert_fusion.1
  218.4 3.7 copy.260
  222.2 3.9 convert_element_type.332
  226.0 3.3 fusion.94
  231.7 7.1 %all-to-all-start.3 = ((bf16[1,64,4,768]{3,2,0,1:T(4,128)(2,1)}), bf16[1,64,4,768]{3,2,0,1:T(4,128)(2,1)}, u32[]{:S(2)}, u32[]{:S(2)}) async-start(bf16[1,64,4,768]{3,2,0,1:T(4,128)(2,1)} %fusion.51), calls=%async_computation.3 | async-start | bytes 786432 | tf_op jit(solution)/shard_map/all_to_all | solution.py:107
  238.9 81.7 %reduce-scatter.7.cloned.1.call-done = bf16[24,768]{1,0:T(8,128)(2,1)} async-done(((bf16[768,768]{1,0:T(8,128)(2,1)}), bf16[24,768]{1,0:T(8,128)(2,1)}) %reduce-scatter.7.cloned.1.call-update) | async-done | bytes 36880 | tf_op jit(solution)/shard_map/reduce_scatter | solution.py:115
  320.6 97.9 %reduce-scatter.9.cloned.1.call-done = bf16[24,2304]{1,0:T(8,128)(2,1)} async-done(((bf16[768,2304]{1,0:T(8,128)(2,1)}), bf16[24,2304]{1,0:T(8,128)(2,1)}) %reduce-scatter.9.cloned.1.call-update) | async-done | bytes 110608 | tf_op jit(solution)/shard_map/reduce_scatter | solution.py:112
  418.5 98.0 %reduce-scatter.5.cloned.1.call-done = bf16[24,2304]{1,0:T(8,128)(2,1)} async-done(((bf16[768,2304]{1,0:T(8,128)(2,1)}), bf16[24,2304]{1,0:T(8,128)(2,1)}) %reduce-scatter.5.cloned.1.call-update) | async-done | bytes 110608 | tf_op jit(solution)/shard_map/reduce_scatter | solution.py:112
  516.5 3.0 fusion.43
  523.2 68.3 %all-reduce.5.cloned.1.call-done = (bf16[24,768]{1,0:T(8,128)(2,1)}, bf16[24,768]{1,0:T(8,128)(2,1)}) async-done(((bf16[24,768]{1,0:T(8,128)(2,1)}, bf16[24,768]{1,0:T(8,128)(2,1)}), (bf16[24,768]{1,0:T(8,128)(2,1)}, bf16[24,768]{1,0:T(8,128)(2,1)})) %all-reduce.5.cloned.1.call-update) | async-done | bytes 73744 | tf_op jit(solution)/shard_map/psum | solution.py:121
  594.4 76.8 %all-reduce.7.cloned.1.call-done = (bf16[24,2304]{1,0:T(8,128)(2,1)}, bf16[24,2304]{1,0:T(8,128)(2,1)}) async-done(((bf16[24,2304]{1,0:T(8,128)(2,1)}, bf16[24,2304]{1,0:T(8,128)(2,1)}), (bf16[24,2304]{1,0:T(8,128)(2,1)}, bf16[24,2304]{1,0:T(8,128)(2,1)})) %all-reduce.7.cloned.1.call-update) | async-done | bytes 221200 | tf_op jit(solution)/shard_map/psum | solution.py:120
  (153 shorter events, 93.3 us)
Async XLA Ops:
  7.2 98.5 %copy-start = (bf16[768,2304]{1,0:T(8,128)(2,1)S(1)}, bf16[768,2304]{1,0:T(8,128)(2,1)}, u32[]{:S(2)}) copy-start(bf16[768,2304]{1,0:T(8,128)(2,1)} %param.10) | copy-start | bytes 10616836
  67.5 2.1 copy-start.16
  67.6 2.2 copy-start.17
  71.6 20.9 %all-to-all-start.1 = ((bf16[1,64,4,768]{3,2,0,1:T(4,128)(2,1)}), bf16[1,64,4,768]{3,2,0,1:T(4,128)(2,1)}, u32[]{:S(2)}, u32[]{:S(2)}) async-start(bf16[1,64,4,768]{3,2,0,1:T(4,128)(2,1)} %copy.226), calls=%async_computation.1 | async-start | bytes 786432 | tf_op jit(solution)/shard_map/all_to_all | solution.py:107
  78.6 160.2 %reduce-scatter.11.cloned.1.call-start = ((), (), s32[]{:S(2)}) async-start(), calls=%async_computation.11 | async-start | bytes 1216512 | tf_op jit(solution)/shard_map/reduce_scatter | solution.py:115
  97.9 2.3 copy-start.3
  132.7 2.7 copy-start.26
  132.8 2.7 copy-start.27
  132.8 2.7 copy-start.28
  146.2 2.9 copy-start.11
  146.2 2.9 copy-start.12
  149.2 8.0 %copy-start.15 = (bf16[4,12,64,64]{3,2,1,0:T(8,128)(2,1)S(1)}, bf16[4,12,64,64]{3,2,1,0:T(8,128)(2,1)}, u32[]{:S(2)}) copy-start(bf16[4,12,64,64]{3,2,1,0:T(8,128)(2,1)} %copy-done.14) | copy-start | bytes 1179652
  150.6 20.2 %all-to-all-start.2 = ((bf16[1,2,128,768]{3,1,0,2:T(2,128)(2,1)}), bf16[1,2,128,768]{3,1,0,2:T(2,128)(2,1)S(1)}, u32[]{:S(2)}, u32[]{:S(2)}) async-start(bf16[1,2,128,768]{3,1,0,2:T(2,128)(2,1)} %copy.249), calls=%async_computation.2 | async-start | bytes 786432 | tf_op jit(solution)/shard_map/all_to_all | solution.py:103
  157.1 163.4 %reduce-scatter.7.cloned.1.call-start = ((), (), s32[]{:S(2)}) async-start(), calls=%async_computation.9 | async-start | bytes 1216512 | tf_op jit(solution)/shard_map/reduce_scatter | solution.py:115
  171.1 2.4 copy-start.6
  172.7 1.2 copy-start.4
  172.7 245.8 %reduce-scatter.9.cloned.1.call-start = ((), (), s32[]{:S(2)}) async-start(), calls=%async_computation.10 | async-start | bytes 3649536 | tf_op jit(solution)/shard_map/reduce_scatter | solution.py:112
  178.6 8.9 %copy-start.8 = (bf16[1,2,128,768]{3,1,0,2:T(2,128)(2,1)S(1)}, bf16[1,2,128,768]{3,1,0,2:T(2,128)(2,1)}, u32[]{:S(2)}) copy-start(bf16[1,2,128,768]{3,1,0,2:T(2,128)(2,1)} %copy-done.7) | copy-start | bytes 1179652
  178.6 9.0 %copy-start.20 = (f32[32,2,4]{1,0,2:T(8,128)S(1)}, f32[32,2,4]{1,0,2:T(8,128)}, u32[]{:S(2)}) copy-start(f32[32,2,4]{1,0,2:T(8,128)} %copy-done.19) | copy-start | bytes 3076
  178.6 9.0 %copy-start.23 = (f32[32,2,4]{1,0,2:T(8,128)S(1)}, f32[32,2,4]{1,0,2:T(8,128)}, u32[]{:S(2)}) copy-start(f32[32,2,4]{1,0,2:T(8,128)} %add_rsqrt_fusion) | copy-start | bytes 3076
  178.7 10.3 %copy-start.18 = (bf16[768,768]{1,0:T(8,128)(2,1)S(1)}, bf16[768,768]{1,0:T(8,128)(2,1)}, u32[]{:S(2)}) copy-start(bf16[768,768]{1,0:T(8,128)(2,1)} %param.9) | copy-start | bytes 3538948
  178.7 337.8 %reduce-scatter.5.cloned.1.call-start = ((), (), s32[]{:S(2)}) async-start(), calls=%async_computation.8 | async-start | bytes 3649536 | tf_op jit(solution)/shard_map/reduce_scatter | solution.py:112
  190.5 4.0 copy-start.31
  198.4 2.1 copy-start.21
  198.4 2.1 copy-start.22
  204.7 4.8 copy-start.29
  213.8 1.8 copy-start.9
  229.3 1.1 copy-start.10
  231.7 287.8 %all-to-all-start.3 = ((bf16[1,64,4,768]{3,2,0,1:T(4,128)(2,1)}), bf16[1,64,4,768]{3,2,0,1:T(4,128)(2,1)}, u32[]{:S(2)}, u32[]{:S(2)}) async-start(bf16[1,64,4,768]{3,2,0,1:T(4,128)(2,1)} %fusion.51), calls=%async_computation.3 | async-start | bytes 786432 | tf_op jit(solution)/shard_map/all_to_all | solution.py:107
  238.8 352.8 %all-reduce.5.cloned.1.call-start = ((), (), s32[]{:S(2)}) async-start(), calls=%async_computation.12 | async-start | bytes 147456 | tf_op jit(solution)/shard_map/psum | solution.py:121
  320.6 350.6 %all-reduce.7.cloned.1.call-start = ((), (), s32[]{:S(2)}) async-start(), calls=%async_computation.13 | async-start | bytes 442368 | tf_op jit(solution)/shard_map/psum | solution.py:120
  516.5 157.9 %copy-start.1 = (bf16[768,2304]{1,0:T(8,128)(2,1)S(1)}, bf16[768,2304]{1,0:T(8,128)(2,1)}, u32[]{:S(2)}) copy-start(bf16[768,2304]{1,0:T(8,128)(2,1)} %param.10) | copy-start | bytes 10616836
  (9 other events, 8.4 us)
Sparse Core Ops, SparseCore 0:
  146.4 84.6 reduce-scatter.10
  234.9 85.5 reduce-scatter.6
  324.6 93.9 reduce-scatter.8
  422.4 94.0 reduce-scatter.4
  519.0 72.4 all-reduce.4
  594.3 76.8 all-reduce.6
where the time goes:
time: 693 us; the launch traced here: 681 us
  waiting for transfers between devices  443 us (64%)
  local copies, waits for them, and re-layouts  79.7 us (12%)
  matrix products  68.7 us (10%)
  starting transfers between devices  30 us (4%)
  blocking collectives  25.3 us (4%)
  other arithmetic  19.7 us (3%)
  between operations  14.8 us (2%)
    reduce_scatter x2, waiting for transfers between devices, reduce_grads(): lax.psum_scatter(qkv_part.astype(jnp.bfloat16), 'fp', scatter_dimension=0...  196 us
    reduce_scatter x2, waiting for transfers between devices, reduce_grads(): lax.psum_scatter(out_part.astype(jnp.bfloat16), 'fp', scatter_dimension=0...  81.7 us
    psum x1, waiting for transfers between devices, reduce_grads(): lax.psum(shares[0].astype(jnp.bfloat16), 'clip').astype(jnp.float32)  76.8 us
    psum x1, waiting for transfers between devices, reduce_grads(): lax.psum(shares[1].astype(jnp.bfloat16), 'clip').astype(jnp.float32)  68.3 us
    dot_general x10, matrix products, product(): jnp.einsum(formula, lhs_rows, rhs_rows, preferred_element_type=jnp.float32)  29.5 us
    all_to_all x1, blocking collectives, to_patches(): return lax.all_to_all(stream, 'fp', split_axis=2, concat_axis=1, tiled=True)  25.3 us
    convert_element_type x6, local copies, waits for them, and re-layouts, attend_back(): return stacked.reshape(packed.shape).astype(jnp.bfloat16)  18.4 us
    all_to_all x2, starting transfers between devices, to_frames(): return lax.all_to_all(stream, 'fp', split_axis=1, concat_axis=2, tiled=True)  14.1 us
  transfers between devices with their start and end apart: 9, of which 7 were waited for; matrix products, arithmetic and copies ran while one was open for 10% of the time, Pallas kernels for 0%

commit v1 on v0

v1 whole, which is shorter than its diff:
```python
import functools

import jax
import jax.numpy as jnp
from jax import lax
from jax.experimental import pallas as pl
from jax.experimental.pallas import tpu as pltpu
from jax.sharding import Mesh, PartitionSpec as P

D = 768
HEAD = 64
PAIR = 2 * HEAD
PAIRS = D // PAIR
T = 256
ROWS = 24
HALF = D // 2
EPSILON = 1e-06
SCALE = HEAD ** (-0.5)
BF = jnp.bfloat16
F32 = jnp.float32

FP = ("y", "zh", "c")
CLIP = ("x", "zl")

NN = (((1,), (0,)), ((), ()))
NT = (((1,), (1,)), ((), ()))
TN = (((0,), (0,)), ((), ()))


def dot(a, b, dims=NN):
    return lax.dot_general(a, b, dims, preferred_element_type=F32)


def normalize(x):
    centred = x - jnp.mean(x, axis=-1, keepdims=True)
    inverse = lax.rsqrt(jnp.mean(centred * centred, axis=-1, keepdims=True) + EPSILON)
    return centred * inverse, inverse


def normalize_back(normed, inverse, grad):
    first = jnp.mean(grad, axis=-1, keepdims=True)
    second = jnp.mean(grad * normed, axis=-1, keepdims=True)
    return inverse * (grad - first - normed * second)


def iota(shape, dim):
    return lax.broadcasted_iota(jnp.int32, shape, dim)


def order(to_sent):
    sent = iota((T, T), 0 if to_sent else 1)
    natural = iota((T, T), 1 if to_sent else 0)
    source = ((sent // 4) % 2) * 128 + (sent // 8) * 4 + sent % 4
    return jnp.where(source == natural, 1.0, 0.0).astype(BF)


def chosen_rows(core):
    row = iota((HALF, D), 0)
    feature = (row // ROWS) * (2 * ROWS) + core * ROWS + row % ROWS
    return jnp.where(iota((HALF, D), 1) == feature, 1.0, 0.0).astype(BF)


def lanes(rows):
    low = iota((rows, PAIR), 1) < HEAD
    zero = jnp.zeros((rows, PAIR), BF)
    return lambda a, odd: jnp.where(low, zero, a) if odd else jnp.where(low, a, zero)


def same_patch():
    return (iota((T, T), 0) % 4) == (iota((T, T), 1) % 4)


def permute_kernel(to_sent, x_ref, o_ref):
    o_ref[...] = dot(order(to_sent), x_ref[...]).astype(BF)


def time_forward_kernel(core_ref, x_ref, wq_ref, wo_ref, middle_ref, qkv_ref, own_ref, send_ref, mixed_ref):
    x = x_ref[...].astype(F32)
    normed, _ = normalize(x)
    normed = normed.astype(BF)
    for i in range(9):
        cols = slice(i * 256, (i + 1) * 256)
        qkv_ref[:, cols] = dot(normed, wq_ref[:, cols]).astype(BF)
    keep = lanes(T)
    near = same_patch()
    for p in range(PAIRS):
        q = qkv_ref[:, p * PAIR:(p + 1) * PAIR]
        k = qkv_ref[:, D + p * PAIR:D + (p + 1) * PAIR]
        v = qkv_ref[:, 2 * D + p * PAIR:2 * D + (p + 1) * PAIR]
        weights = []
        values = []
        for odd in (False, True):
            s = dot(keep(q, odd), k, NT)
            s = jnp.where(near, s, -1e30)
            e = jnp.exp((s - jnp.max(s, axis=1, keepdims=True)) * SCALE)
            weights.append((e / jnp.sum(e, axis=1, keepdims=True)).astype(BF))
            values.append(keep(v, odd))
        mixed = dot(jnp.concatenate(weights, axis=1), jnp.concatenate(values, axis=0))
        mixed_ref[:, p * PAIR:(p + 1) * PAIR] = mixed.astype(BF)
    mixed = mixed_ref[...]
    middle_ref[...] = (x + dot(mixed, wo_ref[...])).astype(BF)
    core = core_ref[0]
    for ref, which in ((own_ref, core), (send_ref, 1 - core)):
        pick = chosen_rows(which)
        ref[0] = dot(pick, normed, NT).astype(BF)
        ref[1] = dot(pick, mixed, NT).astype(BF)


def probs_back(q, k, v, g, near):
    s = dot(k, q, NT)
    if near is not None:
        s = jnp.where(near, s, -1e30)
    e = jnp.exp((s - jnp.max(s, axis=0, keepdims=True)) * SCALE)
    probs = e / jnp.sum(e, axis=0, keepdims=True)
    dprobs = dot(v, g, NT)
    delta = jnp.sum(dprobs * probs, axis=0, keepdims=True)
    return probs.astype(BF), (probs * (dprobs - delta) * SCALE).astype(BF)


def attend_back(qkv_ref, g_ref, dqkv_ref, mixed_ref, near, blocks):
    size = T // blocks
    keep = lanes(size)
    for p in range(PAIRS):
        for b in range(blocks):
            rows = slice(b * size, (b + 1) * size)
            at = [slice(i * D + p * PAIR, i * D + (p + 1) * PAIR) for i in range(3)]
            q, k, v = (qkv_ref[rows, at[i]] for i in range(3))
            g = g_ref[rows, at[0]]
            qs, ks, vs, gs, ws, ds = [], [], [], [], [], []
            for odd in (False, True):
                q1, k1, v1, g1 = (keep(a, odd) for a in (q, k, v, g))
                w, d = probs_back(q, k1, v1, g, near)
                for into, a in ((qs, q1), (ks, k1), (vs, v1), (gs, g1), (ws, w), (ds, d)):
                    into.append(a)
            qs, ks, vs, gs = (jnp.concatenate(a, axis=0) for a in (qs, ks, vs, gs))
            dqkv_ref[rows, at[1]] = dot(jnp.concatenate(ds, axis=1), qs).astype(BF)
            dqkv_ref[rows, at[2]] = dot(jnp.concatenate(ws, axis=1), gs).astype(BF)
            dqkv_ref[rows, at[0]] = dot(jnp.concatenate(ds, axis=0), ks, TN).astype(BF)
            if mixed_ref is not None:
                mixed_ref[rows, at[0]] = dot(jnp.concatenate(ws, axis=0), vs, TN).astype(BF)


def space_kernel(
    core_ref, m_ref, cot_ref, wq_ref, wo_ref,
    out_ref, grad_ref, dqkv_ref, own_ref, send_ref,
    x_ref, qkv_ref, g_ref, mixed_ref,
):
    x_ref[...] = dot(order(False), m_ref[...]).astype(BF)
    normed, inverse = normalize(x_ref[...].astype(F32))
    low = normed.astype(BF)
    for i in range(9):
        cols = slice(i * 256, (i + 1) * 256)
        qkv_ref[:, cols] = dot(low, wq_ref[:, cols]).astype(BF)
    cot = cot_ref[...]
    g_ref[...] = dot(cot, wo_ref[...], NT).astype(BF)
    attend_back(qkv_ref, g_ref, dqkv_ref, mixed_ref, None, 2)
    grad = dot(dqkv_ref[...], wq_ref[...], NT)
    grad = cot.astype(F32) + normalize_back(normed, inverse, grad)
    grad_ref[...] = dot(order(True), grad.astype(BF)).astype(BF)
    mixed = mixed_ref[...]
    out_ref[...] = (x_ref[...].astype(F32) + dot(mixed, wo_ref[...])).astype(BF)
    core = core_ref[0]
    for ref, which in ((own_ref, core), (send_ref, 1 - core)):
        pick = chosen_rows(which)
        ref[0] = dot(pick, low, NT).astype(BF)
        ref[1] = dot(pick, mixed, NT).astype(BF)


def time_backward_kernel(x_ref, gm_ref, qkv_ref, wq_ref, wo_ref, grad_ref, dqkv_ref, g_ref):
    gm = gm_ref[...]
    g_ref[...] = dot(gm, wo_ref[...], NT).astype(BF)
    attend_back(qkv_ref, g_ref, dqkv_ref, None, same_patch(), 1)
    normed, inverse = normalize(x_ref[...].astype(F32))
    grad = dot(dqkv_ref[...], wq_ref[...], NT)
    grad_ref[...] = (gm.astype(F32) + normalize_back(normed, inverse, grad)).astype(BF)


def weights_kernel(l_ref, l2_ref, d_ref, d2_ref, g_ref, g2_ref, o_ref):
    for which in range(2):
        left = jnp.concatenate([l_ref[which], l2_ref[which]], axis=1)
        a, b = ((d_ref, d2_ref), (g_ref, g2_ref))[which]
        for j in range(a.shape[1] // HALF):
            cols = slice(j * HALF, (j + 1) * HALF)
            right = jnp.concatenate([a[:, cols], b[:, cols]], axis=0)
            o_ref[which * 6 + j] = dot(left, right).astype(BF)


def sds(*shape):
    return jax.ShapeDtypeStruct(shape, BF)


SMEM = pl.BlockSpec(memory_space=pltpu.SMEM)
VMEM = pl.BlockSpec(memory_space=pltpu.VMEM)


def call(kernel, outs, args, flops, scratch=(), name=None):
    moved = sum(a.size * a.dtype.itemsize for a in args) + 2 * sum(o.size for o in outs)
    return pl.pallas_call(
        kernel,
        out_shape=outs,
        in_specs=[SMEM if a.dtype == jnp.int32 else VMEM for a in args],
        out_specs=[VMEM] * len(outs),
        scratch_shapes=scratch,
        compiler_params=pltpu.CompilerParams(vmem_limit_bytes=48 * 2**20),
        cost_estimate=pl.CostEstimate(flops=flops, bytes_accessed=moved, transcendentals=0),
        name=name,
    )(*args)


PROJ = 2 * T * D * 3 * D
OUTP = 2 * T * D * D


def permuted(x, to_sent):
    return call(functools.partial(permute_kernel, to_sent), [sds(T, D)], [x], 2 * T * T * D)[0]


def a2a(x, axes):
    return lax.all_to_all(x, axes, 0, 0, tiled=True)


def swap(x):
    return lax.ppermute(x, "c", [(0, 1), (1, 0)])


def first_stage(left_own, left_other, d, d2, g, g2):
    partial = call(weights_kernel, [sds(8, HALF, HALF)], [left_own, left_other, d, d2, g, g2], 2 * 512 * HALF * 4 * D)[0]
    got = a2a(partial.reshape(32, HALF // 4, HALF), ("x", "zl", "y"))
    return jnp.sum(got.astype(F32), axis=0).astype(BF)


def last_stages(parts):
    both = jnp.concatenate(parts, axis=1).reshape(4, ROWS, D)
    share = jnp.sum(a2a(both, ("zh",)).astype(F32), axis=0).astype(BF)
    got = a2a(jnp.broadcast_to(share[None], (8, ROWS, D)), CLIP)
    got = got.reshape(8, ROWS, 2, HALF).transpose(2, 1, 0, 3).reshape(2, ROWS, 4 * D).astype(F32)
    return [got[0, :, :3 * D], got[0, :, 3 * D:], got[1, :, :3 * D], got[1, :, 3 * D:]]


def on_device(tokens, block_cotangent, time_qkv, time_out, space_qkv, space_out):
    core = lax.axis_index("c").astype(jnp.int32).reshape(1)
    cot = block_cotangent.reshape(T, D)
    cot_other = swap(cot)
    x = a2a(permuted(tokens.reshape(T, D), True), FP)
    middle, t_qkv, t_own, t_send = call(
        time_forward_kernel,
        [sds(T, D), sds(T, 3 * D), sds(2, HALF, T), sds(2, HALF, T)],
        [core, x, time_qkv, time_out],
        PROJ + OUTP, [pltpu.VMEM((T, D), BF)],
    )
    middle = a2a(middle, FP)
    t_other = swap(t_send)
    block_out, grad_middle, s_dqkv, s_own, s_send = call(
        space_kernel,
        [sds(T, D), sds(T, D), sds(T, 3 * D), sds(2, HALF, T), sds(2, HALF, T)],
        [core, middle, cot, space_qkv, space_out],
        2 * (PROJ + OUTP),
        [pltpu.VMEM((T, D), BF), pltpu.VMEM((T, 3 * D), BF), pltpu.VMEM((T, D), BF), pltpu.VMEM((T, D), BF)],
    )
    grad_middle = a2a(grad_middle, FP)
    space_part = first_stage(s_own, swap(s_send), s_dqkv, swap(s_dqkv), cot, cot_other)
    grad_middle_other = swap(grad_middle)
    grad_tokens, t_dqkv = call(
        time_backward_kernel,
        [sds(T, D), sds(T, 3 * D)],
        [x, grad_middle, t_qkv, time_qkv, time_out],
        PROJ + OUTP, [pltpu.VMEM((T, D), BF)],
    )
    time_part = first_stage(t_own, t_other, t_dqkv, swap(t_dqkv), grad_middle, grad_middle_other)
    tokens_grad = permuted(a2a(grad_tokens, FP), False)
    sums = last_stages([time_part, space_part])
    shape = tokens.shape
    return (block_out.reshape(shape), tokens_grad.reshape(shape), *sums)


def solution(mesh):
    fine = Mesh(mesh.devices.reshape(4, 2, 4, 4, 2), ("x", "zl", "y", "zh", "c"))
    activations = P(CLIP, FP, None, None)
    return jax.shard_map(
        on_device,
        mesh=fine,
        in_specs=(activations, activations, P(), P(), P(), P()),
        out_specs=(activations, activations, P(FP, None), P(FP, None), P(FP, None), P(FP, None)),
        check_vma=False,
    )
```

time: 693 us -> 216 us (0.31); the launches traced: 681 us -> 213 us
  waiting for transfers between devices: 443 us -> 93.5 us
  local copies, waits for them, and re-layouts: 79.7 us -> 7.12 us
  matrix products: 68.7 us -> 0 us
  Pallas kernels: 0 us -> 36.6 us
  other arithmetic: 19.7 us -> 2.38 us
  between operations: 14.8 us -> 0.8 us
  starting transfers between devices: 30 us -> 42.2 us
    reduce_scatter x4 -> x0, waiting for transfers between devices: 278 us -> none  [the longest x2 196 us: reduce_grads(): lax.psum_scatter(qkv_part.astype(jnp.bfloat16), 'fp', scatter_dimension=0...]
    psum x2 -> x0, waiting for transfers between devices: 145 us -> none  [the longest x1 76.8 us: reduce_grads(): lax.psum(shares[0].astype(jnp.bfloat16), 'clip').astype(jnp.float32)]
    all_to_all x3 -> x6, waiting for transfers between devices: 20.4 us -> 88.2 us  [a2a(): return lax.all_to_all(x, axes, 0, 0, tiled=True)]
    dot_general x22 -> x0, matrix products: 61.1 us -> none  [the longest x10 29.5 us: product(): jnp.einsum(formula, lhs_rows, rhs_rows, preferred_element_type=jnp.float32)]
    convert_element_type x19 -> x3, local copies, waits for them, and re-layouts: 40.3 us -> 0.6 us  [last_stages(): got.reshape(8, ROWS, 2, HALF).transpose(2, 1, 0, 3).reshape(2, ROWS, 4 * D)]
    pallas_call x0 -> x7, Pallas kernels: none -> 36.6 us  [call(): pl.pallas_call(kernel, out_shape=outs, in_specs=[SMEM if a.dtype == jnp.i...]
    all_to_all x3 -> x6, starting transfers between devices: 20.6 us -> 39.6 us  [a2a(): return lax.all_to_all(x, axes, 0, 0, tiled=True)]
    convert_element_type x12 -> x0, other arithmetic: 13.4 us -> none  [the longest x2 3.25 us: sublayer(): stream.astype(jnp.float32) + project(mixture, out_weight)]
  transfers between devices with their start and end apart: 9 -> 12, of which waited for: 7 -> 10; matrix products, arithmetic and copies ran while one was open for 10% -> 1% of each run, Pallas kernels for 0% -> 8%
where the time goes in v1:
time: 216 us; the launch traced here: 213 us
  waiting for transfers between devices  93.5 us (43%)
  starting transfers between devices  42.2 us (20%)
  Pallas kernels  36.6 us (17%)
  blocking collectives  30.7 us (14%)
  local copies, waits for them, and re-layouts  7.12 us (3%)
  other arithmetic  2.38 us (1%)
    all_to_all x6, waiting for transfers between devices, a2a(): return lax.all_to_all(x, axes, 0, 0, tiled=True)  88.2 us
    all_to_all x6, starting transfers between devices, a2a(): return lax.all_to_all(x, axes, 0, 0, tiled=True)  39.6 us
    pallas_call x7, Pallas kernels, call(): pl.pallas_call(kernel, out_shape=outs, in_specs=[SMEM if a.dtype == jnp.i...  36.6 us
    all_to_all x2, blocking collectives, a2a(): return lax.all_to_all(x, axes, 0, 0, tiled=True)  30.7 us
    ppermute x6, waiting for transfers between devices, swap(): return lax.ppermute(x, 'c', [(0, 1), (1, 0)])  5.26 us
    unnamed x24, local copies, waits for them, and re-layouts  4.34 us
  transfers between devices with their start and end apart: 12, of which 10 were waited for; matrix products, arithmetic and copies ran while one was open for 1% of the time, Pallas kernels for 8%

profile of v1, /device:TPU:8, one launch (start us, length us, event | category | flops | bytes accessed | tf_op | source)
XLA Modules:
  0.0 213.2 jit_solution(3993016428457261938)
XLA Ops:
  0.7 1.1 copy-done.6
  1.7 1.0 shard_map.109
  2.8 11.7 %all-to-all-start = ((bf16[32,8,768]{2,1,0:T(8,128)(2,1)}), bf16[32,8,768]{2,1,0:T(8,128)(2,1)S(1)}, u32[]{:S(2)}, u32[]{:S(2)}) async-start(bf16[32,8,768]{2,1,0:T(8,128)(2,1)} %bitcast.2), calls=%async_computation | async-start | bytes 786432 | tf_op jit(solution)/shard_map/all_to_all | solution.py:219
  14.5 13.8 %all-to-all-done = bf16[32,8,768]{2,1,0:T(8,128)(2,1)S(1)} async-done(((bf16[32,8,768]{2,1,0:T(8,128)(2,1)}), bf16[32,8,768]{2,1,0:T(8,128)(2,1)S(1)}, u32[]{:S(2)}, u32[]{:S(2)}) %all-to-all-start) | async-done | bytes 393248 | tf_op jit(solution)/shard_map/all_to_all | solution.py:219
  28.2 6.9 %shard_map.110 = (bf16[256,768]{1,0:T(8,128)(2,1)S(1)}, bf16[256,2304]{1,0:T(8,128)(2,1)S(1)}, bf16[2,384,256]{2,1,0:T(8,128)(2,1)S(1)}, bf16[2,384,256]{2,1,0:T(8,128)(2,1)S(1)}) custom-call(s32[1]{0:T(128)} %bitcast.core_ref, bf16[256,768]{1,0:T(8,128)(2,1)S(1)} %bitcast.30, bf16[768,2304]{1,0:T(8,128)(2,1)} %wq_ref.5, bf16[768,768]{1,0:T(8,128)(2,1)S(1)} %copy-done), custom_call_target="tpu_custom_call" | custom-call | flops 1207959552 | bytes 7471108 | tf_op jit(solution)/shard_map/pallas_call | solution.py:198
  35.2 19.5 %all_to_all.64 = bf16[32,8,768]{2,1,0:T(8,128)(2,1)S(1)} all-to-all(bf16[32,8,768]{2,1,0:T(8,128)(2,1)S(1)} %bitcast.39), channel_id=1, replica_groups=mesh['x'=4,'zl'=2,'y'=4,'zh'=4,'c'=2] {'y','zh','c'}, dimensions={0} | all-to-all | bytes 786432 | tf_op jit(solution)/shard_map/all_to_all | solution.py:219
  54.6 11.2 %shard_map.111 = (bf16[256,768]{1,0:T(8,128)(2,1)}, bf16[256,768]{1,0:T(8,128)(2,1)S(1)}, bf16[256,2304]{1,0:T(8,128)(2,1)}, bf16[2,384,256]{2,1,0:T(8,128)(2,1)S(1)}, bf16[2,384,256]{2,1,0:T(8,128)(2,1)S(1)}) custom-call(s32[1]{0:T(128)} %bitcast.core_ref, bf16[256,768]{1,0:T(8,128)(2,1)S(1)} %bitcast.38, bf16[256,768]{1,0:T(8,128)(2,1)S(1)} %bitcast.33, ...), custom_call_target="tpu_custom_call" | custom-call | flops 2415919104 | bytes 8257540 | tf_op jit(solution)/shard_map/pallas_call | solution.py:198
  65.9 0.7 copy-done.4
  66.6 0.7 copy-done.7
  67.3 0.7 copy-done.11
  68.1 1.3 collective-permute-start.4
  69.4 5.1 %all-to-all-start.2 = ((bf16[32,8,768]{2,1,0:T(8,128)(2,1)}), bf16[32,8,768]{2,1,0:T(8,128)(2,1)S(1)}, u32[]{:S(2)}, u32[]{:S(2)}) async-start(bf16[32,8,768]{2,1,0:T(8,128)(2,1)} %bitcast.37), calls=%async_computation.2 | async-start | bytes 786432 | tf_op jit(solution)/shard_map/all_to_all | solution.py:219
  75.1 1.2 collective-permute-done.5.g2_ref
  76.3 0.8 collective-permute-done.3.l2_ref
  77.1 1.0 copy-done.5
  78.1 4.9 %shard_map.115 = bf16[8,384,384]{2,1,0:T(8,128)(2,1)} custom-call(bf16[2,384,256]{2,1,0:T(8,128)(2,1)S(1)} %copy-done.5, bf16[2,384,256]{2,1,0:T(8,128)(2,1)S(1)} %collective-permute-done.3.l2_ref, bf16[256,2304]{1,0:T(8,128)(2,1)} %get-tuple-element.27.d_ref, bf16[256,2304]{1,0:T(8,128)(2,1)} %collective-permute-done.4.d2_ref, ...), custom_call_target="tpu_custom_call" | custom-call | flops 1207959552 | bytes 6291456 | tf_op jit(solution)/shard_map/pallas_call | solution.py:198
  83.0 5.7 %all-to-all-done.2 = bf16[32,8,768]{2,1,0:T(8,128)(2,1)S(1)} async-done(((bf16[32,8,768]{2,1,0:T(8,128)(2,1)}), bf16[32,8,768]{2,1,0:T(8,128)(2,1)S(1)}, u32[]{:S(2)}, u32[]{:S(2)}) %all-to-all-start.2) | async-done | bytes 393248 | tf_op jit(solution)/shard_map/all_to_all | solution.py:219
  88.7 8.1 %all-to-all-start.5 = ((bf16[32,96,384]{2,1,0:T(8,128)(2,1)}), bf16[32,96,384]{2,1,0:T(8,128)(2,1)}, u32[]{:S(2)}, u32[]{:S(2)}) async-start(bf16[32,96,384]{2,1,0:T(8,128)(2,1)} %bitcast.40), calls=%async_computation.5 | async-start | bytes 4718592 | tf_op jit(solution)/shard_map/all_to_all | solution.py:219
  96.7 8.4 %shard_map.112 = (bf16[256,768]{1,0:T(8,128)(2,1)}, bf16[256,2304]{1,0:T(8,128)(2,1)S(1)}) custom-call(bf16[256,768]{1,0:T(8,128)(2,1)S(1)} %bitcast.31, bf16[256,768]{1,0:T(8,128)(2,1)S(1)} %bitcast.27, bf16[256,2304]{1,0:T(8,128)(2,1)S(1)} %get-tuple-element.20.qkv_ref, bf16[768,2304]{1,0:T(8,128)(2,1)} %wq_ref.5, bf16[768,768]{1,0:T(8,128)(2,1)S(1)} %copy-done), custom_call_target="tpu_custom_call" | custom-call | flops 1207959552 | bytes 8257536 | tf_op jit(solution)/shard_map/pallas_call | solution.py:198
  105.8 2.7 %collective-permute-done.l2_ref = bf16[2,384,256]{2,1,0:T(8,128)(2,1)S(1)} collective-permute-done((bf16[2,384,256]{2,1,0:T(8,128)(2,1)S(1)}, bf16[2,384,256]{2,1,0:T(8,128)(2,1)S(1)}, u32[]{:S(2)}, u32[]{:S(2)}) %collective-permute-start) | collective-permute-done | bytes 393248 | tf_op jit(solution)/shard_map/ppermute | solution.py:223
  109.1 3.2 %shard_map.114 = bf16[8,384,384]{2,1,0:T(8,128)(2,1)} custom-call(bf16[2,384,256]{2,1,0:T(8,128)(2,1)S(1)} %copy-done.3, bf16[2,384,256]{2,1,0:T(8,128)(2,1)S(1)} %collective-permute-done.l2_ref, bf16[256,2304]{1,0:T(8,128)(2,1)S(1)} %get-tuple-element.24.d_ref, bf16[256,2304]{1,0:T(8,128)(2,1)S(1)} %collective-permute-done.1.d2_ref, ...), custom_call_target="tpu_custom_call" | custom-call | flops 1207959552 | bytes 6291456 | tf_op jit(solution)/shard_map/pallas_call | solution.py:198
  112.3 19.5 %all-to-all-done.5 = bf16[32,96,384]{2,1,0:T(8,128)(2,1)} async-done(((bf16[32,96,384]{2,1,0:T(8,128)(2,1)}), bf16[32,96,384]{2,1,0:T(8,128)(2,1)}, u32[]{:S(2)}, u32[]{:S(2)}) %all-to-all-start.5) | async-done | bytes 2359328 | tf_op jit(solution)/shard_map/all_to_all | solution.py:219
  131.8 5.5 %all-to-all-start.4 = ((bf16[32,96,384]{2,1,0:T(8,128)(2,1)}), bf16[32,96,384]{2,1,0:T(8,128)(2,1)S(1)}, u32[]{:S(2)}, u32[]{:S(2)}) async-start(bf16[32,96,384]{2,1,0:T(8,128)(2,1)} %bitcast.41), calls=%async_computation.4 | async-start | bytes 4718592 | tf_op jit(solution)/shard_map/all_to_all | solution.py:219
  137.3 2.0 reduce_sum.37
  139.3 29.2 %all-to-all-done.4 = bf16[32,96,384]{2,1,0:T(8,128)(2,1)S(1)} async-done(((bf16[32,96,384]{2,1,0:T(8,128)(2,1)}), bf16[32,96,384]{2,1,0:T(8,128)(2,1)S(1)}, u32[]{:S(2)}, u32[]{:S(2)}) %all-to-all-start.4) | async-done | bytes 2359328 | tf_op jit(solution)/shard_map/all_to_all | solution.py:219
  168.8 11.2 %all_to_all.65 = bf16[4,24,768]{2,1,0:T(8,128)(2,1)S(1)} all-to-all(bf16[4,24,768]{2,1,0:T(8,128)(2,1)S(1)} %bitcast.43), channel_id=1, replica_groups=mesh['x'=4,'zl'=2,'y'=4,'zh'=4,'c'=2] {'zh'}, dimensions={0} | all-to-all | bytes 294912 | tf_op jit(solution)/shard_map/all_to_all | solution.py:219
  180.0 5.8 %all-to-all-start.3 = ((bf16[32,8,768]{2,1,0:T(8,128)(2,1)}), bf16[32,8,768]{2,1,0:T(8,128)(2,1)S(1)}, u32[]{:S(2)}, u32[]{:S(2)}) async-start(bf16[32,8,768]{2,1,0:T(8,128)(2,1)} %bitcast.10), calls=%async_computation.3 | async-start | bytes 786432 | tf_op jit(solution)/shard_map/all_to_all | solution.py:219
  185.9 12.4 %all-to-all-done.3 = bf16[32,8,768]{2,1,0:T(8,128)(2,1)S(1)} async-done(((bf16[32,8,768]{2,1,0:T(8,128)(2,1)}), bf16[32,8,768]{2,1,0:T(8,128)(2,1)S(1)}, u32[]{:S(2)}, u32[]{:S(2)}) %all-to-all-start.3) | async-done | bytes 393248 | tf_op jit(solution)/shard_map/all_to_all | solution.py:219
  199.1 3.4 %all-to-all-start.7 = ((bf16[8,24,768]{2,1,0:T(8,128)(2,1)}), bf16[8,24,768]{2,1,0:T(8,128)(2,1)S(1)}, u32[]{:S(2)}, u32[]{:S(2)}) async-start(bf16[8,24,768]{2,1,0:T(8,128)(2,1)} %broadcast_in_dim.2), calls=%async_computation.7 | async-start | bytes 589824 | tf_op jit(solution)/shard_map/all_to_all | solution.py:219
  202.5 1.0 shard_map.113
  203.5 7.6 %all-to-all-done.7 = bf16[8,24,768]{2,1,0:T(8,128)(2,1)S(1)} async-done(((bf16[8,24,768]{2,1,0:T(8,128)(2,1)}), bf16[8,24,768]{2,1,0:T(8,128)(2,1)S(1)}, u32[]{:S(2)}, u32[]{:S(2)}) %all-to-all-start.7) | async-done | bytes 294944 | tf_op jit(solution)/shard_map/all_to_all | solution.py:219
  211.8 0.8 slice_bitcast_fusion
  (35 shorter events, 4.3 us)
Async XLA Ops:
  0.6 27.6 %copy-start = (bf16[768,768]{1,0:T(8,128)(2,1)S(1)}, bf16[768,768]{1,0:T(8,128)(2,1)}, u32[]{:S(2)}) copy-start(bf16[768,768]{1,0:T(8,128)(2,1)} %wo_ref.5) | copy-start | bytes 3538948
  0.6 1.1 copy-start.6
  2.8 25.5 %all-to-all-start = ((bf16[32,8,768]{2,1,0:T(8,128)(2,1)}), bf16[32,8,768]{2,1,0:T(8,128)(2,1)S(1)}, u32[]{:S(2)}, u32[]{:S(2)}) async-start(bf16[32,8,768]{2,1,0:T(8,128)(2,1)} %bitcast.2), calls=%async_computation | async-start | bytes 786432 | tf_op jit(solution)/shard_map/all_to_all | solution.py:219
  28.2 26.4 %copy-start.1 = (bf16[1,2,128,768]{3,2,1,0:T(8,128)(2,1)S(1)}, bf16[1,2,128,768]{3,2,1,0:T(8,128)(2,1)}, u32[]{:S(2)}) copy-start(bf16[1,2,128,768]{3,2,1,0:T(8,128)(2,1)} %param.7) | copy-start | bytes 1179652
  28.2 26.4 %copy-start.8 = (bf16[768,768]{1,0:T(8,128)(2,1)S(1)}, bf16[768,768]{1,0:T(8,128)(2,1)}, u32[]{:S(2)}) copy-start(bf16[768,768]{1,0:T(8,128)(2,1)} %wo_ref.4) | copy-start | bytes 3538948
  35.2 30.7 %copy-start.2 = (bf16[2,384,256]{2,1,0:T(8,128)(2,1)}, bf16[2,384,256]{2,1,0:T(8,128)(2,1)S(1)}, u32[]{:S(2)}) copy-start(bf16[2,384,256]{2,1,0:T(8,128)(2,1)S(1)} %get-tuple-element.22.l_ref) | copy-start | bytes 1179652
  35.2 30.7 %copy-start.9 = (bf16[2,384,256]{2,1,0:T(8,128)(2,1)}, bf16[2,384,256]{2,1,0:T(8,128)(2,1)S(1)}, u32[]{:S(2)}) copy-start(bf16[2,384,256]{2,1,0:T(8,128)(2,1)S(1)} %get-tuple-element.23) | copy-start | bytes 1179652
  65.8 0.8 copy-start.4
  66.6 0.7 copy-start.7
  67.3 0.7 copy-start.11
  68.1 9.0 %collective-permute-start.4 = (bf16[256,2304]{1,0:T(8,128)(2,1)}, bf16[256,2304]{1,0:T(8,128)(2,1)}, u32[]{:S(2)}, u32[]{:S(2)}) collective-permute-start(bf16[256,2304]{1,0:T(8,128)(2,1)} %get-tuple-element.27.d_ref), channel_id=1, source_target_pairs={{0,1},{1,0},{2,3},{3,2},{4,5},{5,4},{6,7},{7,6},{8,9},{9,8},{10,11... | collective-permute-start | bytes 3538952 | tf_op jit(solution)/shard_map/ppermute | solution.py:223
  69.4 19.3 %all-to-all-start.2 = ((bf16[32,8,768]{2,1,0:T(8,128)(2,1)}), bf16[32,8,768]{2,1,0:T(8,128)(2,1)S(1)}, u32[]{:S(2)}, u32[]{:S(2)}) async-start(bf16[32,8,768]{2,1,0:T(8,128)(2,1)} %bitcast.37), calls=%async_computation.2 | async-start | bytes 786432 | tf_op jit(solution)/shard_map/all_to_all | solution.py:219
  74.5 1.8 collective-permute-start.5
  74.8 2.3 %collective-permute-start.3 = (bf16[2,384,256]{2,1,0:T(8,128)(2,1)}, bf16[2,384,256]{2,1,0:T(8,128)(2,1)S(1)}, u32[]{:S(2)}, u32[]{:S(2)}) collective-permute-start(bf16[2,384,256]{2,1,0:T(8,128)(2,1)} %copy-done.11), channel_id=1, source_target_pairs={{0,1},{1,0},{2,3},{3,2},{4,5},{5,4},{6,7},{7,6},{8,9},{9,8},{10,11... | collective-permute-start | bytes 1179656 | tf_op jit(solution)/shard_map/ppermute | solution.py:223
  77.1 1.0 copy-start.5
  88.7 43.1 %all-to-all-start.5 = ((bf16[32,96,384]{2,1,0:T(8,128)(2,1)}), bf16[32,96,384]{2,1,0:T(8,128)(2,1)}, u32[]{:S(2)}, u32[]{:S(2)}) async-start(bf16[32,96,384]{2,1,0:T(8,128)(2,1)} %bitcast.40), calls=%async_computation.5 | async-start | bytes 4718592 | tf_op jit(solution)/shard_map/all_to_all | solution.py:219
  96.7 8.6 %copy-start.10 = (bf16[2,384,256]{2,1,0:T(8,128)(2,1)S(1)}, bf16[2,384,256]{2,1,0:T(8,128)(2,1)}, u32[]{:S(2)}) copy-start(bf16[2,384,256]{2,1,0:T(8,128)(2,1)} %copy-done.9) | copy-start | bytes 1179652
  96.7 12.4 %copy-start.3 = (bf16[2,384,256]{2,1,0:T(8,128)(2,1)S(1)}, bf16[2,384,256]{2,1,0:T(8,128)(2,1)}, u32[]{:S(2)}) copy-start(bf16[2,384,256]{2,1,0:T(8,128)(2,1)} %copy-done.2) | copy-start | bytes 1179652
  105.1 4.0 %collective-permute-start.1 = (bf16[256,2304]{1,0:T(8,128)(2,1)S(1)}, bf16[256,2304]{1,0:T(8,128)(2,1)S(1)}, u32[]{:S(2)}, u32[]{:S(2)}) collective-permute-start(bf16[256,2304]{1,0:T(8,128)(2,1)S(1)} %get-tuple-element.24.d_ref), channel_id=1, source_target_pairs={{0,1},{1,0},{2,3},{3,2},{4,5},{5,4},{6,7},{7,6},{8,9},{9,8},{10,11... | collective-permute-start | bytes 3538952 | tf_op jit(solution)/shard_map/ppermute | solution.py:223
  105.3 3.2 %collective-permute-start = (bf16[2,384,256]{2,1,0:T(8,128)(2,1)S(1)}, bf16[2,384,256]{2,1,0:T(8,128)(2,1)S(1)}, u32[]{:S(2)}, u32[]{:S(2)}) collective-permute-start(bf16[2,384,256]{2,1,0:T(8,128)(2,1)S(1)} %copy-done.10), channel_id=1, source_target_pairs={{0,1},{1,0},{2,3},{3,2},{4,5},{5,4},{6,7},{7,6},{8,9},{9,8},{10,11... | collective-permute-start | bytes 1179656 | tf_op jit(solution)/shard_map/ppermute | solution.py:223
  105.6 3.5 %collective-permute-start.2 = (bf16[256,768]{1,0:T(8,128)(2,1)S(1)}, bf16[256,768]{1,0:T(8,128)(2,1)S(1)}, u32[]{:S(2)}, u32[]{:S(2)}) collective-permute-start(bf16[256,768]{1,0:T(8,128)(2,1)S(1)} %bitcast.28), channel_id=1, source_target_pairs={{0,1},{1,0},{2,3},{3,2},{4,5},{5,4},{6,7},{7,6},{8,9},{9,8},{10,11... | collective-permute-start | bytes 1179656 | tf_op jit(solution)/shard_map/ppermute | solution.py:223
  131.8 36.7 %all-to-all-start.4 = ((bf16[32,96,384]{2,1,0:T(8,128)(2,1)}), bf16[32,96,384]{2,1,0:T(8,128)(2,1)S(1)}, u32[]{:S(2)}, u32[]{:S(2)}) async-start(bf16[32,96,384]{2,1,0:T(8,128)(2,1)} %bitcast.41), calls=%async_computation.4 | async-start | bytes 4718592 | tf_op jit(solution)/shard_map/all_to_all | solution.py:219
  180.0 18.3 %all-to-all-start.3 = ((bf16[32,8,768]{2,1,0:T(8,128)(2,1)}), bf16[32,8,768]{2,1,0:T(8,128)(2,1)S(1)}, u32[]{:S(2)}, u32[]{:S(2)}) async-start(bf16[32,8,768]{2,1,0:T(8,128)(2,1)} %bitcast.10), calls=%async_computation.3 | async-start | bytes 786432 | tf_op jit(solution)/shard_map/all_to_all | solution.py:219
  199.1 12.1 %all-to-all-start.7 = ((bf16[8,24,768]{2,1,0:T(8,128)(2,1)}), bf16[8,24,768]{2,1,0:T(8,128)(2,1)S(1)}, u32[]{:S(2)}, u32[]{:S(2)}) async-start(bf16[8,24,768]{2,1,0:T(8,128)(2,1)} %broadcast_in_dim.2), calls=%async_computation.7 | async-start | bytes 589824 | tf_op jit(solution)/shard_map/all_to_all | solution.py:219

commit v2 on v1

v2 whole, which is shorter than its diff:
```python
import functools

import jax
import jax.numpy as jnp
from jax import lax
from jax.experimental import pallas as pl
from jax.experimental.pallas import tpu as pltpu
from jax.sharding import Mesh, PartitionSpec as P

D = 768
HEAD = 64
PAIR = 2 * HEAD
PAIRS = D // PAIR
T = 256
ROWS = 24
HALF = D // 2
BLOCK = 4 * ROWS
WHOLE = 60
QKV = 3 * D // 4
OUT = D // 4
EPSILON = 1e-06
SCALE = HEAD ** (-0.5)
BF = jnp.bfloat16
F32 = jnp.float32

FP = ("y", "zh", "c")
CLIP = ("x", "zl")

NN = (((1,), (0,)), ((), ()))
NT = (((1,), (1,)), ((), ()))
TN = (((0,), (0,)), ((), ()))


def dot(a, b, dims=NN):
    return lax.dot_general(a, b, dims, preferred_element_type=F32)


def normalize(x):
    centred = x - jnp.mean(x, axis=-1, keepdims=True)
    inverse = lax.rsqrt(jnp.mean(centred * centred, axis=-1, keepdims=True) + EPSILON)
    return centred * inverse, inverse


def normalize_back(normed, inverse, grad):
    first = jnp.mean(grad, axis=-1, keepdims=True)
    second = jnp.mean(grad * normed, axis=-1, keepdims=True)
    return inverse * (grad - first - normed * second)


def iota(shape, dim):
    return lax.broadcasted_iota(jnp.int32, shape, dim)


def order(to_sent):
    sent = iota((T, T), 0 if to_sent else 1)
    natural = iota((T, T), 1 if to_sent else 0)
    source = ((sent // 4) % 2) * 128 + (sent // 8) * 4 + sent % 4
    return jnp.where(source == natural, 1.0, 0.0).astype(BF)


def chosen_rows(core):
    row = iota((HALF, D), 0)
    feature = (row // ROWS) * (2 * ROWS) + core * ROWS + row % ROWS
    return jnp.where(iota((HALF, D), 1) == feature, 1.0, 0.0).astype(BF)


def lanes(rows):
    low = iota((rows, PAIR), 1) < HEAD
    zero = jnp.zeros((rows, PAIR), BF)
    return lambda a, odd: jnp.where(low, zero, a) if odd else jnp.where(low, a, zero)


def same_patch():
    return (iota((T, T), 0) % 4) == (iota((T, T), 1) % 4)


def permute_kernel(to_sent, x_ref, o_ref):
    o_ref[...] = dot(order(to_sent), x_ref[...]).astype(BF)


def factors_kernel(pos_ref, low_ref, mixed_ref, own_ref, send_ref):
    for ref, which in ((own_ref, pos_ref[1]), (send_ref, 1 - pos_ref[1])):
        pick = chosen_rows(which)
        ref[0] = dot(pick, low_ref[...], NT).astype(BF)
        ref[1] = dot(pick, mixed_ref[...], NT).astype(BF)


def time_forward_kernel(x_ref, wq_ref, wo_ref, middle_ref, qkv_ref, low_ref, mixed_ref):
    x = x_ref[...].astype(F32)
    normed, _ = normalize(x)
    low = normed.astype(BF)
    low_ref[...] = low
    for i in range(9):
        cols = slice(i * 256, (i + 1) * 256)
        qkv_ref[:, cols] = dot(low, wq_ref[:, cols]).astype(BF)
    keep = lanes(T)
    near = same_patch()
    for p in range(PAIRS):
        q, k, v = (qkv_ref[:, i * D + p * PAIR:i * D + (p + 1) * PAIR] for i in range(3))
        weights = []
        values = []
        for odd in (False, True):
            s = dot(keep(q, odd), k, NT)
            s = jnp.where(near, s, -1e30)
            e = jnp.exp((s - jnp.max(s, axis=1, keepdims=True)) * SCALE)
            weights.append((e / jnp.sum(e, axis=1, keepdims=True)).astype(BF))
            values.append(keep(v, odd))
        mixed = dot(jnp.concatenate(weights, axis=1), jnp.concatenate(values, axis=0))
        mixed_ref[:, p * PAIR:(p + 1) * PAIR] = mixed.astype(BF)
    middle_ref[...] = (x + dot(mixed_ref[...], wo_ref[...])).astype(BF)


def probs_back(q, k, v, g, near):
    s = dot(k, q, NT)
    if near is not None:
        s = jnp.where(near, s, -1e30)
    e = jnp.exp((s - jnp.max(s, axis=0, keepdims=True)) * SCALE)
    probs = e / jnp.sum(e, axis=0, keepdims=True)
    dprobs = dot(v, g, NT)
    delta = jnp.sum(dprobs * probs, axis=0, keepdims=True)
    return probs.astype(BF), (probs * (dprobs - delta) * SCALE).astype(BF)


def attend_back(qkv_ref, g_ref, dqkv_ref, mixed_ref, near, blocks):
    size = T // blocks
    keep = lanes(size)
    for p in range(PAIRS):
        for b in range(blocks):
            rows = slice(b * size, (b + 1) * size)
            at = [slice(i * D + p * PAIR, i * D + (p + 1) * PAIR) for i in range(3)]
            q, k, v = (qkv_ref[rows, at[i]] for i in range(3))
            g = g_ref[rows, at[0]]
            qs, ks, vs, gs, ws, ds = [], [], [], [], [], []
            for odd in (False, True):
                q1, k1, v1, g1 = (keep(a, odd) for a in (q, k, v, g))
                w, d = probs_back(q, k1, v1, g, near)
                for into, a in ((qs, q1), (ks, k1), (vs, v1), (gs, g1), (ws, w), (ds, d)):
                    into.append(a)
            qs, ks, vs, gs = (jnp.concatenate(a, axis=0) for a in (qs, ks, vs, gs))
            dqkv_ref[rows, at[1]] = dot(jnp.concatenate(ds, axis=1), qs).astype(BF)
            dqkv_ref[rows, at[2]] = dot(jnp.concatenate(ws, axis=1), gs).astype(BF)
            dqkv_ref[rows, at[0]] = dot(jnp.concatenate(ds, axis=0), ks, TN).astype(BF)
            if mixed_ref is not None:
                mixed_ref[rows, at[0]] = dot(jnp.concatenate(ws, axis=0), vs, TN).astype(BF)


def space_kernel(m_ref, cot_ref, wq_ref, wo_ref, grad_ref, dqkv_ref, x_ref, low_ref, mixed_ref, qkv_ref, g_ref):
    x_ref[...] = dot(order(False), m_ref[...]).astype(BF)
    normed, inverse = normalize(x_ref[...].astype(F32))
    low = normed.astype(BF)
    low_ref[...] = low
    for i in range(9):
        cols = slice(i * 256, (i + 1) * 256)
        qkv_ref[:, cols] = dot(low, wq_ref[:, cols]).astype(BF)
    cot = cot_ref[...]
    g_ref[...] = dot(cot, wo_ref[...], NT).astype(BF)
    attend_back(qkv_ref, g_ref, dqkv_ref, mixed_ref, None, 2)
    grad = dot(dqkv_ref[...], wq_ref[...], NT)
    grad = cot.astype(F32) + normalize_back(normed, inverse, grad)
    grad_ref[...] = dot(order(True), grad.astype(BF)).astype(BF)


def space_out_kernel(x_ref, mixed_ref, wo_ref, out_ref):
    out_ref[...] = (x_ref[...].astype(F32) + dot(mixed_ref[...], wo_ref[...])).astype(BF)


def turned(pos, k):
    return (pos + k) % 4


def turned(pos, k):
    return (pos + k) % 4


def time_attend_kernel(gm_ref, qkv_ref, wo_ref, dqkv_ref, g_ref):
    g_ref[...] = dot(gm_ref[...], wo_ref[...], NT).astype(BF)
    attend_back(qkv_ref, g_ref, dqkv_ref, None, same_patch(), 1)


def time_grad_kernel(x_ref, gm_ref, dqkv_ref, wq_ref, grad_ref):
    normed, inverse = normalize(x_ref[...].astype(F32))
    grad = dot(dqkv_ref[...], wq_ref[...], NT)
    grad_ref[...] = (gm_ref[...].astype(F32) + normalize_back(normed, inverse, grad)).astype(BF)


def weights_kernel(pos_ref, l_ref, l2_ref, d_ref, d2_ref, g_ref, g2_ref, o_ref):
    over_x = pos_ref[1] == 0
    for a_ref, b_ref, which, at, width in ((g_ref, g2_ref, 1, QKV, OUT), (d_ref, d2_ref, 0, 0, QKV)):
        left = jnp.concatenate([l_ref[which], l2_ref[which]], axis=1)
        part = dot(left, jnp.concatenate([a_ref[...], b_ref[...]], axis=0)).astype(BF)
        for i in range(4):
            for j in range(4):
                block = part[i * BLOCK:(i + 1) * BLOCK, j * width:(j + 1) * width]
                o_ref[jnp.where(over_x, j, i), jnp.where(over_x, i, j), :, at:at + width] = block


def add(refs):
    total = refs[0][...].astype(F32)
    for ref in refs[1:]:
        total += ref[...].astype(F32)
    return total.astype(BF)


def add_first(ref):
    total = ref[0].astype(F32)
    for i in range(1, ref.shape[0]):
        total += ref[i].astype(F32)
    return total.astype(BF)


def pieces_kernel(t_ref, s_ref, o_ref):
    for i in range(4):
        o_ref[i, :, :D] = add([t_ref.at[k, i] for k in range(4)])
        o_ref[i, :, D:] = add([s_ref.at[k, i] for k in range(4)])


def first_sum_kernel(got_ref, o_ref):
    o_ref[...] = add_first(got_ref)


def pair_sum_kernel(own_ref, other_ref, o_ref):
    o_ref[...] = add([own_ref, other_ref])


def spread_kernel(pos_ref, *refs):
    outs, held_ref = refs[4:8], refs[8]
    for k in range(4):
        held_ref[turned(pos_ref[0], 4 - k)] = refs[k][...].astype(F32)
    for i in range(2):
        for j in range(4):
            outs[2 * i][:, j * QKV:(j + 1) * QKV] = held_ref[j, :, i * D:i * D + QKV]
            outs[2 * i + 1][:, j * OUT:(j + 1) * OUT] = held_ref[j, :, i * D + QKV:(i + 1) * D]


def sds(*shape, dtype=BF):
    return jax.ShapeDtypeStruct(shape, dtype)


SMEM = pl.BlockSpec(memory_space=pltpu.SMEM)
VMEM = pl.BlockSpec(memory_space=pltpu.VMEM)


def call(kernel, outs, args, flops, scratch=(), mib=48):
    moved = sum(a.size * a.dtype.itemsize for a in (*args, *outs))
    return pl.pallas_call(
        kernel,
        out_shape=outs,
        in_specs=[SMEM if a.dtype == jnp.int32 else VMEM for a in args],
        out_specs=[VMEM] * len(outs),
        scratch_shapes=scratch,
        compiler_params=pltpu.CompilerParams(vmem_limit_bytes=mib * 2**20),
        cost_estimate=pl.CostEstimate(flops=flops, bytes_accessed=moved if flops else 0, transcendentals=0),
    )(*args)


PROJ = 2 * T * D * 3 * D
OUTP = 2 * T * D * D


def permuted(x, to_sent):
    return call(functools.partial(permute_kernel, to_sent), [sds(T, D)], [x], 2 * T * T * D)[0]


def a2a(x, axes):
    return lax.all_to_all(x, axes, 0, 0, tiled=True)


def factors(pos, low, mixed):
    return call(
        factors_kernel, [sds(2, HALF, T)] * 2, [pos, low, mixed], 2 * OUTP, mib=WHOLE
    )


def weights(*factors):
    return call(weights_kernel, [sds(4, 4, BLOCK, D)], factors, 2 * 512 * HALF * 4 * D, mib=WHOLE)[0]


def crossed(x, first):
    device = [[[(i * 4 + j) * 2 + core for core in range(2)] for j in range(4)] for i in range(4)]
    along_x = [[device[i][j][1 - first] for i in range(4)] for j in range(4)]
    along_y = [[device[i][j][first] for j in range(4)] for i in range(4)]
    return lax.all_to_all(x, ("x", "y", "c"), 0, 0, tiled=True, axis_index_groups=along_x + along_y)


def swap(x):
    return lax.ppermute(x, "c", [(0, 1), (1, 0)])


def shifted(x, axis, k):
    return lax.ppermute(x, axis, [(i, (i + k) % 4) for i in range(4)])


def exchange(pieces, axis):
    return [pieces[0]] + [shifted(pieces[k], axis, k) for k in (1, 2, 3)]


def after(*arrays):
    return lax.optimization_barrier(arrays)


def on_device(tokens, block_cotangent, time_qkv, time_out, space_qkv, space_out):
    pos = jnp.stack([lax.axis_index(axis).astype(jnp.int32) for axis in ("x", "c")])
    cot = block_cotangent.reshape(T, D)
    x = a2a(permuted(tokens.reshape(T, D), True), FP)
    x, cot_other = after(x, swap(cot))
    middle, t_qkv, t_low, t_mixed = call(
        time_forward_kernel,
        [sds(T, D), sds(T, 3 * D), sds(T, D), sds(T, D)],
        [x, time_qkv, time_out],
        PROJ + OUTP, mib=WHOLE,
    )
    middle = a2a(middle, FP)
    t_own, t_send = factors(pos, t_low, t_mixed)
    middle, t_other = after(middle, swap(t_send))
    grad_middle, s_dqkv, natural, s_low, s_mixed = call(
        space_kernel,
        [sds(T, D), sds(T, 3 * D), sds(T, D), sds(T, D), sds(T, D)],
        [middle, cot, space_qkv, space_out],
        2 * (PROJ + OUTP),
        [pltpu.VMEM((T, 3 * D), BF), pltpu.VMEM((T, D), BF)], mib=WHOLE,
    )
    grad_middle = a2a(grad_middle, FP)
    s_own, s_send = factors(pos, s_low, s_mixed)
    space = weights(pos, s_own, swap(s_send), s_dqkv, swap(s_dqkv), cot, cot_other)
    block_out = call(space_out_kernel, [sds(T, D)], [natural, s_mixed, space_out], OUTP, mib=WHOLE)[0]
    grad_middle, block_out, space = after(grad_middle, block_out, space)
    space = crossed(space, 1)
    t_dqkv = call(
        time_attend_kernel, [sds(T, 3 * D)], [grad_middle, t_qkv, time_out], PROJ + OUTP, [pltpu.VMEM((T, D), BF)]
    )[0]
    grad_tokens = call(time_grad_kernel, [sds(T, D)], [x, grad_middle, t_dqkv, time_qkv], PROJ)[0]
    time = weights(pos, t_own, t_other, t_dqkv, swap(t_dqkv), grad_middle, swap(grad_middle))
    time, grad_tokens = after(time, grad_tokens)
    time = crossed(time, 1)
    got = crossed(call(pieces_kernel, [sds(4, BLOCK, 2 * D)], [time, space], 0)[0], 0)
    got = call(first_sum_kernel, [sds(BLOCK, 2 * D)], [got], 0)[0]
    got = a2a(got.reshape(4, ROWS, 2 * D), ("zh",))
    got, grad_tokens = after(got, grad_tokens)
    tokens_grad = permuted(a2a(grad_tokens, FP), False)
    share = call(first_sum_kernel, [sds(ROWS, 2 * D)], [got], 0)[0]
    other = lax.ppermute(share, "zl", [(0, 1), (1, 0)])
    share = call(pair_sum_kernel, [sds(ROWS, 2 * D)], [share, other], 0)[0]
    sizes = [3 * D, D, 3 * D, D]
    sums = call(
        spread_kernel, [sds(ROWS, size, dtype=F32) for size in sizes], [pos, *exchange([share] * 4, "x")], 0,
        [pltpu.VMEM((4, ROWS, 2 * D), F32)],
    )
    shape = tokens.shape
    return (block_out.reshape(shape), tokens_grad.reshape(shape), *sums)


def solution(mesh):
    fine = Mesh(mesh.devices.reshape(4, 2, 4, 4, 2), ("x", "zl", "y", "zh", "c"))
    activations = P(CLIP, FP, None, None)
    return jax.shard_map(
        on_device,
        mesh=fine,
        in_specs=(activations, activations, P(), P(), P(), P()),
        out_specs=(activations, activations, P(FP, None), P(FP, None), P(FP, None), P(FP, None)),
        check_vma=False,
    )
```

time: 216 us -> 193 us (0.89)
  waiting for transfers between devices: 93.5 us -> 42.6 us
  blocking collectives: 30.7 us -> 51.4 us
  Pallas kernels: 36.6 us -> 47.7 us
    all_to_all x6 -> x4, waiting for transfers between devices: 88.2 us -> 21.7 us  [a2a(): return lax.all_to_all(x, axes, 0, 0, tiled=True)]
    all_to_all x0 -> x2, blocking collectives: none -> 36.8 us  [crossed(): lax.all_to_all(x, ('x', 'y', 'c'), 0, 0, tiled=True, axis_index_groups=al...]
    ppermute x0 -> x4, waiting for transfers between devices: none -> 16.6 us  [the longest x1 11 us: on_device(): other = lax.ppermute(share, 'zl', [(0, 1), (1, 0)])]
    all_to_all x2 -> x1, blocking collectives: 30.7 us -> 14.6 us  [a2a(): return lax.all_to_all(x, axes, 0, 0, tiled=True)]
    all_to_all x6 -> x4, starting transfers between devices: 39.6 us -> 28.3 us  [a2a(): return lax.all_to_all(x, axes, 0, 0, tiled=True)]
    pallas_call x7 -> x16, Pallas kernels: 36.6 us -> 47.7 us  [call(): pl.pallas_call(kernel, out_shape=outs, in_specs=[SMEM if a.dtype == jnp.i...]
    all_to_all x0 -> x1, starting transfers between devices: none -> 4.99 us  [crossed(): lax.all_to_all(x, ('x', 'y', 'c'), 0, 0, tiled=True, axis_index_groups=al...]
    unnamed x24 -> x34, local copies, waits for them, and re-layouts: 4.34 us -> 9.16 us
  transfers between devices with their start and end apart: 12 -> 15, of which waited for: 10 -> 10; matrix products, arithmetic and copies ran while one was open for 1% -> 0% of each run, Pallas kernels for 8% -> 14%
where the time goes in v2:
time: 193 us; the launch traced here: 192 us
  blocking collectives  51.4 us (27%)
  Pallas kernels  47.7 us (25%)
  waiting for transfers between devices  42.6 us (22%)
  starting transfers between devices  40.1 us (21%)
  local copies, waits for them, and re-layouts  9.16 us (5%)
    pallas_call x16, Pallas kernels, call(): pl.pallas_call(kernel, out_shape=outs, in_specs=[SMEM if a.dtype == jnp.i...  47.7 us
    all_to_all x2, blocking collectives, crossed(): lax.all_to_all(x, ('x', 'y', 'c'), 0, 0, tiled=True, axis_index_groups=al...  36.8 us
    all_to_all x4, starting transfers between devices, a2a(): return lax.all_to_all(x, axes, 0, 0, tiled=True)  28.3 us
    all_to_all x4, waiting for transfers between devices, a2a(): return lax.all_to_all(x, axes, 0, 0, tiled=True)  21.7 us
    all_to_all x1, blocking collectives, a2a(): return lax.all_to_all(x, axes, 0, 0, tiled=True)  14.6 us
    ppermute x1, waiting for transfers between devices, on_device(): other = lax.ppermute(share, 'zl', [(0, 1), (1, 0)])  11 us
    unnamed x34, local copies, waits for them, and re-layouts  9.16 us
    ppermute x3, waiting for transfers between devices, shifted(): return lax.ppermute(x, axis, [(i, (i + k) % 4) for i in range(4)])  5.56 us
  transfers between devices with their start and end apart: 15, of which 10 were waited for; matrix products, arithmetic and copies ran while one was open for 0% of the time, Pallas kernels for 14%

profile of v2, /device:TPU:8, one launch (start us, length us, event | category | flops | bytes accessed | tf_op | source)
XLA Modules:
  0.0 192.3 jit_solution(12678104533414408826)
XLA Ops:
  2.6 11.7 %all-to-all-start = ((bf16[32,8,768]{2,1,0:T(8,128)(2,1)}), bf16[32,8,768]{2,1,0:T(8,128)(2,1)S(1)}, u32[]{:S(2)}, u32[]{:S(2)}) async-start(bf16[32,8,768]{2,1,0:T(8,128)(2,1)} %bitcast.1), calls=%async_computation | async-start | bytes 786432 | tf_op jit(solution)/shard_map/all_to_all | solution.py:265
  14.6 1.6 collective-permute-done.g2_ref
  16.2 12.0 %all-to-all-done = bf16[32,8,768]{2,1,0:T(8,128)(2,1)S(1)} async-done(((bf16[32,8,768]{2,1,0:T(8,128)(2,1)}), bf16[32,8,768]{2,1,0:T(8,128)(2,1)S(1)}, u32[]{:S(2)}, u32[]{:S(2)}) %all-to-all-start) | async-done | bytes 393248 | tf_op jit(solution)/shard_map/all_to_all | solution.py:265
  28.9 7.4 %shard_map.110 = (bf16[256,768]{1,0:T(8,128)(2,1)}, bf16[256,2304]{1,0:T(8,128)(2,1)}, bf16[256,768]{1,0:T(8,128)(2,1)}, bf16[256,768]{1,0:T(8,128)(2,1)}) custom-call(bf16[256,768]{1,0:T(8,128)(2,1)} %bitcast.15, bf16[768,2304]{1,0:T(8,128)(2,1)} %wq_ref.5, bf16[768,768]{1,0:T(8,128)(2,1)} %wo_ref.7), custom_call_target="tpu_custom_call" | custom-call | flops 1207959552 | bytes 7471104 | tf_op jit(solution)/shard_map/pallas_call | solution.py:245
  36.2 6.4 %all-to-all-start.1 = ((bf16[32,8,768]{2,1,0:T(8,128)(2,1)}), bf16[32,8,768]{2,1,0:T(8,128)(2,1)S(1)}, u32[]{:S(2)}, u32[]{:S(2)}) async-start(bf16[32,8,768]{2,1,0:T(8,128)(2,1)} %bitcast.29), calls=%async_computation.1 | async-start | bytes 786432 | tf_op jit(solution)/shard_map/all_to_all | solution.py:265
  43.2 2.7 %shard_map.111 = (bf16[2,384,256]{2,1,0:T(8,128)(2,1)}, bf16[2,384,256]{2,1,0:T(8,128)(2,1)}) custom-call(s32[2]{0:T(128)} %pad_add_fusion.pos_ref, bf16[256,768]{1,0:T(8,128)(2,1)} %get-tuple-element.36.low_ref, bf16[256,768]{1,0:T(8,128)(2,1)} %get-tuple-element.37.mixed_ref), custom_call_target="tpu_custom_call" | custom-call | flops 603979776 | bytes 1572872 | tf_op jit(solution)/shard_map/pallas_call | solution.py:245
  46.1 1.9 collective-permute-done.1.l2_ref
  48.0 8.4 %all-to-all-done.1 = bf16[32,8,768]{2,1,0:T(8,128)(2,1)S(1)} async-done(((bf16[32,8,768]{2,1,0:T(8,128)(2,1)}), bf16[32,8,768]{2,1,0:T(8,128)(2,1)S(1)}, u32[]{:S(2)}, u32[]{:S(2)}) %all-to-all-start.1) | async-done | bytes 393248 | tf_op jit(solution)/shard_map/all_to_all | solution.py:265
  57.2 11.5 %shard_map.112 = (bf16[256,768]{1,0:T(8,128)(2,1)}, bf16[256,2304]{1,0:T(8,128)(2,1)}, bf16[256,768]{1,0:T(8,128)(2,1)}, bf16[256,768]{1,0:T(8,128)(2,1)}, bf16[256,768]{1,0:T(8,128)(2,1)}) custom-call(bf16[256,768]{1,0:T(8,128)(2,1)} %bitcast.28, bf16[256,768]{1,0:T(8,128)(2,1)} %bitcast.24, bf16[768,2304]{1,0:T(8,128)(2,1)} %wq_ref.4, bf16[768,768]{1,0:T(8,128)(2,1)} %wo_ref.6), custom_call_target="tpu_custom_call" | custom-call | flops 2415919104 | bytes 8257536 | tf_op jit(solution)/shard_map/pallas_call | solution.py:245
  68.7 1.4 collective-permute-start.3
  70.0 5.1 %all-to-all-start.2 = ((bf16[32,8,768]{2,1,0:T(8,128)(2,1)}), bf16[32,8,768]{2,1,0:T(8,128)(2,1)S(1)}, u32[]{:S(2)}, u32[]{:S(2)}) async-start(bf16[32,8,768]{2,1,0:T(8,128)(2,1)} %bitcast.30), calls=%async_computation.2 | async-start | bytes 786432 | tf_op jit(solution)/shard_map/all_to_all | solution.py:265
  75.1 2.7 %shard_map.114 = (bf16[2,384,256]{2,1,0:T(8,128)(2,1)}, bf16[2,384,256]{2,1,0:T(8,128)(2,1)}) custom-call(s32[2]{0:T(128)} %pad_add_fusion.pos_ref, bf16[256,768]{1,0:T(8,128)(2,1)} %get-tuple-element.43.low_ref, bf16[256,768]{1,0:T(8,128)(2,1)} %get-tuple-element.42.mixed_ref), custom_call_target="tpu_custom_call" | custom-call | flops 603979776 | bytes 1572872 | tf_op jit(solution)/shard_map/pallas_call | solution.py:245
  78.0 2.7 %shard_map.113 = bf16[256,768]{1,0:T(8,128)(2,1)} custom-call(bf16[256,768]{1,0:T(8,128)(2,1)} %get-tuple-element.41.x_ref, bf16[256,768]{1,0:T(8,128)(2,1)} %get-tuple-element.42.mixed_ref, bf16[768,768]{1,0:T(8,128)(2,1)} %wo_ref.6), custom_call_target="tpu_custom_call" | custom-call | flops 301989888 | bytes 2359296 | tf_op jit(solution)/shard_map/pallas_call | solution.py:245
  81.9 5.1 %shard_map.115 = bf16[4,4,96,768]{3,2,1,0:T(8,128)(2,1)} custom-call(s32[2]{0:T(128)} %pad_add_fusion.pos_ref, bf16[2,384,256]{2,1,0:T(8,128)(2,1)} %get-tuple-element.44.l_ref, bf16[2,384,256]{2,1,0:T(8,128)(2,1)} %copy-done.14, bf16[256,2304]{1,0:T(8,128)(2,1)} %get-tuple-element.46.d_ref, bf16[256,2304]{1,0:T(8,128)(2,1)} %copy-done.10, ...), custom_call_target="tpu_custom_call" | custom-call | flops 1207959552 | bytes 6291464 | tf_op jit(solution)/shard_map/pallas_call | solution.py:245
  87.1 1.3 all-to-all-done.2
  89.2 5.0 %all-to-all-start.4 = ((bf16[4,4,96,768]{3,2,1,0:T(8,128)(2,1)}), bf16[4,4,96,768]{3,2,1,0:T(8,128)(2,1)S(1)}, u32[]{:S(2)}, u32[]{:S(2)}) async-start(bf16[4,4,96,768]{3,2,1,0:T(8,128)(2,1)} %shard_map.115), calls=%async_computation.4 | async-start | bytes 4718592 | tf_op jit(solution)/shard_map/all_to_all | solution.py:282
  95.2 1.3 copy-done.6
  96.4 1.3 copy-done.9
  97.7 4.1 %shard_map.116.d_ref.dqkv_ref = bf16[256,2304]{1,0:T(8,128)(2,1)S(1)} custom-call(bf16[256,768]{1,0:T(8,128)(2,1)S(1)} %bitcast.18, bf16[256,2304]{1,0:T(8,128)(2,1)S(1)} %copy-done.9, bf16[768,768]{1,0:T(8,128)(2,1)S(1)} %copy-done.6), custom_call_target="tpu_custom_call" | custom-call | flops 1207959552 | bytes 3932160 | tf_op jit(solution)/shard_map/pallas_call | solution.py:245
  101.8 1.4 collective-permute-start.4
  103.2 2.1 %shard_map.118 = bf16[256,768]{1,0:T(8,128)(2,1)} custom-call(bf16[256,768]{1,0:T(8,128)(2,1)S(1)} %bitcast.16, bf16[256,768]{1,0:T(8,128)(2,1)S(1)} %bitcast.20, bf16[256,2304]{1,0:T(8,128)(2,1)S(1)} %shard_map.116.d_ref.dqkv_ref, bf16[768,2304]{1,0:T(8,128)(2,1)S(1)} %copy-done), custom_call_target="tpu_custom_call" | custom-call | flops 905969664 | bytes 5898240 | tf_op jit(solution)/shard_map/pallas_call | solution.py:245
  107.3 5.1 %shard_map.117 = bf16[4,4,96,768]{3,2,1,0:T(8,128)(2,1)} custom-call(s32[2]{0:T(128)} %pad_add_fusion.pos_ref, bf16[2,384,256]{2,1,0:T(8,128)(2,1)} %get-tuple-element.49.l_ref, bf16[2,384,256]{2,1,0:T(8,128)(2,1)} %collective-permute-done.1.l2_ref, bf16[256,2304]{1,0:T(8,128)(2,1)} %copy-done.1, bf16[256,2304]{1,0:T(8,128)(2,1)} %copy-done.11, ...), custom_call_target="tpu_custom_call" | custom-call | flops 1207959552 | bytes 6291464 | tf_op jit(solution)/shard_map/pallas_call | solution.py:245
  112.5 22.1 %all_to_all.67.t_ref = bf16[4,4,96,768]{3,2,1,0:T(8,128)(2,1)S(1)} all-to-all(bf16[4,4,96,768]{3,2,1,0:T(8,128)(2,1)} %shard_map.117), channel_id=1, replica_groups={{0,64,128,192},{8,72,136,200},{16,80,144,208},{24,88,152,216},{1,9,17,2..., dimensions={0} | all-to-all | bytes 4718592 | tf_op jit(solution)/shard_map/all_to_all | solution.py:282
  135.1 14.7 %all_to_all.68.got_ref = bf16[4,96,1536]{2,1,0:T(8,128)(2,1)S(1)} all-to-all(bf16[4,96,1536]{2,1,0:T(8,128)(2,1)S(1)} %shard_map.119), channel_id=1, replica_groups={{1,65,129,193},{9,73,137,201},{17,81,145,209},{25,89,153,217},{0,8,16,2..., dimensions={0} | all-to-all | bytes 2359296 | tf_op jit(solution)/shard_map/all_to_all | solution.py:282
  150.0 14.6 %all_to_all.69.got_ref = bf16[4,24,1536]{2,1,0:T(8,128)(2,1)S(1)} all-to-all(bf16[4,24,1536]{2,1,0:T(8,128)(2,1)S(1)} %bitcast.22), channel_id=1, replica_groups=mesh['x'=4,'zl'=2,'y'=4,'zh'=4,'c'=2] {'zh'}, dimensions={0} | all-to-all | bytes 589824 | tf_op jit(solution)/shard_map/all_to_all | solution.py:265
  164.6 5.0 %all-to-all-start.7 = ((bf16[32,8,768]{2,1,0:T(8,128)(2,1)}), bf16[32,8,768]{2,1,0:T(8,128)(2,1)S(1)}, u32[]{:S(2)}, u32[]{:S(2)}) async-start(bf16[32,8,768]{2,1,0:T(8,128)(2,1)} %bitcast.12), calls=%async_computation.7 | async-start | bytes 786432 | tf_op jit(solution)/shard_map/all_to_all | solution.py:265
  170.5 11.0 %collective-permute-done.6.other_ref = bf16[24,1536]{1,0:T(8,128)(2,1)S(1)} collective-permute-done((bf16[24,1536]{1,0:T(8,128)(2,1)S(1)}, bf16[24,1536]{1,0:T(8,128)(2,1)S(1)}, u32[]{:S(2)}, u32[]{:S(2)}) %collective-permute-start.6) | collective-permute-done | bytes 73760 | tf_op jit(solution)/shard_map/ppermute | solution.py:341
  181.5 1.2 collective-permute-start.9
  182.8 1.5 collective-permute-start.8
  184.2 2.0 %collective-permute-done.9.refs_3_ = bf16[24,1536]{1,0:T(8,128)(2,1)S(1)} collective-permute-done((bf16[24,1536]{1,0:T(8,128)(2,1)S(1)}, bf16[24,1536]{1,0:T(8,128)(2,1)S(1)}, u32[]{:S(2)}, u32[]{:S(2)}) %collective-permute-start.9) | collective-permute-done | bytes 73760 | tf_op jit(solution)/shard_map/ppermute | solution.py:290
  186.2 2.8 %collective-permute-done.8.refs_2_ = bf16[24,1536]{1,0:T(8,128)(2,1)S(1)} collective-permute-done((bf16[24,1536]{1,0:T(8,128)(2,1)S(1)}, bf16[24,1536]{1,0:T(8,128)(2,1)S(1)}, u32[]{:S(2)}, u32[]{:S(2)}) %collective-permute-start.8) | collective-permute-done | bytes 73760 | tf_op jit(solution)/shard_map/ppermute | solution.py:290
  189.8 1.5 shard_map.124
  (52 shorter events, 13.0 us)
Async XLA Ops:
  0.6 1.0 copy-start.7
  1.6 12.7 %copy-start.12 = (bf16[1,2,128,768]{3,2,1,0:T(8,128)(2,1)S(1)}, bf16[1,2,128,768]{3,2,1,0:T(8,128)(2,1)}, u32[]{:S(2)}) copy-start(bf16[1,2,128,768]{3,2,1,0:T(8,128)(2,1)} %param.7) | copy-start | bytes 1179652
  2.6 25.5 %all-to-all-start = ((bf16[32,8,768]{2,1,0:T(8,128)(2,1)}), bf16[32,8,768]{2,1,0:T(8,128)(2,1)S(1)}, u32[]{:S(2)}, u32[]{:S(2)}) async-start(bf16[32,8,768]{2,1,0:T(8,128)(2,1)} %bitcast.1), calls=%async_computation | async-start | bytes 786432 | tf_op jit(solution)/shard_map/all_to_all | solution.py:265
  14.4 1.8 collective-permute-start
  16.2 29.7 %copy-start.13 = (bf16[256,768]{1,0:T(8,128)(2,1)}, bf16[256,768]{1,0:T(8,128)(2,1)S(1)}, u32[]{:S(2)}) copy-start(bf16[256,768]{1,0:T(8,128)(2,1)S(1)} %collective-permute-done.g2_ref) | copy-start | bytes 1179652
  28.1 0.7 copy-start.2
  36.2 20.2 %all-to-all-start.1 = ((bf16[32,8,768]{2,1,0:T(8,128)(2,1)}), bf16[32,8,768]{2,1,0:T(8,128)(2,1)S(1)}, u32[]{:S(2)}, u32[]{:S(2)}) async-start(bf16[32,8,768]{2,1,0:T(8,128)(2,1)} %bitcast.29), calls=%async_computation.1 | async-start | bytes 786432 | tf_op jit(solution)/shard_map/all_to_all | solution.py:265
  45.9 2.1 %collective-permute-start.1 = (bf16[2,384,256]{2,1,0:T(8,128)(2,1)}, bf16[2,384,256]{2,1,0:T(8,128)(2,1)}, u32[]{:S(2)}, u32[]{:S(2)}) collective-permute-start(bf16[2,384,256]{2,1,0:T(8,128)(2,1)} %get-tuple-element.38), channel_id=1, source_target_pairs={{0,1},{1,0},{2,3},{3,2},{4,5},{5,4},{6,7},{7,6},{8,9},{9,8},{10,11... | collective-permute-start | bytes 1179656 | tf_op jit(solution)/shard_map/ppermute | solution.py:286
  56.4 0.7 copy-start.16
  68.7 12.1 %collective-permute-start.3 = (bf16[256,2304]{1,0:T(8,128)(2,1)}, bf16[256,2304]{1,0:T(8,128)(2,1)S(1)}, u32[]{:S(2)}, u32[]{:S(2)}) collective-permute-start(bf16[256,2304]{1,0:T(8,128)(2,1)} %get-tuple-element.46.d_ref), channel_id=1, source_target_pairs={{0,1},{1,0},{2,3},{3,2},{4,5},{5,4},{6,7},{7,6},{8,9},{9,8},{10,11... | collective-permute-start | bytes 3538952 | tf_op jit(solution)/shard_map/ppermute | solution.py:286
  70.0 18.4 %all-to-all-start.2 = ((bf16[32,8,768]{2,1,0:T(8,128)(2,1)}), bf16[32,8,768]{2,1,0:T(8,128)(2,1)S(1)}, u32[]{:S(2)}, u32[]{:S(2)}) async-start(bf16[32,8,768]{2,1,0:T(8,128)(2,1)} %bitcast.30), calls=%async_computation.2 | async-start | bytes 786432 | tf_op jit(solution)/shard_map/all_to_all | solution.py:265
  77.8 2.9 %collective-permute-start.2 = (bf16[2,384,256]{2,1,0:T(8,128)(2,1)}, bf16[2,384,256]{2,1,0:T(8,128)(2,1)S(1)}, u32[]{:S(2)}, u32[]{:S(2)}) collective-permute-start(bf16[2,384,256]{2,1,0:T(8,128)(2,1)} %get-tuple-element.45), channel_id=1, source_target_pairs={{0,1},{1,0},{2,3},{3,2},{4,5},{5,4},{6,7},{7,6},{8,9},{9,8},{10,11... | collective-permute-start | bytes 1179656 | tf_op jit(solution)/shard_map/ppermute | solution.py:286
  80.7 0.8 copy-start.14
  80.7 1.2 copy-start.10
  88.4 0.8 copy-start.4
  89.2 23.3 %all-to-all-start.4 = ((bf16[4,4,96,768]{3,2,1,0:T(8,128)(2,1)}), bf16[4,4,96,768]{3,2,1,0:T(8,128)(2,1)S(1)}, u32[]{:S(2)}, u32[]{:S(2)}) async-start(bf16[4,4,96,768]{3,2,1,0:T(8,128)(2,1)} %shard_map.115), calls=%async_computation.4 | async-start | bytes 4718592 | tf_op jit(solution)/shard_map/all_to_all | solution.py:282
  94.2 1.0 copy-start.5
  95.2 1.3 copy-start.6
  96.4 1.3 copy-start.9
  97.7 5.5 %copy-start = (bf16[768,2304]{1,0:T(8,128)(2,1)S(1)}, bf16[768,2304]{1,0:T(8,128)(2,1)}, u32[]{:S(2)}) copy-start(bf16[768,2304]{1,0:T(8,128)(2,1)} %wq_ref.5) | copy-start | bytes 10616836
  97.7 5.5 %copy-start.3 = (bf16[32,8,768]{2,1,0:T(8,128)(2,1)S(1)}, bf16[32,8,768]{2,1,0:T(8,128)(2,1)}, u32[]{:S(2)}) copy-start(bf16[32,8,768]{2,1,0:T(8,128)(2,1)} %copy-done.2) | copy-start | bytes 1179652
  101.8 3.6 %copy-start.1 = (bf16[256,2304]{1,0:T(8,128)(2,1)}, bf16[256,2304]{1,0:T(8,128)(2,1)S(1)}, u32[]{:S(2)}) copy-start(bf16[256,2304]{1,0:T(8,128)(2,1)S(1)} %shard_map.116.d_ref.dqkv_ref) | copy-start | bytes 3538948
  101.8 4.4 %collective-permute-start.4 = (bf16[256,2304]{1,0:T(8,128)(2,1)S(1)}, bf16[256,2304]{1,0:T(8,128)(2,1)S(1)}, u32[]{:S(2)}, u32[]{:S(2)}) collective-permute-start(bf16[256,2304]{1,0:T(8,128)(2,1)S(1)} %shard_map.116.d_ref.dqkv_ref), channel_id=1, source_target_pairs={{0,1},{1,0},{2,3},{3,2},{4,5},{5,4},{6,7},{7,6},{8,9},{9,8},{10,11... | collective-permute-start | bytes 3538952 | tf_op jit(solution)/shard_map/ppermute | solution.py:286
  103.1 3.0 %collective-permute-start.5 = (bf16[256,768]{1,0:T(8,128)(2,1)S(1)}, bf16[256,768]{1,0:T(8,128)(2,1)S(1)}, u32[]{:S(2)}, u32[]{:S(2)}) collective-permute-start(bf16[256,768]{1,0:T(8,128)(2,1)S(1)} %bitcast.19), channel_id=1, source_target_pairs={{0,1},{1,0},{2,3},{3,2},{4,5},{5,4},{6,7},{7,6},{8,9},{9,8},{10,11... | collective-permute-start | bytes 1179656 | tf_op jit(solution)/shard_map/ppermute | solution.py:286
  106.2 0.8 copy-start.15
  106.2 1.1 copy-start.11
  150.0 39.8 %copy-start.8 = (s32[2]{0:T(128)S(1)}, s32[2]{0:T(128)}, u32[]{:S(2)}) copy-start(s32[2]{0:T(128)} %pad_add_fusion.pos_ref) | copy-start | bytes 28
  164.6 26.7 %all-to-all-start.7 = ((bf16[32,8,768]{2,1,0:T(8,128)(2,1)}), bf16[32,8,768]{2,1,0:T(8,128)(2,1)S(1)}, u32[]{:S(2)}, u32[]{:S(2)}) async-start(bf16[32,8,768]{2,1,0:T(8,128)(2,1)} %bitcast.12), calls=%async_computation.7 | async-start | bytes 786432 | tf_op jit(solution)/shard_map/all_to_all | solution.py:265
  169.7 11.8 %collective-permute-start.6 = (bf16[24,1536]{1,0:T(8,128)(2,1)S(1)}, bf16[24,1536]{1,0:T(8,128)(2,1)S(1)}, u32[]{:S(2)}, u32[]{:S(2)}) collective-permute-start(bf16[24,1536]{1,0:T(8,128)(2,1)S(1)} %shard_map.122.own_ref), channel_id=1, source_target_pairs={{0,32},{32,0},{1,33},{33,1},{2,34},{34,2},{3,35},{35,3},{4,36},{36... | collective-permute-start | bytes 221192 | tf_op jit(solution)/shard_map/ppermute | solution.py:341
  181.5 4.7 %collective-permute-start.9 = (bf16[24,1536]{1,0:T(8,128)(2,1)S(1)}, bf16[24,1536]{1,0:T(8,128)(2,1)S(1)}, u32[]{:S(2)}, u32[]{:S(2)}) collective-permute-start(bf16[24,1536]{1,0:T(8,128)(2,1)S(1)} %shard_map.123.refs_0_), channel_id=1, source_target_pairs={{0,192},{64,0},{128,64},{192,128},{1,193},{65,1},{129,65},{193,129... | collective-permute-start | bytes 221192 | tf_op jit(solution)/shard_map/ppermute | solution.py:290
  182.8 6.2 %collective-permute-start.8 = (bf16[24,1536]{1,0:T(8,128)(2,1)S(1)}, bf16[24,1536]{1,0:T(8,128)(2,1)S(1)}, u32[]{:S(2)}, u32[]{:S(2)}) collective-permute-start(bf16[24,1536]{1,0:T(8,128)(2,1)S(1)} %shard_map.123.refs_0_), channel_id=1, source_target_pairs={{0,128},{64,192},{128,0},{192,64},{1,129},{65,193},{129,1},{193,65... | collective-permute-start | bytes 221192 | tf_op jit(solution)/shard_map/ppermute | solution.py:290
  184.2 5.6 %collective-permute-start.7 = (bf16[24,1536]{1,0:T(8,128)(2,1)S(1)}, bf16[24,1536]{1,0:T(8,128)(2,1)S(1)}, u32[]{:S(2)}, u32[]{:S(2)}) collective-permute-start(bf16[24,1536]{1,0:T(8,128)(2,1)S(1)} %shard_map.123.refs_0_), channel_id=1, source_target_pairs={{0,64},{64,128},{128,192},{192,0},{1,65},{65,129},{129,193},{193,1... | collective-permute-start | bytes 221192 | tf_op jit(solution)/shard_map/ppermute | solution.py:290

commit v3 on v2

--- a/solution.py
+++ b/solution.py
@@ -194,6 +194,13 @@
                 o_ref[jnp.where(over_x, j, i), jnp.where(over_x, i, j), :, at:at + width] = block
 
 
+def weights_by_distance_kernel(pos_ref, l_ref, l2_ref, d_ref, d2_ref, g_ref, g2_ref, *refs):
+    outs, held_ref = refs[:4], refs[4]
+    weights_kernel(pos_ref, l_ref, l2_ref, d_ref, d2_ref, g_ref, g2_ref, held_ref)
+    for k in range(4):
+        outs[k][...] = held_ref[turned(pos_ref[2], k)]
+
+
 def add(refs):
     total = refs[0][...].astype(F32)
     for ref in refs[1:]:
@@ -208,28 +215,29 @@
     return total.astype(BF)
 
 
-def pieces_kernel(t_ref, s_ref, o_ref):
-    for i in range(4):
-        o_ref[i, :, :D] = add([t_ref.at[k, i] for k in range(4)])
-        o_ref[i, :, D:] = add([s_ref.at[k, i] for k in range(4)])
-
-
 def first_sum_kernel(got_ref, o_ref):
     o_ref[...] = add_first(got_ref)
 
 
-def pair_sum_kernel(own_ref, other_ref, o_ref):
-    o_ref[...] = add([own_ref, other_ref])
-
-
-def spread_kernel(pos_ref, *refs):
-    outs, held_ref = refs[4:8], refs[8]
-    for k in range(4):
-        held_ref[turned(pos_ref[0], 4 - k)] = refs[k][...].astype(F32)
+def pieces_kernel(s_ref, *refs):
+    o_ref = refs[4]
+    for i in range(4):
+        o_ref[i, :, :D] = add([ref.at[i] for ref in refs[:4]])
+        o_ref[i, :, D:] = add([s_ref.at[k, i] for k in range(4)])
+
+
+def copies_kernel(got_ref, o_ref):
+    total = add_first(got_ref)
+    for i in range(8):
+        o_ref[i] = total
+
+
+def spread_kernel(got_ref, *outs):
     for i in range(2):
         for j in range(4):
-            outs[2 * i][:, j * QKV:(j + 1) * QKV] = held_ref[j, :, i * D:i * D + QKV]
-            outs[2 * i + 1][:, j * OUT:(j + 1) * OUT] = held_ref[j, :, i * D + QKV:(i + 1) * D]
+            part = add([got_ref.at[2 * j, :, i * D:(i + 1) * D], got_ref.at[2 * j + 1, :, i * D:(i + 1) * D]]).astype(F32)
+            outs[2 * i][:, j * QKV:(j + 1) * QKV] = part[:, :QKV]
+            outs[2 * i + 1][:, j * OUT:(j + 1) * OUT] = part[:, QKV:]
 
 
 def sds(*shape, dtype=BF):
@@ -275,31 +283,35 @@
     return call(weights_kernel, [sds(4, 4, BLOCK, D)], factors, 2 * 512 * HALF * 4 * D, mib=WHOLE)[0]
 
 
-def crossed(x, first):
+def rings(first):
     device = [[[(i * 4 + j) * 2 + core for core in range(2)] for j in range(4)] for i in range(4)]
     along_x = [[device[i][j][1 - first] for i in range(4)] for j in range(4)]
     along_y = [[device[i][j][first] for j in range(4)] for i in range(4)]
-    return lax.all_to_all(x, ("x", "y", "c"), 0, 0, tiled=True, axis_index_groups=along_x + along_y)
+    return along_x + along_y
+
+
+def crossed(x, first):
+    return lax.all_to_all(x, ("x", "y", "c"), 0, 0, tiled=True, axis_index_groups=rings(first))
+
+
+def crossed_steps(pieces, first):
+    return [pieces[0]] + [
+        lax.ppermute(pieces[k], ("x", "y", "c"), [(ring[i], ring[(i + k) % 4]) for ring in rings(first) for i in range(4)])
+        for k in (1, 2, 3)
+    ]
 
 
 def swap(x):
     return lax.ppermute(x, "c", [(0, 1), (1, 0)])
 
 
-def shifted(x, axis, k):
-    return lax.ppermute(x, axis, [(i, (i + k) % 4) for i in range(4)])
-
-
-def exchange(pieces, axis):
-    return [pieces[0]] + [shifted(pieces[k], axis, k) for k in (1, 2, 3)]
-
-
 def after(*arrays):
     return lax.optimization_barrier(arrays)
 
 
 def on_device(tokens, block_cotangent, time_qkv, time_out, space_qkv, space_out):
-    pos = jnp.stack([lax.axis_index(axis).astype(jnp.int32) for axis in ("x", "c")])
+    x_at, y_at, core = (lax.axis_index(axis).astype(jnp.int32) for axis in ("x", "y", "c"))
+    pos = jnp.stack([x_at, core, jnp.where(core == 0, x_at, y_at)])
     cot = block_cotangent.reshape(T, D)
     x = a2a(permuted(tokens.reshape(T, D), True), FP)
     x, cot_other = after(x, swap(cot))
@@ -329,22 +341,21 @@
         time_attend_kernel, [sds(T, 3 * D)], [grad_middle, t_qkv, time_out], PROJ + OUTP, [pltpu.VMEM((T, D), BF)]
     )[0]
     grad_tokens = call(time_grad_kernel, [sds(T, D)], [x, grad_middle, t_dqkv, time_qkv], PROJ)[0]
-    time = weights(pos, t_own, t_other, t_dqkv, swap(t_dqkv), grad_middle, swap(grad_middle))
-    time, grad_tokens = after(time, grad_tokens)
-    time = crossed(time, 1)
-    got = crossed(call(pieces_kernel, [sds(4, BLOCK, 2 * D)], [time, space], 0)[0], 0)
-    got = call(first_sum_kernel, [sds(BLOCK, 2 * D)], [got], 0)[0]
+    time = call(
+        weights_by_distance_kernel, [sds(4, BLOCK, D)] * 4,
+        [pos, t_own, t_other, t_dqkv, swap(t_dqkv), grad_middle, swap(grad_middle)], 2 * 512 * HALF * 4 * D,
+        [pltpu.VMEM((4, 4, BLOCK, D), BF)], mib=WHOLE,
+    )
+    grad_tokens, space, *time = after(grad_tokens, space, *time)
+    tokens_grad = a2a(grad_tokens, FP)
+    got = call(pieces_kernel, [sds(4, BLOCK, 2 * D)], [space, *crossed_steps(time, 1)], 0)[0]
+    got, tokens_grad = after(got, tokens_grad)
+    got = call(first_sum_kernel, [sds(BLOCK, 2 * D)], [crossed(got, 0)], 0)[0]
     got = a2a(got.reshape(4, ROWS, 2 * D), ("zh",))
-    got, grad_tokens = after(got, grad_tokens)
-    tokens_grad = permuted(a2a(grad_tokens, FP), False)
-    share = call(first_sum_kernel, [sds(ROWS, 2 * D)], [got], 0)[0]
-    other = lax.ppermute(share, "zl", [(0, 1), (1, 0)])
-    share = call(pair_sum_kernel, [sds(ROWS, 2 * D)], [share, other], 0)[0]
+    tokens_grad = permuted(tokens_grad, False)
+    shares = call(copies_kernel, [sds(8, ROWS, 2 * D)], [got], 0)[0]
     sizes = [3 * D, D, 3 * D, D]
-    sums = call(
-        spread_kernel, [sds(ROWS, size, dtype=F32) for size in sizes], [pos, *exchange([share] * 4, "x")], 0,
-        [pltpu.VMEM((4, ROWS, 2 * D), F32)],
-    )
+    sums = call(spread_kernel, [sds(ROWS, size, dtype=F32) for size in sizes], [a2a(shares, CLIP)], 0)
     shape = tokens.shape
     return (block_out.reshape(shape), tokens_grad.reshape(shape), *sums)
 

time: 193 us -> 188 us (0.974)
  blocking collectives: 51.4 us -> 33.5 us
  starting transfers between devices: 40.1 us -> 47.8 us
  waiting for transfers between devices: 42.6 us -> 47.3 us
    all_to_all x2 -> x1, blocking collectives: 36.8 us -> 14.7 us  [crossed(): lax.all_to_all(x, ('x', 'y', 'c'), 0, 0, tiled=True, axis_index_groups=ri...]
    all_to_all x4 -> x5, waiting for transfers between devices: 21.7 us -> 28.8 us  [a2a(): return lax.all_to_all(x, axes, 0, 0, tiled=True)]
    all_to_all x4 -> x5, starting transfers between devices: 28.3 us -> 34.7 us  [a2a(): return lax.all_to_all(x, axes, 0, 0, tiled=True)]
    all_to_all x1, blocking collectives: 14.6 us -> 18.8 us  [a2a(): return lax.all_to_all(x, axes, 0, 0, tiled=True)]
    ppermute x4 -> x3, waiting for transfers between devices: 16.6 us -> 13.8 us  [crossed_steps(): lax.ppermute(pieces[k], ('x', 'y', 'c'), [(ring[i], ring[(i + k) % 4]) fo...]
    ppermute x4 -> x3, starting transfers between devices: 3.47 us -> 4.78 us  [crossed_steps(): lax.ppermute(pieces[k], ('x', 'y', 'c'), [(ring[i], ring[(i + k) % 4]) fo...]
    pallas_call x16 -> x15, Pallas kernels: 47.7 us -> 48.9 us  [call(): pl.pallas_call(kernel, out_shape=outs, in_specs=[SMEM if a.dtype == jnp.i...]
  transfers between devices with their start and end apart: 15 -> 15, of which waited for: 10 -> 11; matrix products, arithmetic and copies ran while one was open for 0% -> 0% of each run, Pallas kernels for 14% -> 14%
where the time goes in v3:
time: 188 us; the launch traced here: 187 us
  Pallas kernels  48.9 us (26%)
  starting transfers between devices  47.8 us (25%)
  waiting for transfers between devices  47.3 us (25%)
  blocking collectives  33.5 us (18%)
  local copies, waits for them, and re-layouts  8.47 us (5%)
    pallas_call x15, Pallas kernels, call(): pl.pallas_call(kernel, out_shape=outs, in_specs=[SMEM if a.dtype == jnp.i...  48.9 us
    all_to_all x5, starting transfers between devices, a2a(): return lax.all_to_all(x, axes, 0, 0, tiled=True)  34.7 us
    all_to_all x5, waiting for transfers between devices, a2a(): return lax.all_to_all(x, axes, 0, 0, tiled=True)  28.8 us
    all_to_all x1, blocking collectives, a2a(): return lax.all_to_all(x, axes, 0, 0, tiled=True)  18.8 us
    all_to_all x1, blocking collectives, crossed(): lax.all_to_all(x, ('x', 'y', 'c'), 0, 0, tiled=True, axis_index_groups=ri...  14.7 us
    ppermute x3, waiting for transfers between devices, crossed_steps(): lax.ppermute(pieces[k], ('x', 'y', 'c'), [(ring[i], ring[(i + k) % 4]) fo...  13.8 us
    unnamed x34, local copies, waits for them, and re-layouts  8.47 us
    all_to_all x1, starting transfers between devices, crossed(): lax.all_to_all(x, ('x', 'y', 'c'), 0, 0, tiled=True, axis_index_groups=ri...  4.99 us
  transfers between devices with their start and end apart: 15, of which 11 were waited for; matrix products, arithmetic and copies ran while one was open for 0% of the time, Pallas kernels for 14%

profile of v3, /device:TPU:8, one launch (start us, length us, event | category | flops | bytes accessed | tf_op | source)
XLA Modules:
  0.0 187.4 jit_solution(4326332599951543430)
XLA Ops:
  2.6 11.7 %all-to-all-start = ((bf16[32,8,768]{2,1,0:T(8,128)(2,1)}), bf16[32,8,768]{2,1,0:T(8,128)(2,1)S(1)}, u32[]{:S(2)}, u32[]{:S(2)}) async-start(bf16[32,8,768]{2,1,0:T(8,128)(2,1)} %bitcast.1), calls=%async_computation | async-start | bytes 786432 | tf_op jit(solution)/shard_map/all_to_all | solution.py:273
  14.6 1.6 collective-permute-done.g2_ref
  16.2 12.0 %all-to-all-done = bf16[32,8,768]{2,1,0:T(8,128)(2,1)S(1)} async-done(((bf16[32,8,768]{2,1,0:T(8,128)(2,1)}), bf16[32,8,768]{2,1,0:T(8,128)(2,1)S(1)}, u32[]{:S(2)}, u32[]{:S(2)}) %all-to-all-start) | async-done | bytes 393248 | tf_op jit(solution)/shard_map/all_to_all | solution.py:273
  28.9 7.4 %shard_map.110 = (bf16[256,768]{1,0:T(8,128)(2,1)}, bf16[256,2304]{1,0:T(8,128)(2,1)}, bf16[256,768]{1,0:T(8,128)(2,1)}, bf16[256,768]{1,0:T(8,128)(2,1)}) custom-call(bf16[256,768]{1,0:T(8,128)(2,1)} %bitcast.16, bf16[768,2304]{1,0:T(8,128)(2,1)} %wq_ref.5, bf16[768,768]{1,0:T(8,128)(2,1)} %wo_ref.7), custom_call_target="tpu_custom_call" | custom-call | flops 1207959552 | bytes 7471104 | tf_op jit(solution)/shard_map/pallas_call | solution.py:253
  36.2 6.4 %all-to-all-start.1 = ((bf16[32,8,768]{2,1,0:T(8,128)(2,1)}), bf16[32,8,768]{2,1,0:T(8,128)(2,1)S(1)}, u32[]{:S(2)}, u32[]{:S(2)}) async-start(bf16[32,8,768]{2,1,0:T(8,128)(2,1)} %bitcast.29), calls=%async_computation.1 | async-start | bytes 786432 | tf_op jit(solution)/shard_map/all_to_all | solution.py:273
  43.2 2.7 %shard_map.111 = (bf16[2,384,256]{2,1,0:T(8,128)(2,1)}, bf16[2,384,256]{2,1,0:T(8,128)(2,1)}) custom-call(s32[3]{0:T(128)} %pad_add_fusion.pos_ref, bf16[256,768]{1,0:T(8,128)(2,1)} %get-tuple-element.44.low_ref, bf16[256,768]{1,0:T(8,128)(2,1)} %get-tuple-element.45.mixed_ref), custom_call_target="tpu_custom_call" | custom-call | flops 603979776 | bytes 1572876 | tf_op jit(solution)/shard_map/pallas_call | solution.py:253
  46.1 1.8 collective-permute-done.1.l2_ref
  47.9 8.6 %all-to-all-done.1 = bf16[32,8,768]{2,1,0:T(8,128)(2,1)S(1)} async-done(((bf16[32,8,768]{2,1,0:T(8,128)(2,1)}), bf16[32,8,768]{2,1,0:T(8,128)(2,1)S(1)}, u32[]{:S(2)}, u32[]{:S(2)}) %all-to-all-start.1) | async-done | bytes 393248 | tf_op jit(solution)/shard_map/all_to_all | solution.py:273
  57.2 11.5 %shard_map.112 = (bf16[256,768]{1,0:T(8,128)(2,1)}, bf16[256,2304]{1,0:T(8,128)(2,1)}, bf16[256,768]{1,0:T(8,128)(2,1)}, bf16[256,768]{1,0:T(8,128)(2,1)}, bf16[256,768]{1,0:T(8,128)(2,1)}) custom-call(bf16[256,768]{1,0:T(8,128)(2,1)} %bitcast.28, bf16[256,768]{1,0:T(8,128)(2,1)} %bitcast.24, bf16[768,2304]{1,0:T(8,128)(2,1)} %wq_ref.4, bf16[768,768]{1,0:T(8,128)(2,1)} %wo_ref.6), custom_call_target="tpu_custom_call" | custom-call | flops 2415919104 | bytes 8257536 | tf_op jit(solution)/shard_map/pallas_call | solution.py:253
  68.7 1.3 collective-permute-start.3
  70.0 5.2 %all-to-all-start.2 = ((bf16[32,8,768]{2,1,0:T(8,128)(2,1)}), bf16[32,8,768]{2,1,0:T(8,128)(2,1)S(1)}, u32[]{:S(2)}, u32[]{:S(2)}) async-start(bf16[32,8,768]{2,1,0:T(8,128)(2,1)} %bitcast.30), calls=%async_computation.2 | async-start | bytes 786432 | tf_op jit(solution)/shard_map/all_to_all | solution.py:273
  75.2 2.7 %shard_map.114 = (bf16[2,384,256]{2,1,0:T(8,128)(2,1)}, bf16[2,384,256]{2,1,0:T(8,128)(2,1)}) custom-call(s32[3]{0:T(128)} %pad_add_fusion.pos_ref, bf16[256,768]{1,0:T(8,128)(2,1)} %get-tuple-element.51.low_ref, bf16[256,768]{1,0:T(8,128)(2,1)} %get-tuple-element.50.mixed_ref), custom_call_target="tpu_custom_call" | custom-call | flops 603979776 | bytes 1572876 | tf_op jit(solution)/shard_map/pallas_call | solution.py:253
  78.0 2.7 %shard_map.113 = bf16[256,768]{1,0:T(8,128)(2,1)} custom-call(bf16[256,768]{1,0:T(8,128)(2,1)} %get-tuple-element.49.x_ref, bf16[256,768]{1,0:T(8,128)(2,1)} %get-tuple-element.50.mixed_ref, bf16[768,768]{1,0:T(8,128)(2,1)} %wo_ref.6), custom_call_target="tpu_custom_call" | custom-call | flops 301989888 | bytes 2359296 | tf_op jit(solution)/shard_map/pallas_call | solution.py:253
  81.9 5.1 %shard_map.115 = bf16[4,4,96,768]{3,2,1,0:T(8,128)(2,1)} custom-call(s32[3]{0:T(128)} %pad_add_fusion.pos_ref, bf16[2,384,256]{2,1,0:T(8,128)(2,1)} %get-tuple-element.52.l_ref, bf16[2,384,256]{2,1,0:T(8,128)(2,1)} %copy-done.12, bf16[256,2304]{1,0:T(8,128)(2,1)} %get-tuple-element.54.d_ref, bf16[256,2304]{1,0:T(8,128)(2,1)} %copy-done.9, ...), custom_call_target="tpu_custom_call" | custom-call | flops 1207959552 | bytes 6291468 | tf_op jit(solution)/shard_map/pallas_call | solution.py:253
  87.1 1.3 all-to-all-done.2
  88.4 5.0 %all-to-all-start.3 = ((bf16[4,4,96,768]{3,2,1,0:T(8,128)(2,1)}), bf16[4,4,96,768]{3,2,1,0:T(8,128)(2,1)S(1)}, u32[]{:S(2)}, u32[]{:S(2)}) async-start(bf16[4,4,96,768]{3,2,1,0:T(8,128)(2,1)} %shard_map.115), calls=%async_computation.3 | async-start | bytes 4718592 | tf_op jit(solution)/shard_map/all_to_all | solution.py:294
  93.4 1.3 copy-done.4
  94.7 1.3 copy-done.8
  95.9 4.0 %shard_map.116.dqkv_ref.d_ref = bf16[256,2304]{1,0:T(8,128)(2,1)S(1)} custom-call(bf16[256,768]{1,0:T(8,128)(2,1)S(1)} %bitcast.18, bf16[256,2304]{1,0:T(8,128)(2,1)S(1)} %copy-done.8, bf16[768,768]{1,0:T(8,128)(2,1)S(1)} %copy-done.4), custom_call_target="tpu_custom_call" | custom-call | flops 1207959552 | bytes 3932160 | tf_op jit(solution)/shard_map/pallas_call | solution.py:253
  100.0 1.4 collective-permute-start.4
  101.5 2.1 %shard_map.117 = bf16[256,768]{1,0:T(8,128)(2,1)} custom-call(bf16[256,768]{1,0:T(8,128)(2,1)S(1)} %bitcast.17, bf16[256,768]{1,0:T(8,128)(2,1)S(1)} %bitcast.20, bf16[256,2304]{1,0:T(8,128)(2,1)S(1)} %shard_map.116.dqkv_ref.d_ref, bf16[768,2304]{1,0:T(8,128)(2,1)S(1)} %copy-done), custom_call_target="tpu_custom_call" | custom-call | flops 905969664 | bytes 5898240 | tf_op jit(solution)/shard_map/pallas_call | solution.py:253
  105.6 5.1 %shard_map.118 = (bf16[4,96,768]{2,1,0:T(8,128)(2,1)}, bf16[4,96,768]{2,1,0:T(8,128)(2,1)}, bf16[4,96,768]{2,1,0:T(8,128)(2,1)}, bf16[4,96,768]{2,1,0:T(8,128)(2,1)}) custom-call(s32[3]{0:T(128)} %pad_add_fusion.pos_ref, bf16[2,384,256]{2,1,0:T(8,128)(2,1)} %get-tuple-element.60.l_ref, bf16[2,384,256]{2,1,0:T(8,128)(2,1)} %copy-done.15, ...), custom_call_target="tpu_custom_call" | custom-call | flops 1207959552 | bytes 6291468 | tf_op jit(solution)/shard_map/pallas_call | solution.py:253
  111.3 7.9 %all-to-all-start.4 = ((bf16[32,8,768]{2,1,0:T(8,128)(2,1)}), bf16[32,8,768]{2,1,0:T(8,128)(2,1)}, u32[]{:S(2)}, u32[]{:S(2)}) async-start(bf16[32,8,768]{2,1,0:T(8,128)(2,1)} %bitcast.12), calls=%async_computation.4 | async-start | bytes 786432 | tf_op jit(solution)/shard_map/all_to_all | solution.py:273
  119.8 2.7 %collective-permute-start.7 = (bf16[4,96,768]{2,1,0:T(8,128)(2,1)}, bf16[4,96,768]{2,1,0:T(8,128)(2,1)S(1)}, u32[]{:S(2)}, u32[]{:S(2)}) collective-permute-start(bf16[4,96,768]{2,1,0:T(8,128)(2,1)} %get-tuple-element.69), channel_id=1, source_target_pairs={{0,128},{64,192},{128,0},{192,64},{8,136},{72,200},{136,8},{200,72... | collective-permute-start | bytes 1769480 | tf_op jit(solution)/shard_map/ppermute | solution.py:299
  122.5 1.5 collective-permute-start.8
  124.0 6.6 %collective-permute-done.6.refs_1_ = bf16[4,96,768]{2,1,0:T(8,128)(2,1)S(1)} collective-permute-done((bf16[4,96,768]{2,1,0:T(8,128)(2,1)}, bf16[4,96,768]{2,1,0:T(8,128)(2,1)S(1)}, u32[]{:S(2)}, u32[]{:S(2)}) %collective-permute-start.6) | collective-permute-done | bytes 589856 | tf_op jit(solution)/shard_map/ppermute | solution.py:299
  130.6 6.3 %collective-permute-done.7.refs_2_ = bf16[4,96,768]{2,1,0:T(8,128)(2,1)S(1)} collective-permute-done((bf16[4,96,768]{2,1,0:T(8,128)(2,1)}, bf16[4,96,768]{2,1,0:T(8,128)(2,1)S(1)}, u32[]{:S(2)}, u32[]{:S(2)}) %collective-permute-start.7) | collective-permute-done | bytes 589856 | tf_op jit(solution)/shard_map/ppermute | solution.py:299
  139.4 14.7 %all_to_all.68.got_ref = bf16[4,96,1536]{2,1,0:T(8,128)(2,1)S(1)} all-to-all(bf16[4,96,1536]{2,1,0:T(8,128)(2,1)S(1)} %shard_map.119), channel_id=1, replica_groups={{1,65,129,193},{9,73,137,201},{17,81,145,209},{25,89,153,217},{0,8,16,2..., dimensions={0} | all-to-all | bytes 2359296 | tf_op jit(solution)/shard_map/all_to_all | solution.py:294
  154.3 18.8 %all_to_all.69.got_ref = bf16[4,24,1536]{2,1,0:T(8,128)(2,1)S(1)} all-to-all(bf16[4,24,1536]{2,1,0:T(8,128)(2,1)S(1)} %bitcast.22), channel_id=1, replica_groups=mesh['x'=4,'zl'=2,'y'=4,'zh'=4,'c'=2] {'zh'}, dimensions={0} | all-to-all | bytes 589824 | tf_op jit(solution)/shard_map/all_to_all | solution.py:273
  174.0 3.5 %all-to-all-start.7 = ((bf16[8,24,1536]{2,1,0:T(8,128)(2,1)}), bf16[8,24,1536]{2,1,0:T(8,128)(2,1)S(1)}, u32[]{:S(2)}, u32[]{:S(2)}) async-start(bf16[8,24,1536]{2,1,0:T(8,128)(2,1)} %shard_map.122), calls=%async_computation.7 | async-start | bytes 1179648 | tf_op jit(solution)/shard_map/all_to_all | solution.py:273
  177.5 2.0 %shard_map.120 = bf16[256,768]{1,0:T(8,128)(2,1)} custom-call(bf16[256,768]{1,0:T(8,128)(2,1)} %bitcast.13.x_ref), custom_call_target="tpu_custom_call" | custom-call | flops 100663296 | bytes 786432 | tf_op jit(solution)/shard_map/pallas_call | solution.py:253
  179.5 7.0 %all-to-all-done.7.got_ref = bf16[8,24,1536]{2,1,0:T(8,128)(2,1)S(1)} async-done(((bf16[8,24,1536]{2,1,0:T(8,128)(2,1)}), bf16[8,24,1536]{2,1,0:T(8,128)(2,1)S(1)}, u32[]{:S(2)}, u32[]{:S(2)}) %all-to-all-start.7) | async-done | bytes 589856 | tf_op jit(solution)/shard_map/all_to_all | solution.py:273
  (50 shorter events, 13.5 us)
Async XLA Ops:
  0.6 1.0 copy-start.7
  1.6 12.7 %copy-start.10 = (bf16[1,2,128,768]{3,2,1,0:T(8,128)(2,1)S(1)}, bf16[1,2,128,768]{3,2,1,0:T(8,128)(2,1)}, u32[]{:S(2)}) copy-start(bf16[1,2,128,768]{3,2,1,0:T(8,128)(2,1)} %param.7) | copy-start | bytes 1179652
  2.6 25.5 %all-to-all-start = ((bf16[32,8,768]{2,1,0:T(8,128)(2,1)}), bf16[32,8,768]{2,1,0:T(8,128)(2,1)S(1)}, u32[]{:S(2)}, u32[]{:S(2)}) async-start(bf16[32,8,768]{2,1,0:T(8,128)(2,1)} %bitcast.1), calls=%async_computation | async-start | bytes 786432 | tf_op jit(solution)/shard_map/all_to_all | solution.py:273
  14.4 1.8 collective-permute-start
  16.2 29.7 %copy-start.11 = (bf16[256,768]{1,0:T(8,128)(2,1)}, bf16[256,768]{1,0:T(8,128)(2,1)S(1)}, u32[]{:S(2)}) copy-start(bf16[256,768]{1,0:T(8,128)(2,1)S(1)} %collective-permute-done.g2_ref) | copy-start | bytes 1179652
  28.1 0.7 copy-start.1
  36.2 20.2 %all-to-all-start.1 = ((bf16[32,8,768]{2,1,0:T(8,128)(2,1)}), bf16[32,8,768]{2,1,0:T(8,128)(2,1)S(1)}, u32[]{:S(2)}, u32[]{:S(2)}) async-start(bf16[32,8,768]{2,1,0:T(8,128)(2,1)} %bitcast.29), calls=%async_computation.1 | async-start | bytes 786432 | tf_op jit(solution)/shard_map/all_to_all | solution.py:273
  45.9 1.9 %collective-permute-start.1 = (bf16[2,384,256]{2,1,0:T(8,128)(2,1)}, bf16[2,384,256]{2,1,0:T(8,128)(2,1)S(1)}, u32[]{:S(2)}, u32[]{:S(2)}) collective-permute-start(bf16[2,384,256]{2,1,0:T(8,128)(2,1)} %get-tuple-element.46), channel_id=1, source_target_pairs={{0,1},{1,0},{2,3},{3,2},{4,5},{5,4},{6,7},{7,6},{8,9},{9,8},{10,11... | collective-permute-start | bytes 1179656 | tf_op jit(solution)/shard_map/ppermute | solution.py:305
  47.9 20.8 %copy-start.15 = (bf16[2,384,256]{2,1,0:T(8,128)(2,1)}, bf16[2,384,256]{2,1,0:T(8,128)(2,1)S(1)}, u32[]{:S(2)}) copy-start(bf16[2,384,256]{2,1,0:T(8,128)(2,1)S(1)} %collective-permute-done.1.l2_ref) | copy-start | bytes 1179652
  56.4 0.7 copy-start.13
  68.7 12.1 %collective-permute-start.3 = (bf16[256,2304]{1,0:T(8,128)(2,1)}, bf16[256,2304]{1,0:T(8,128)(2,1)S(1)}, u32[]{:S(2)}, u32[]{:S(2)}) collective-permute-start(bf16[256,2304]{1,0:T(8,128)(2,1)} %get-tuple-element.54.d_ref), channel_id=1, source_target_pairs={{0,1},{1,0},{2,3},{3,2},{4,5},{5,4},{6,7},{7,6},{8,9},{9,8},{10,11... | collective-permute-start | bytes 3538952 | tf_op jit(solution)/shard_map/ppermute | solution.py:305
  70.0 18.4 %all-to-all-start.2 = ((bf16[32,8,768]{2,1,0:T(8,128)(2,1)}), bf16[32,8,768]{2,1,0:T(8,128)(2,1)S(1)}, u32[]{:S(2)}, u32[]{:S(2)}) async-start(bf16[32,8,768]{2,1,0:T(8,128)(2,1)} %bitcast.30), calls=%async_computation.2 | async-start | bytes 786432 | tf_op jit(solution)/shard_map/all_to_all | solution.py:273
  77.9 2.9 %collective-permute-start.2 = (bf16[2,384,256]{2,1,0:T(8,128)(2,1)}, bf16[2,384,256]{2,1,0:T(8,128)(2,1)S(1)}, u32[]{:S(2)}, u32[]{:S(2)}) collective-permute-start(bf16[2,384,256]{2,1,0:T(8,128)(2,1)} %get-tuple-element.53), channel_id=1, source_target_pairs={{0,1},{1,0},{2,3},{3,2},{4,5},{5,4},{6,7},{7,6},{8,9},{9,8},{10,11... | collective-permute-start | bytes 1179656 | tf_op jit(solution)/shard_map/ppermute | solution.py:305
  80.8 0.8 copy-start.12
  80.8 1.2 copy-start.9
  88.4 13.1 %copy-start.3 = (bf16[32,8,768]{2,1,0:T(8,128)(2,1)}, bf16[32,8,768]{2,1,0:T(8,128)(2,1)S(1)}, u32[]{:S(2)}) copy-start(bf16[32,8,768]{2,1,0:T(8,128)(2,1)S(1)} %all-to-all-done.2) | copy-start | bytes 1179652
  88.4 22.9 %all-to-all-start.3 = ((bf16[4,4,96,768]{3,2,1,0:T(8,128)(2,1)}), bf16[4,4,96,768]{3,2,1,0:T(8,128)(2,1)S(1)}, u32[]{:S(2)}, u32[]{:S(2)}) async-start(bf16[4,4,96,768]{3,2,1,0:T(8,128)(2,1)} %shard_map.115), calls=%async_computation.3 | async-start | bytes 4718592 | tf_op jit(solution)/shard_map/all_to_all | solution.py:294
  93.4 1.3 copy-start.4
  94.7 1.3 copy-start.8
  95.9 5.6 %copy-start = (bf16[768,2304]{1,0:T(8,128)(2,1)S(1)}, bf16[768,2304]{1,0:T(8,128)(2,1)}, u32[]{:S(2)}) copy-start(bf16[768,2304]{1,0:T(8,128)(2,1)} %wq_ref.5) | copy-start | bytes 10616836
  95.9 5.6 %copy-start.2 = (bf16[32,8,768]{2,1,0:T(8,128)(2,1)S(1)}, bf16[32,8,768]{2,1,0:T(8,128)(2,1)}, u32[]{:S(2)}) copy-start(bf16[32,8,768]{2,1,0:T(8,128)(2,1)} %copy-done.1) | copy-start | bytes 1179652
  100.0 3.6 %copy-start.5 = (bf16[256,2304]{1,0:T(8,128)(2,1)}, bf16[256,2304]{1,0:T(8,128)(2,1)S(1)}, u32[]{:S(2)}) copy-start(bf16[256,2304]{1,0:T(8,128)(2,1)S(1)} %shard_map.116.dqkv_ref.d_ref) | copy-start | bytes 3538948
  100.0 4.4 %collective-permute-start.4 = (bf16[256,2304]{1,0:T(8,128)(2,1)S(1)}, bf16[256,2304]{1,0:T(8,128)(2,1)S(1)}, u32[]{:S(2)}, u32[]{:S(2)}) collective-permute-start(bf16[256,2304]{1,0:T(8,128)(2,1)S(1)} %shard_map.116.dqkv_ref.d_ref), channel_id=1, source_target_pairs={{0,1},{1,0},{2,3},{3,2},{4,5},{5,4},{6,7},{7,6},{8,9},{9,8},{10,11... | collective-permute-start | bytes 3538952 | tf_op jit(solution)/shard_map/ppermute | solution.py:305
  101.4 3.0 %collective-permute-start.5 = (bf16[256,768]{1,0:T(8,128)(2,1)S(1)}, bf16[256,768]{1,0:T(8,128)(2,1)S(1)}, u32[]{:S(2)}, u32[]{:S(2)}) collective-permute-start(bf16[256,768]{1,0:T(8,128)(2,1)S(1)} %bitcast.19), channel_id=1, source_target_pairs={{0,1},{1,0},{2,3},{3,2},{4,5},{5,4},{6,7},{7,6},{8,9},{9,8},{10,11... | collective-permute-start | bytes 1179656 | tf_op jit(solution)/shard_map/ppermute | solution.py:305
  104.4 1.2 copy-start.16
  104.4 1.1 copy-start.14
  111.3 28.1 %all-to-all-start.4 = ((bf16[32,8,768]{2,1,0:T(8,128)(2,1)}), bf16[32,8,768]{2,1,0:T(8,128)(2,1)}, u32[]{:S(2)}, u32[]{:S(2)}) async-start(bf16[32,8,768]{2,1,0:T(8,128)(2,1)} %bitcast.12), calls=%async_computation.4 | async-start | bytes 786432 | tf_op jit(solution)/shard_map/all_to_all | solution.py:273
  119.2 11.4 %collective-permute-start.6 = (bf16[4,96,768]{2,1,0:T(8,128)(2,1)}, bf16[4,96,768]{2,1,0:T(8,128)(2,1)S(1)}, u32[]{:S(2)}, u32[]{:S(2)}) collective-permute-start(bf16[4,96,768]{2,1,0:T(8,128)(2,1)} %get-tuple-element.68), channel_id=1, source_target_pairs={{0,64},{64,128},{128,192},{192,0},{8,72},{72,136},{136,200},{200,8... | collective-permute-start | bytes 1769480 | tf_op jit(solution)/shard_map/ppermute | solution.py:299
  119.8 17.1 %collective-permute-start.7 = (bf16[4,96,768]{2,1,0:T(8,128)(2,1)}, bf16[4,96,768]{2,1,0:T(8,128)(2,1)S(1)}, u32[]{:S(2)}, u32[]{:S(2)}) collective-permute-start(bf16[4,96,768]{2,1,0:T(8,128)(2,1)} %get-tuple-element.69), channel_id=1, source_target_pairs={{0,128},{64,192},{128,0},{192,64},{8,136},{72,200},{136,8},{200,72... | collective-permute-start | bytes 1769480 | tf_op jit(solution)/shard_map/ppermute | solution.py:299
  122.5 15.3 %collective-permute-start.8 = (bf16[4,96,768]{2,1,0:T(8,128)(2,1)}, bf16[4,96,768]{2,1,0:T(8,128)(2,1)S(1)}, u32[]{:S(2)}, u32[]{:S(2)}) collective-permute-start(bf16[4,96,768]{2,1,0:T(8,128)(2,1)} %get-tuple-element.70), channel_id=1, source_target_pairs={{0,192},{64,0},{128,64},{192,128},{8,200},{72,8},{136,72},{200,136... | collective-permute-start | bytes 1769480 | tf_op jit(solution)/shard_map/ppermute | solution.py:299
  137.8 1.1 copy-start.6
  174.0 12.5 %all-to-all-start.7 = ((bf16[8,24,1536]{2,1,0:T(8,128)(2,1)}), bf16[8,24,1536]{2,1,0:T(8,128)(2,1)S(1)}, u32[]{:S(2)}, u32[]{:S(2)}) async-start(bf16[8,24,1536]{2,1,0:T(8,128)(2,1)} %shard_map.122), calls=%async_computation.7 | async-start | bytes 1179648 | tf_op jit(solution)/shard_map/all_to_all | solution.py:273

commit v4 on v3

--- a/solution.py
+++ b/solution.py
@@ -144,7 +144,11 @@
                 mixed_ref[rows, at[0]] = dot(jnp.concatenate(ws, axis=0), vs, TN).astype(BF)
 
 
-def space_kernel(m_ref, cot_ref, wq_ref, wo_ref, grad_ref, dqkv_ref, x_ref, low_ref, mixed_ref, qkv_ref, g_ref):
+def project_back_kernel(cot_ref, wo_ref, g_ref):
+    g_ref[...] = dot(cot_ref[...], wo_ref[...], NT).astype(BF)
+
+
+def space_kernel(m_ref, cot_ref, g_ref, wq_ref, grad_ref, dqkv_ref, x_ref, low_ref, mixed_ref, qkv_ref):
     x_ref[...] = dot(order(False), m_ref[...]).astype(BF)
     normed, inverse = normalize(x_ref[...].astype(F32))
     low = normed.astype(BF)
@@ -152,11 +156,9 @@
     for i in range(9):
         cols = slice(i * 256, (i + 1) * 256)
         qkv_ref[:, cols] = dot(low, wq_ref[:, cols]).astype(BF)
-    cot = cot_ref[...]
-    g_ref[...] = dot(cot, wo_ref[...], NT).astype(BF)
     attend_back(qkv_ref, g_ref, dqkv_ref, mixed_ref, None, 2)
     grad = dot(dqkv_ref[...], wq_ref[...], NT)
-    grad = cot.astype(F32) + normalize_back(normed, inverse, grad)
+    grad = cot_ref[...].astype(F32) + normalize_back(normed, inverse, grad)
     grad_ref[...] = dot(order(True), grad.astype(BF)).astype(BF)
 
 
@@ -215,15 +217,15 @@
     return total.astype(BF)
 
 
-def first_sum_kernel(got_ref, o_ref):
-    o_ref[...] = add_first(got_ref)
-
-
-def pieces_kernel(s_ref, *refs):
-    o_ref = refs[4]
-    for i in range(4):
-        o_ref[i, :, :D] = add([ref.at[i] for ref in refs[:4]])
-        o_ref[i, :, D:] = add([s_ref.at[k, i] for k in range(4)])
+def sum_kernel(*refs):
+    refs[4][...] = add(refs[:4])
+
+
+def pieces_kernel(pos_ref, s_ref, *refs):
+    for k in range(4):
+        owner = turned(pos_ref[3], k)
+        refs[4 + k][:, :D] = add([ref.at[owner] for ref in refs[:4]])
+        refs[4 + k][:, D:] = add([s_ref.at[i, owner] for i in range(4)])
 
 
 def copies_kernel(got_ref, o_ref):
@@ -311,7 +313,7 @@
 
 def on_device(tokens, block_cotangent, time_qkv, time_out, space_qkv, space_out):
     x_at, y_at, core = (lax.axis_index(axis).astype(jnp.int32) for axis in ("x", "y", "c"))
-    pos = jnp.stack([x_at, core, jnp.where(core == 0, x_at, y_at)])
+    pos = jnp.stack([x_at, core, jnp.where(core == 0, x_at, y_at), jnp.where(core == 0, y_at, x_at)])
     cot = block_cotangent.reshape(T, D)
     x = a2a(permuted(tokens.reshape(T, D), True), FP)
     x, cot_other = after(x, swap(cot))
@@ -323,13 +325,14 @@
     )
     middle = a2a(middle, FP)
     t_own, t_send = factors(pos, t_low, t_mixed)
-    middle, t_other = after(middle, swap(t_send))
+    s_dmixed = call(project_back_kernel, [sds(T, D)], [cot, space_out], OUTP, mib=WHOLE)[0]
+    middle, t_other, s_dmixed = after(middle, swap(t_send), s_dmixed)
     grad_middle, s_dqkv, natural, s_low, s_mixed = call(
         space_kernel,
         [sds(T, D), sds(T, 3 * D), sds(T, D), sds(T, D), sds(T, D)],
-        [middle, cot, space_qkv, space_out],
-        2 * (PROJ + OUTP),
-        [pltpu.VMEM((T, 3 * D), BF), pltpu.VMEM((T, D), BF)], mib=WHOLE,
+        [middle, cot, s_dmixed, space_qkv],
+        2 * PROJ,
+        [pltpu.VMEM((T, 3 * D), BF)], mib=WHOLE,
     )
     grad_middle = a2a(grad_middle, FP)
     s_own, s_send = factors(pos, s_low, s_mixed)
@@ -348,9 +351,11 @@
     )
     grad_tokens, space, *time = after(grad_tokens, space, *time)
     tokens_grad = a2a(grad_tokens, FP)
-    got = call(pieces_kernel, [sds(4, BLOCK, 2 * D)], [space, *crossed_steps(time, 1)], 0)[0]
+    pieces = call(
+        pieces_kernel, [sds(BLOCK, 2 * D)] * 4, [pos, space, *crossed_steps(time, 1)], 0,
+    )
+    got = call(sum_kernel, [sds(BLOCK, 2 * D)], crossed_steps(pieces, 0), 0)[0]
     got, tokens_grad = after(got, tokens_grad)
-    got = call(first_sum_kernel, [sds(BLOCK, 2 * D)], [crossed(got, 0)], 0)[0]
     got = a2a(got.reshape(4, ROWS, 2 * D), ("zh",))
     tokens_grad = permuted(tokens_grad, False)
     shares = call(copies_kernel, [sds(8, ROWS, 2 * D)], [got], 0)[0]

time: 188 us -> 177 us (0.941)
  blocking collectives: 33.5 us -> 16 us
  starting transfers between devices: 47.8 us -> 53.1 us
  Pallas kernels: 48.9 us -> 51.2 us
    all_to_all x1 -> x0, blocking collectives: 14.7 us -> none  [crossed(): lax.all_to_all(x, ('x', 'y', 'c'), 0, 0, tiled=True, axis_index_groups=ri...]
    ppermute x3 -> x6, starting transfers between devices: 4.78 us -> 9.71 us  [crossed_steps(): lax.ppermute(pieces[k], ('x', 'y', 'c'), [(ring[i], ring[(i + k) % 4]) fo...]
    all_to_all x1, blocking collectives: 18.8 us -> 16 us  [a2a(): return lax.all_to_all(x, axes, 0, 0, tiled=True)]
    pallas_call x15 -> x16, Pallas kernels: 48.9 us -> 51.2 us  [call(): pl.pallas_call(kernel, out_shape=outs, in_specs=[SMEM if a.dtype == jnp.i...]
    unnamed x34 -> x36, local copies, waits for them, and re-layouts: 8.47 us -> 7.43 us
    ppermute x3 -> x6, waiting for transfers between devices: 13.8 us -> 14.2 us  [crossed_steps(): lax.ppermute(pieces[k], ('x', 'y', 'c'), [(ring[i], ring[(i + k) % 4]) fo...]
  transfers between devices with their start and end apart: 15 -> 18, of which waited for: 11 -> 12; matrix products, arithmetic and copies ran while one was open for 0% -> 0% of each run, Pallas kernels for 14% -> 17%
where the time goes in v4:
time: 177 us; the launch traced here: 176 us
  starting transfers between devices  53.1 us (30%)
  Pallas kernels  51.2 us (29%)
  waiting for transfers between devices  46.6 us (26%)
  blocking collectives  16 us (9%)
  local copies, waits for them, and re-layouts  7.43 us (4%)
    pallas_call x16, Pallas kernels, call(): pl.pallas_call(kernel, out_shape=outs, in_specs=[SMEM if a.dtype == jnp.i...  51.2 us
    all_to_all x5, starting transfers between devices, a2a(): return lax.all_to_all(x, axes, 0, 0, tiled=True)  35 us
    all_to_all x5, waiting for transfers between devices, a2a(): return lax.all_to_all(x, axes, 0, 0, tiled=True)  29.5 us
    all_to_all x1, blocking collectives, a2a(): return lax.all_to_all(x, axes, 0, 0, tiled=True)  16 us
    ppermute x6, waiting for transfers between devices, crossed_steps(): lax.ppermute(pieces[k], ('x', 'y', 'c'), [(ring[i], ring[(i + k) % 4]) fo...  14.2 us
    ppermute x6, starting transfers between devices, crossed_steps(): lax.ppermute(pieces[k], ('x', 'y', 'c'), [(ring[i], ring[(i + k) % 4]) fo...  9.71 us
    unnamed x36, local copies, waits for them, and re-layouts  7.43 us
    all_to_all x1, starting transfers between devices, crossed(): lax.all_to_all(x, ('x', 'y', 'c'), 0, 0, tiled=True, axis_index_groups=ri...  4.99 us
  transfers between devices with their start and end apart: 18, of which 12 were waited for; matrix products, arithmetic and copies ran while one was open for 0% of the time, Pallas kernels for 17%

profile of v4, /device:TPU:8, one launch (start us, length us, event | category | flops | bytes accessed | tf_op | source)
XLA Modules:
  0.0 175.7 jit_solution(2925432782875336881)
XLA Ops:
  2.6 11.7 %all-to-all-start = ((bf16[32,8,768]{2,1,0:T(8,128)(2,1)}), bf16[32,8,768]{2,1,0:T(8,128)(2,1)S(1)}, u32[]{:S(2)}, u32[]{:S(2)}) async-start(bf16[32,8,768]{2,1,0:T(8,128)(2,1)} %bitcast.1), calls=%async_computation | async-start | bytes 786432 | tf_op jit(solution)/shard_map/all_to_all | solution.py:275
  14.6 1.6 collective-permute-done.g2_ref
  16.2 12.0 %all-to-all-done = bf16[32,8,768]{2,1,0:T(8,128)(2,1)S(1)} async-done(((bf16[32,8,768]{2,1,0:T(8,128)(2,1)}), bf16[32,8,768]{2,1,0:T(8,128)(2,1)S(1)}, u32[]{:S(2)}, u32[]{:S(2)}) %all-to-all-start) | async-done | bytes 393248 | tf_op jit(solution)/shard_map/all_to_all | solution.py:275
  28.9 7.4 %shard_map.110 = (bf16[256,768]{1,0:T(8,128)(2,1)}, bf16[256,2304]{1,0:T(8,128)(2,1)}, bf16[256,768]{1,0:T(8,128)(2,1)}, bf16[256,768]{1,0:T(8,128)(2,1)}) custom-call(bf16[256,768]{1,0:T(8,128)(2,1)} %bitcast.17, bf16[768,2304]{1,0:T(8,128)(2,1)} %wq_ref.5, bf16[768,768]{1,0:T(8,128)(2,1)} %wo_ref.7), custom_call_target="tpu_custom_call" | custom-call | flops 1207959552 | bytes 7471104 | tf_op jit(solution)/shard_map/pallas_call | solution.py:255
  36.2 6.4 %all-to-all-start.1 = ((bf16[32,8,768]{2,1,0:T(8,128)(2,1)}), bf16[32,8,768]{2,1,0:T(8,128)(2,1)S(1)}, u32[]{:S(2)}, u32[]{:S(2)}) async-start(bf16[32,8,768]{2,1,0:T(8,128)(2,1)} %bitcast.32), calls=%async_computation.1 | async-start | bytes 786432 | tf_op jit(solution)/shard_map/all_to_all | solution.py:275
  43.3 2.7 %shard_map.111 = (bf16[2,384,256]{2,1,0:T(8,128)(2,1)}, bf16[2,384,256]{2,1,0:T(8,128)(2,1)}) custom-call(s32[4]{0:T(128)} %pad_add_fusion.pos_ref, bf16[256,768]{1,0:T(8,128)(2,1)} %get-tuple-element.49.low_ref, bf16[256,768]{1,0:T(8,128)(2,1)} %get-tuple-element.50.mixed_ref), custom_call_target="tpu_custom_call" | custom-call | flops 603979776 | bytes 1572880 | tf_op jit(solution)/shard_map/pallas_call | solution.py:255
  46.1 2.6 %shard_map.112.g_ref = bf16[256,768]{1,0:T(8,128)(2,1)} custom-call(bf16[256,768]{1,0:T(8,128)(2,1)} %bitcast.26, bf16[768,768]{1,0:T(8,128)(2,1)} %wo_ref.6), custom_call_target="tpu_custom_call" | custom-call | flops 301989888 | bytes 1966080 | tf_op jit(solution)/shard_map/pallas_call | solution.py:255
  48.8 7.6 %all-to-all-done.1 = bf16[32,8,768]{2,1,0:T(8,128)(2,1)S(1)} async-done(((bf16[32,8,768]{2,1,0:T(8,128)(2,1)}), bf16[32,8,768]{2,1,0:T(8,128)(2,1)S(1)}, u32[]{:S(2)}, u32[]{:S(2)}) %all-to-all-start.1) | async-done | bytes 393248 | tf_op jit(solution)/shard_map/all_to_all | solution.py:275
  57.2 10.7 %shard_map.113 = (bf16[256,768]{1,0:T(8,128)(2,1)}, bf16[256,2304]{1,0:T(8,128)(2,1)}, bf16[256,768]{1,0:T(8,128)(2,1)}, bf16[256,768]{1,0:T(8,128)(2,1)}, bf16[256,768]{1,0:T(8,128)(2,1)}) custom-call(bf16[256,768]{1,0:T(8,128)(2,1)} %bitcast.31, bf16[256,768]{1,0:T(8,128)(2,1)} %bitcast.27, bf16[256,768]{1,0:T(8,128)(2,1)} %shard_map.112.g_ref, ...), custom_call_target="tpu_custom_call" | custom-call | flops 1811939328 | bytes 7471104 | tf_op jit(solution)/shard_map/pallas_call | solution.py:255
  67.8 1.4 collective-permute-start.3
  69.2 5.1 %all-to-all-start.2 = ((bf16[32,8,768]{2,1,0:T(8,128)(2,1)}), bf16[32,8,768]{2,1,0:T(8,128)(2,1)S(1)}, u32[]{:S(2)}, u32[]{:S(2)}) async-start(bf16[32,8,768]{2,1,0:T(8,128)(2,1)} %bitcast.33), calls=%async_computation.2 | async-start | bytes 786432 | tf_op jit(solution)/shard_map/all_to_all | solution.py:275
  74.3 2.7 %shard_map.115 = (bf16[2,384,256]{2,1,0:T(8,128)(2,1)}, bf16[2,384,256]{2,1,0:T(8,128)(2,1)}) custom-call(s32[4]{0:T(128)} %pad_add_fusion.pos_ref, bf16[256,768]{1,0:T(8,128)(2,1)} %get-tuple-element.57.low_ref, bf16[256,768]{1,0:T(8,128)(2,1)} %get-tuple-element.56.mixed_ref), custom_call_target="tpu_custom_call" | custom-call | flops 603979776 | bytes 1572880 | tf_op jit(solution)/shard_map/pallas_call | solution.py:255
  77.2 2.7 %shard_map.114 = bf16[256,768]{1,0:T(8,128)(2,1)} custom-call(bf16[256,768]{1,0:T(8,128)(2,1)} %get-tuple-element.55.x_ref, bf16[256,768]{1,0:T(8,128)(2,1)} %get-tuple-element.56.mixed_ref, bf16[768,768]{1,0:T(8,128)(2,1)} %wo_ref.6), custom_call_target="tpu_custom_call" | custom-call | flops 301989888 | bytes 2359296 | tf_op jit(solution)/shard_map/pallas_call | solution.py:255
  81.1 5.1 %shard_map.116 = bf16[4,4,96,768]{3,2,1,0:T(8,128)(2,1)} custom-call(s32[4]{0:T(128)} %pad_add_fusion.pos_ref, bf16[2,384,256]{2,1,0:T(8,128)(2,1)} %get-tuple-element.58.l_ref, bf16[2,384,256]{2,1,0:T(8,128)(2,1)} %copy-done.13, bf16[256,2304]{1,0:T(8,128)(2,1)} %get-tuple-element.60.d_ref, bf16[256,2304]{1,0:T(8,128)(2,1)} %copy-done.11, ...), custom_call_target="tpu_custom_call" | custom-call | flops 1207959552 | bytes 6291472 | tf_op jit(solution)/shard_map/pallas_call | solution.py:255
  86.2 1.3 all-to-all-done.2
  87.6 5.0 %all-to-all-start.3 = ((bf16[4,4,96,768]{3,2,1,0:T(8,128)(2,1)}), bf16[4,4,96,768]{3,2,1,0:T(8,128)(2,1)S(1)}, u32[]{:S(2)}, u32[]{:S(2)}) async-start(bf16[4,4,96,768]{3,2,1,0:T(8,128)(2,1)} %shard_map.116), calls=%async_computation.3 | async-start | bytes 4718592 | tf_op jit(solution)/shard_map/all_to_all | solution.py:296
  95.1 4.1 %shard_map.117.dqkv_ref.d_ref = bf16[256,2304]{1,0:T(8,128)(2,1)S(1)} custom-call(bf16[256,768]{1,0:T(8,128)(2,1)S(1)} %bitcast.20, bf16[256,2304]{1,0:T(8,128)(2,1)S(1)} %copy-done.9, bf16[768,768]{1,0:T(8,128)(2,1)S(1)} %copy-done.4), custom_call_target="tpu_custom_call" | custom-call | flops 1207959552 | bytes 3932160 | tf_op jit(solution)/shard_map/pallas_call | solution.py:255
  99.2 1.4 collective-permute-start.4
  100.7 2.1 %shard_map.118 = bf16[256,768]{1,0:T(8,128)(2,1)} custom-call(bf16[256,768]{1,0:T(8,128)(2,1)S(1)} %bitcast.18, bf16[256,768]{1,0:T(8,128)(2,1)S(1)} %bitcast.22, bf16[256,2304]{1,0:T(8,128)(2,1)S(1)} %shard_map.117.dqkv_ref.d_ref, bf16[768,2304]{1,0:T(8,128)(2,1)S(1)} %copy-done), custom_call_target="tpu_custom_call" | custom-call | flops 905969664 | bytes 5898240 | tf_op jit(solution)/shard_map/pallas_call | solution.py:255
  104.8 5.2 %shard_map.119 = (bf16[4,96,768]{2,1,0:T(8,128)(2,1)}, bf16[4,96,768]{2,1,0:T(8,128)(2,1)}, bf16[4,96,768]{2,1,0:T(8,128)(2,1)}, bf16[4,96,768]{2,1,0:T(8,128)(2,1)}) custom-call(s32[4]{0:T(128)} %pad_add_fusion.pos_ref, bf16[2,384,256]{2,1,0:T(8,128)(2,1)} %get-tuple-element.66.l_ref, bf16[2,384,256]{2,1,0:T(8,128)(2,1)} %copy-done.16, ...), custom_call_target="tpu_custom_call" | custom-call | flops 1207959552 | bytes 6291472 | tf_op jit(solution)/shard_map/pallas_call | solution.py:255
  111.5 2.8 %collective-permute-start.7 = (bf16[4,96,768]{2,1,0:T(8,128)(2,1)}, bf16[4,96,768]{2,1,0:T(8,128)(2,1)}, u32[]{:S(2)}, u32[]{:S(2)}) collective-permute-start(bf16[4,96,768]{2,1,0:T(8,128)(2,1)} %get-tuple-element.75), channel_id=1, source_target_pairs={{0,128},{64,192},{128,0},{192,64},{8,136},{72,200},{136,8},{200,72... | collective-permute-start | bytes 1769480 | tf_op jit(solution)/shard_map/ppermute | solution.py:301
  114.3 1.3 collective-permute-start.8
  115.6 7.5 %all-to-all-start.4 = ((bf16[32,8,768]{2,1,0:T(8,128)(2,1)}), bf16[32,8,768]{2,1,0:T(8,128)(2,1)S(1)}, u32[]{:S(2)}, u32[]{:S(2)}) async-start(bf16[32,8,768]{2,1,0:T(8,128)(2,1)} %bitcast.13), calls=%async_computation.4 | async-start | bytes 786432 | tf_op jit(solution)/shard_map/all_to_all | solution.py:275
  123.1 5.7 %collective-permute-done.7.refs_2_ = bf16[4,96,768]{2,1,0:T(8,128)(2,1)} collective-permute-done((bf16[4,96,768]{2,1,0:T(8,128)(2,1)}, bf16[4,96,768]{2,1,0:T(8,128)(2,1)}, u32[]{:S(2)}, u32[]{:S(2)}) %collective-permute-start.7) | collective-permute-done | bytes 589856 | tf_op jit(solution)/shard_map/ppermute | solution.py:301
  129.1 2.0 %shard_map.120 = (bf16[96,1536]{1,0:T(8,128)(2,1)S(1)}, bf16[96,1536]{1,0:T(8,128)(2,1)S(1)}, bf16[96,1536]{1,0:T(8,128)(2,1)S(1)}, bf16[96,1536]{1,0:T(8,128)(2,1)S(1)}) custom-call(s32[4]{0:T(128)S(1)} %copy-done.8, bf16[4,4,96,768]{3,2,1,0:T(8,128)(2,1)S(1)} %all-to-all-done.3.s_ref, bf16[4,96,768]{2,1,0:T(8,128)(2,1)S(1)} %copy-done.6, ...), custom_call_target="tpu_custom_call" | custom-call | tf_op jit(solution)/shard_map/pallas_call | solution.py:255
  132.4 3.2 %collective-permute-start.10 = (bf16[96,1536]{1,0:T(8,128)(2,1)S(1)}, bf16[96,1536]{1,0:T(8,128)(2,1)S(1)}, u32[]{:S(2)}, u32[]{:S(2)}) collective-permute-start(bf16[96,1536]{1,0:T(8,128)(2,1)S(1)} %get-tuple-element.79), channel_id=1, source_target_pairs={{1,129},{65,193},{129,1},{193,65},{9,137},{73,201},{137,9},{201,73... | collective-permute-start | bytes 884744 | tf_op jit(solution)/shard_map/ppermute | solution.py:301
  135.7 2.7 %collective-permute-done.9.refs_1_ = bf16[96,1536]{1,0:T(8,128)(2,1)S(1)} collective-permute-done((bf16[96,1536]{1,0:T(8,128)(2,1)S(1)}, bf16[96,1536]{1,0:T(8,128)(2,1)S(1)}, u32[]{:S(2)}, u32[]{:S(2)}) %collective-permute-start.9) | collective-permute-done | bytes 294944 | tf_op jit(solution)/shard_map/ppermute | solution.py:301
  138.4 2.4 %collective-permute-done.10.refs_2_ = bf16[96,1536]{1,0:T(8,128)(2,1)S(1)} collective-permute-done((bf16[96,1536]{1,0:T(8,128)(2,1)S(1)}, bf16[96,1536]{1,0:T(8,128)(2,1)S(1)}, u32[]{:S(2)}, u32[]{:S(2)}) %collective-permute-start.10) | collective-permute-done | bytes 294944 | tf_op jit(solution)/shard_map/ppermute | solution.py:301
  140.8 3.1 %collective-permute-done.11.refs_3_ = bf16[96,1536]{1,0:T(8,128)(2,1)S(1)} collective-permute-done((bf16[96,1536]{1,0:T(8,128)(2,1)S(1)}, bf16[96,1536]{1,0:T(8,128)(2,1)S(1)}, u32[]{:S(2)}, u32[]{:S(2)}) %collective-permute-start.11) | collective-permute-done | bytes 294944 | tf_op jit(solution)/shard_map/ppermute | solution.py:301
  144.1 16.0 %all_to_all.63.got_ref = bf16[4,24,1536]{2,1,0:T(8,128)(2,1)S(1)} all-to-all(bf16[4,24,1536]{2,1,0:T(8,128)(2,1)S(1)} %bitcast.24), channel_id=1, replica_groups=mesh['x'=4,'zl'=2,'y'=4,'zh'=4,'c'=2] {'zh'}, dimensions={0} | all-to-all | bytes 589824 | tf_op jit(solution)/shard_map/all_to_all | solution.py:275
  160.9 4.2 %all-to-all-start.6 = ((bf16[8,24,1536]{2,1,0:T(8,128)(2,1)}), bf16[8,24,1536]{2,1,0:T(8,128)(2,1)S(1)}, u32[]{:S(2)}, u32[]{:S(2)}) async-start(bf16[8,24,1536]{2,1,0:T(8,128)(2,1)} %shard_map.123), calls=%async_computation.6 | async-start | bytes 1179648 | tf_op jit(solution)/shard_map/all_to_all | solution.py:275
  166.2 8.6 %all-to-all-done.6.got_ref = bf16[8,24,1536]{2,1,0:T(8,128)(2,1)S(1)} async-done(((bf16[8,24,1536]{2,1,0:T(8,128)(2,1)}), bf16[8,24,1536]{2,1,0:T(8,128)(2,1)S(1)}, u32[]{:S(2)}, u32[]{:S(2)}) %all-to-all-start.6) | async-done | bytes 589856 | tf_op jit(solution)/shard_map/all_to_all | solution.py:275
  (58 shorter events, 16.8 us)
Async XLA Ops:
  1.6 12.7 %copy-start.10 = (bf16[1,2,128,768]{3,2,1,0:T(8,128)(2,1)S(1)}, bf16[1,2,128,768]{3,2,1,0:T(8,128)(2,1)}, u32[]{:S(2)}) copy-start(bf16[1,2,128,768]{3,2,1,0:T(8,128)(2,1)} %param.7) | copy-start | bytes 1179652
  2.6 25.5 %all-to-all-start = ((bf16[32,8,768]{2,1,0:T(8,128)(2,1)}), bf16[32,8,768]{2,1,0:T(8,128)(2,1)S(1)}, u32[]{:S(2)}, u32[]{:S(2)}) async-start(bf16[32,8,768]{2,1,0:T(8,128)(2,1)} %bitcast.1), calls=%async_computation | async-start | bytes 786432 | tf_op jit(solution)/shard_map/all_to_all | solution.py:275
  14.4 1.8 %collective-permute-start = (bf16[256,768]{1,0:T(8,128)(2,1)S(1)}, bf16[256,768]{1,0:T(8,128)(2,1)S(1)}, u32[]{:S(2)}, u32[]{:S(2)}) collective-permute-start(bf16[256,768]{1,0:T(8,128)(2,1)S(1)} %bitcast.29), channel_id=1, source_target_pairs={{0,1},{1,0},{2,3},{3,2},{4,5},{5,4},{6,7},{7,6},{8,9},{9,8},{10,11... | collective-permute-start | bytes 1179656 | tf_op jit(solution)/shard_map/ppermute | solution.py:307
  16.2 29.8 %copy-start.12 = (bf16[256,768]{1,0:T(8,128)(2,1)}, bf16[256,768]{1,0:T(8,128)(2,1)S(1)}, u32[]{:S(2)}) copy-start(bf16[256,768]{1,0:T(8,128)(2,1)S(1)} %collective-permute-done.g2_ref) | copy-start | bytes 1179652
  36.2 20.2 %all-to-all-start.1 = ((bf16[32,8,768]{2,1,0:T(8,128)(2,1)}), bf16[32,8,768]{2,1,0:T(8,128)(2,1)S(1)}, u32[]{:S(2)}, u32[]{:S(2)}) async-start(bf16[32,8,768]{2,1,0:T(8,128)(2,1)} %bitcast.32), calls=%async_computation.1 | async-start | bytes 786432 | tf_op jit(solution)/shard_map/all_to_all | solution.py:275
  46.0 2.8 %collective-permute-start.1 = (bf16[2,384,256]{2,1,0:T(8,128)(2,1)}, bf16[2,384,256]{2,1,0:T(8,128)(2,1)S(1)}, u32[]{:S(2)}, u32[]{:S(2)}) collective-permute-start(bf16[2,384,256]{2,1,0:T(8,128)(2,1)} %get-tuple-element.51), channel_id=1, source_target_pairs={{0,1},{1,0},{2,3},{3,2},{4,5},{5,4},{6,7},{7,6},{8,9},{9,8},{10,11... | collective-permute-start | bytes 1179656 | tf_op jit(solution)/shard_map/ppermute | solution.py:307
  48.8 20.4 %copy-start.16 = (bf16[2,384,256]{2,1,0:T(8,128)(2,1)}, bf16[2,384,256]{2,1,0:T(8,128)(2,1)S(1)}, u32[]{:S(2)}) copy-start(bf16[2,384,256]{2,1,0:T(8,128)(2,1)S(1)} %collective-permute-done.1.l2_ref) | copy-start | bytes 1179652
  67.8 12.1 %collective-permute-start.3 = (bf16[256,2304]{1,0:T(8,128)(2,1)}, bf16[256,2304]{1,0:T(8,128)(2,1)S(1)}, u32[]{:S(2)}, u32[]{:S(2)}) collective-permute-start(bf16[256,2304]{1,0:T(8,128)(2,1)} %get-tuple-element.60.d_ref), channel_id=1, source_target_pairs={{0,1},{1,0},{2,3},{3,2},{4,5},{5,4},{6,7},{7,6},{8,9},{9,8},{10,11... | collective-permute-start | bytes 3538952 | tf_op jit(solution)/shard_map/ppermute | solution.py:307
  69.2 18.4 %all-to-all-start.2 = ((bf16[32,8,768]{2,1,0:T(8,128)(2,1)}), bf16[32,8,768]{2,1,0:T(8,128)(2,1)S(1)}, u32[]{:S(2)}, u32[]{:S(2)}) async-start(bf16[32,8,768]{2,1,0:T(8,128)(2,1)} %bitcast.33), calls=%async_computation.2 | async-start | bytes 786432 | tf_op jit(solution)/shard_map/all_to_all | solution.py:275
  77.0 2.9 %collective-permute-start.2 = (bf16[2,384,256]{2,1,0:T(8,128)(2,1)}, bf16[2,384,256]{2,1,0:T(8,128)(2,1)S(1)}, u32[]{:S(2)}, u32[]{:S(2)}) collective-permute-start(bf16[2,384,256]{2,1,0:T(8,128)(2,1)} %get-tuple-element.59), channel_id=1, source_target_pairs={{0,1},{1,0},{2,3},{3,2},{4,5},{5,4},{6,7},{7,6},{8,9},{9,8},{10,11... | collective-permute-start | bytes 1179656 | tf_op jit(solution)/shard_map/ppermute | solution.py:307
  79.9 1.2 copy-start.11
  87.6 13.1 %copy-start.3 = (bf16[32,8,768]{2,1,0:T(8,128)(2,1)}, bf16[32,8,768]{2,1,0:T(8,128)(2,1)S(1)}, u32[]{:S(2)}) copy-start(bf16[32,8,768]{2,1,0:T(8,128)(2,1)S(1)} %all-to-all-done.2) | copy-start | bytes 1179652
  87.6 22.9 %all-to-all-start.3 = ((bf16[4,4,96,768]{3,2,1,0:T(8,128)(2,1)}), bf16[4,4,96,768]{3,2,1,0:T(8,128)(2,1)S(1)}, u32[]{:S(2)}, u32[]{:S(2)}) async-start(bf16[4,4,96,768]{3,2,1,0:T(8,128)(2,1)} %shard_map.116), calls=%async_computation.3 | async-start | bytes 4718592 | tf_op jit(solution)/shard_map/all_to_all | solution.py:296
  92.6 1.3 copy-start.4
  93.8 1.3 copy-start.9
  95.1 5.6 %copy-start = (bf16[768,2304]{1,0:T(8,128)(2,1)S(1)}, bf16[768,2304]{1,0:T(8,128)(2,1)}, u32[]{:S(2)}) copy-start(bf16[768,2304]{1,0:T(8,128)(2,1)} %wq_ref.5) | copy-start | bytes 10616836
  95.1 5.6 %copy-start.2 = (bf16[32,8,768]{2,1,0:T(8,128)(2,1)S(1)}, bf16[32,8,768]{2,1,0:T(8,128)(2,1)}, u32[]{:S(2)}) copy-start(bf16[32,8,768]{2,1,0:T(8,128)(2,1)} %copy-done.1) | copy-start | bytes 1179652
  99.2 3.6 %copy-start.5 = (bf16[256,2304]{1,0:T(8,128)(2,1)}, bf16[256,2304]{1,0:T(8,128)(2,1)S(1)}, u32[]{:S(2)}) copy-start(bf16[256,2304]{1,0:T(8,128)(2,1)S(1)} %shard_map.117.dqkv_ref.d_ref) | copy-start | bytes 3538948
  99.2 4.4 %collective-permute-start.4 = (bf16[256,2304]{1,0:T(8,128)(2,1)S(1)}, bf16[256,2304]{1,0:T(8,128)(2,1)S(1)}, u32[]{:S(2)}, u32[]{:S(2)}) collective-permute-start(bf16[256,2304]{1,0:T(8,128)(2,1)S(1)} %shard_map.117.dqkv_ref.d_ref), channel_id=1, source_target_pairs={{0,1},{1,0},{2,3},{3,2},{4,5},{5,4},{6,7},{7,6},{8,9},{9,8},{10,11... | collective-permute-start | bytes 3538952 | tf_op jit(solution)/shard_map/ppermute | solution.py:307
  100.6 3.0 %collective-permute-start.5 = (bf16[256,768]{1,0:T(8,128)(2,1)S(1)}, bf16[256,768]{1,0:T(8,128)(2,1)S(1)}, u32[]{:S(2)}, u32[]{:S(2)}) collective-permute-start(bf16[256,768]{1,0:T(8,128)(2,1)S(1)} %bitcast.21), channel_id=1, source_target_pairs={{0,1},{1,0},{2,3},{3,2},{4,5},{5,4},{6,7},{7,6},{8,9},{9,8},{10,11... | collective-permute-start | bytes 1179656 | tf_op jit(solution)/shard_map/ppermute | solution.py:307
  103.6 1.2 copy-start.17
  103.6 1.1 copy-start.15
  104.8 24.3 %copy-start.8 = (s32[4]{0:T(128)S(1)}, s32[4]{0:T(128)}, u32[]{:S(2)}) copy-start(s32[4]{0:T(128)} %pad_add_fusion.pos_ref) | copy-start | bytes 52
  110.0 19.1 %copy-start.6 = (bf16[4,96,768]{2,1,0:T(8,128)(2,1)S(1)}, bf16[4,96,768]{2,1,0:T(8,128)(2,1)}, u32[]{:S(2)}) copy-start(bf16[4,96,768]{2,1,0:T(8,128)(2,1)} %get-tuple-element.73.refs_0_) | copy-start | bytes 1769476
  110.5 12.6 %collective-permute-start.6 = (bf16[4,96,768]{2,1,0:T(8,128)(2,1)}, bf16[4,96,768]{2,1,0:T(8,128)(2,1)}, u32[]{:S(2)}, u32[]{:S(2)}) collective-permute-start(bf16[4,96,768]{2,1,0:T(8,128)(2,1)} %get-tuple-element.74), channel_id=1, source_target_pairs={{0,64},{64,128},{128,192},{192,0},{8,72},{72,136},{136,200},{200,8... | collective-permute-start | bytes 1769480 | tf_op jit(solution)/shard_map/ppermute | solution.py:301
  111.5 17.2 %collective-permute-start.7 = (bf16[4,96,768]{2,1,0:T(8,128)(2,1)}, bf16[4,96,768]{2,1,0:T(8,128)(2,1)}, u32[]{:S(2)}, u32[]{:S(2)}) collective-permute-start(bf16[4,96,768]{2,1,0:T(8,128)(2,1)} %get-tuple-element.75), channel_id=1, source_target_pairs={{0,128},{64,192},{128,0},{192,64},{8,136},{72,200},{136,8},{200,72... | collective-permute-start | bytes 1769480 | tf_op jit(solution)/shard_map/ppermute | solution.py:301
  114.3 14.8 %collective-permute-start.8 = (bf16[4,96,768]{2,1,0:T(8,128)(2,1)}, bf16[4,96,768]{2,1,0:T(8,128)(2,1)}, u32[]{:S(2)}, u32[]{:S(2)}) collective-permute-start(bf16[4,96,768]{2,1,0:T(8,128)(2,1)} %get-tuple-element.76), channel_id=1, source_target_pairs={{0,192},{64,0},{128,64},{192,128},{8,200},{72,8},{136,72},{200,136... | collective-permute-start | bytes 1769480 | tf_op jit(solution)/shard_map/ppermute | solution.py:301
  115.6 28.4 %all-to-all-start.4 = ((bf16[32,8,768]{2,1,0:T(8,128)(2,1)}), bf16[32,8,768]{2,1,0:T(8,128)(2,1)S(1)}, u32[]{:S(2)}, u32[]{:S(2)}) async-start(bf16[32,8,768]{2,1,0:T(8,128)(2,1)} %bitcast.13), calls=%async_computation.4 | async-start | bytes 786432 | tf_op jit(solution)/shard_map/all_to_all | solution.py:275
  131.1 7.3 %collective-permute-start.9 = (bf16[96,1536]{1,0:T(8,128)(2,1)S(1)}, bf16[96,1536]{1,0:T(8,128)(2,1)S(1)}, u32[]{:S(2)}, u32[]{:S(2)}) collective-permute-start(bf16[96,1536]{1,0:T(8,128)(2,1)S(1)} %get-tuple-element.78), channel_id=1, source_target_pairs={{1,65},{65,129},{129,193},{193,1},{9,73},{73,137},{137,201},{201,9... | collective-permute-start | bytes 884744 | tf_op jit(solution)/shard_map/ppermute | solution.py:301
  132.4 8.5 %collective-permute-start.10 = (bf16[96,1536]{1,0:T(8,128)(2,1)S(1)}, bf16[96,1536]{1,0:T(8,128)(2,1)S(1)}, u32[]{:S(2)}, u32[]{:S(2)}) collective-permute-start(bf16[96,1536]{1,0:T(8,128)(2,1)S(1)} %get-tuple-element.79), channel_id=1, source_target_pairs={{1,129},{65,193},{129,1},{193,65},{9,137},{73,201},{137,9},{201,73... | collective-permute-start | bytes 884744 | tf_op jit(solution)/shard_map/ppermute | solution.py:301
  135.5 8.4 %collective-permute-start.11 = (bf16[96,1536]{1,0:T(8,128)(2,1)S(1)}, bf16[96,1536]{1,0:T(8,128)(2,1)S(1)}, u32[]{:S(2)}, u32[]{:S(2)}) collective-permute-start(bf16[96,1536]{1,0:T(8,128)(2,1)S(1)} %get-tuple-element.80), channel_id=1, source_target_pairs={{1,193},{65,1},{129,65},{193,129},{9,201},{73,9},{137,73},{201,137... | collective-permute-start | bytes 884744 | tf_op jit(solution)/shard_map/ppermute | solution.py:301
  160.9 13.9 %all-to-all-start.6 = ((bf16[8,24,1536]{2,1,0:T(8,128)(2,1)}), bf16[8,24,1536]{2,1,0:T(8,128)(2,1)S(1)}, u32[]{:S(2)}, u32[]{:S(2)}) async-start(bf16[8,24,1536]{2,1,0:T(8,128)(2,1)} %shard_map.123), calls=%async_computation.6 | async-start | bytes 1179648 | tf_op jit(solution)/shard_map/all_to_all | solution.py:275
  (4 other events, 3.2 us)

commit v5 on v4

--- a/solution.py
+++ b/solution.py
@@ -297,10 +297,11 @@
 
 
 def crossed_steps(pieces, first):
-    return [pieces[0]] + [
-        lax.ppermute(pieces[k], ("x", "y", "c"), [(ring[i], ring[(i + k) % 4]) for ring in rings(first) for i in range(4)])
-        for k in (1, 2, 3)
-    ]
+    steps = {0: pieces[0]}
+    for k in (2, 1, 3):
+        pairs = [(ring[i], ring[(i + k) % 4]) for ring in rings(first) for i in range(4)]
+        steps[k] = lax.ppermute(pieces[k], ("x", "y", "c"), pairs)
+    return [steps[k] for k in (0, 2, 1, 3)]
 
 
 def swap(x):

time: 177 us -> 175 us (0.989)
  waiting for transfers between devices: 46.6 us -> 44.6 us
  transfers between devices with their start and end apart: 18 -> 18, of which waited for: 12 -> 11; matrix products, arithmetic and copies ran while one was open for 0% -> 0% of each run, Pallas kernels for 17% -> 17%
where the time goes in v5:
time: 175 us; the launch traced here: 174 us
  starting transfers between devices  53.4 us (31%)
  Pallas kernels  51.2 us (29%)
  waiting for transfers between devices  44.6 us (25%)
  blocking collectives  16.4 us (9%)
  local copies, waits for them, and re-layouts  7.43 us (4%)
    pallas_call x16, Pallas kernels, call(): pl.pallas_call(kernel, out_shape=outs, in_specs=[SMEM if a.dtype == jnp.i...  51.2 us
    all_to_all x5, starting transfers between devices, a2a(): return lax.all_to_all(x, axes, 0, 0, tiled=True)  35.3 us
    all_to_all x5, waiting for transfers between devices, a2a(): return lax.all_to_all(x, axes, 0, 0, tiled=True)  29.1 us
    all_to_all x1, blocking collectives, a2a(): return lax.all_to_all(x, axes, 0, 0, tiled=True)  16.4 us
    ppermute x6, waiting for transfers between devices, crossed_steps(): steps[k] = lax.ppermute(pieces[k], ('x', 'y', 'c'), pairs)  12.5 us
    ppermute x6, starting transfers between devices, crossed_steps(): steps[k] = lax.ppermute(pieces[k], ('x', 'y', 'c'), pairs)  9.73 us
    unnamed x36, local copies, waits for them, and re-layouts  7.43 us
    all_to_all x1, starting transfers between devices, crossed(): lax.all_to_all(x, ('x', 'y', 'c'), 0, 0, tiled=True, axis_index_groups=ri...  4.99 us
  transfers between devices with their start and end apart: 18, of which 11 were waited for; matrix products, arithmetic and copies ran while one was open for 0% of the time, Pallas kernels for 17%

profile of v5, /device:TPU:8, one launch (start us, length us, event | category | flops | bytes accessed | tf_op | source)
XLA Modules:
  0.0 174.4 jit_solution(914487699002101260)
XLA Ops:
  2.6 11.7 %all-to-all-start = ((bf16[32,8,768]{2,1,0:T(8,128)(2,1)}), bf16[32,8,768]{2,1,0:T(8,128)(2,1)S(1)}, u32[]{:S(2)}, u32[]{:S(2)}) async-start(bf16[32,8,768]{2,1,0:T(8,128)(2,1)} %bitcast.1), calls=%async_computation | async-start | bytes 786432 | tf_op jit(solution)/shard_map/all_to_all | solution.py:275
  14.6 1.6 collective-permute-done.g2_ref
  16.2 12.0 %all-to-all-done = bf16[32,8,768]{2,1,0:T(8,128)(2,1)S(1)} async-done(((bf16[32,8,768]{2,1,0:T(8,128)(2,1)}), bf16[32,8,768]{2,1,0:T(8,128)(2,1)S(1)}, u32[]{:S(2)}, u32[]{:S(2)}) %all-to-all-start) | async-done | bytes 393248 | tf_op jit(solution)/shard_map/all_to_all | solution.py:275
  28.9 7.4 %shard_map.110 = (bf16[256,768]{1,0:T(8,128)(2,1)}, bf16[256,2304]{1,0:T(8,128)(2,1)}, bf16[256,768]{1,0:T(8,128)(2,1)}, bf16[256,768]{1,0:T(8,128)(2,1)}) custom-call(bf16[256,768]{1,0:T(8,128)(2,1)} %bitcast.17, bf16[768,2304]{1,0:T(8,128)(2,1)} %wq_ref.5, bf16[768,768]{1,0:T(8,128)(2,1)} %wo_ref.7), custom_call_target="tpu_custom_call" | custom-call | flops 1207959552 | bytes 7471104 | tf_op jit(solution)/shard_map/pallas_call | solution.py:255
  36.2 6.4 %all-to-all-start.1 = ((bf16[32,8,768]{2,1,0:T(8,128)(2,1)}), bf16[32,8,768]{2,1,0:T(8,128)(2,1)S(1)}, u32[]{:S(2)}, u32[]{:S(2)}) async-start(bf16[32,8,768]{2,1,0:T(8,128)(2,1)} %bitcast.32), calls=%async_computation.1 | async-start | bytes 786432 | tf_op jit(solution)/shard_map/all_to_all | solution.py:275
  43.3 2.7 %shard_map.111 = (bf16[2,384,256]{2,1,0:T(8,128)(2,1)}, bf16[2,384,256]{2,1,0:T(8,128)(2,1)}) custom-call(s32[4]{0:T(128)} %pad_add_fusion.pos_ref, bf16[256,768]{1,0:T(8,128)(2,1)} %get-tuple-element.49.low_ref, bf16[256,768]{1,0:T(8,128)(2,1)} %get-tuple-element.50.mixed_ref), custom_call_target="tpu_custom_call" | custom-call | flops 603979776 | bytes 1572880 | tf_op jit(solution)/shard_map/pallas_call | solution.py:255
  46.1 2.6 %shard_map.112.g_ref = bf16[256,768]{1,0:T(8,128)(2,1)} custom-call(bf16[256,768]{1,0:T(8,128)(2,1)} %bitcast.26, bf16[768,768]{1,0:T(8,128)(2,1)} %wo_ref.6), custom_call_target="tpu_custom_call" | custom-call | flops 301989888 | bytes 1966080 | tf_op jit(solution)/shard_map/pallas_call | solution.py:255
  48.8 7.6 %all-to-all-done.1 = bf16[32,8,768]{2,1,0:T(8,128)(2,1)S(1)} async-done(((bf16[32,8,768]{2,1,0:T(8,128)(2,1)}), bf16[32,8,768]{2,1,0:T(8,128)(2,1)S(1)}, u32[]{:S(2)}, u32[]{:S(2)}) %all-to-all-start.1) | async-done | bytes 393248 | tf_op jit(solution)/shard_map/all_to_all | solution.py:275
  57.2 10.7 %shard_map.113 = (bf16[256,768]{1,0:T(8,128)(2,1)}, bf16[256,2304]{1,0:T(8,128)(2,1)}, bf16[256,768]{1,0:T(8,128)(2,1)}, bf16[256,768]{1,0:T(8,128)(2,1)}, bf16[256,768]{1,0:T(8,128)(2,1)}) custom-call(bf16[256,768]{1,0:T(8,128)(2,1)} %bitcast.31, bf16[256,768]{1,0:T(8,128)(2,1)} %bitcast.27, bf16[256,768]{1,0:T(8,128)(2,1)} %shard_map.112.g_ref, ...), custom_call_target="tpu_custom_call" | custom-call | flops 1811939328 | bytes 7471104 | tf_op jit(solution)/shard_map/pallas_call | solution.py:255
  67.8 1.4 collective-permute-start.3
  69.2 5.1 %all-to-all-start.2 = ((bf16[32,8,768]{2,1,0:T(8,128)(2,1)}), bf16[32,8,768]{2,1,0:T(8,128)(2,1)S(1)}, u32[]{:S(2)}, u32[]{:S(2)}) async-start(bf16[32,8,768]{2,1,0:T(8,128)(2,1)} %bitcast.33), calls=%async_computation.2 | async-start | bytes 786432 | tf_op jit(solution)/shard_map/all_to_all | solution.py:275
  74.3 2.7 %shard_map.115 = (bf16[2,384,256]{2,1,0:T(8,128)(2,1)}, bf16[2,384,256]{2,1,0:T(8,128)(2,1)}) custom-call(s32[4]{0:T(128)} %pad_add_fusion.pos_ref, bf16[256,768]{1,0:T(8,128)(2,1)} %get-tuple-element.57.low_ref, bf16[256,768]{1,0:T(8,128)(2,1)} %get-tuple-element.56.mixed_ref), custom_call_target="tpu_custom_call" | custom-call | flops 603979776 | bytes 1572880 | tf_op jit(solution)/shard_map/pallas_call | solution.py:255
  77.2 2.7 %shard_map.114 = bf16[256,768]{1,0:T(8,128)(2,1)} custom-call(bf16[256,768]{1,0:T(8,128)(2,1)} %get-tuple-element.55.x_ref, bf16[256,768]{1,0:T(8,128)(2,1)} %get-tuple-element.56.mixed_ref, bf16[768,768]{1,0:T(8,128)(2,1)} %wo_ref.6), custom_call_target="tpu_custom_call" | custom-call | flops 301989888 | bytes 2359296 | tf_op jit(solution)/shard_map/pallas_call | solution.py:255
  81.1 5.1 %shard_map.116 = bf16[4,4,96,768]{3,2,1,0:T(8,128)(2,1)} custom-call(s32[4]{0:T(128)} %pad_add_fusion.pos_ref, bf16[2,384,256]{2,1,0:T(8,128)(2,1)} %get-tuple-element.58.l_ref, bf16[2,384,256]{2,1,0:T(8,128)(2,1)} %copy-done.13, bf16[256,2304]{1,0:T(8,128)(2,1)} %get-tuple-element.60.d_ref, bf16[256,2304]{1,0:T(8,128)(2,1)} %copy-done.11, ...), custom_call_target="tpu_custom_call" | custom-call | flops 1207959552 | bytes 6291472 | tf_op jit(solution)/shard_map/pallas_call | solution.py:255
  86.2 1.3 all-to-all-done.2
  87.6 5.0 %all-to-all-start.3 = ((bf16[4,4,96,768]{3,2,1,0:T(8,128)(2,1)}), bf16[4,4,96,768]{3,2,1,0:T(8,128)(2,1)S(1)}, u32[]{:S(2)}, u32[]{:S(2)}) async-start(bf16[4,4,96,768]{3,2,1,0:T(8,128)(2,1)} %shard_map.116), calls=%async_computation.3 | async-start | bytes 4718592 | tf_op jit(solution)/shard_map/all_to_all | solution.py:296
  95.1 4.1 %shard_map.117.dqkv_ref.d_ref = bf16[256,2304]{1,0:T(8,128)(2,1)S(1)} custom-call(bf16[256,768]{1,0:T(8,128)(2,1)S(1)} %bitcast.20, bf16[256,2304]{1,0:T(8,128)(2,1)S(1)} %copy-done.9, bf16[768,768]{1,0:T(8,128)(2,1)S(1)} %copy-done.4), custom_call_target="tpu_custom_call" | custom-call | flops 1207959552 | bytes 3932160 | tf_op jit(solution)/shard_map/pallas_call | solution.py:255
  99.2 1.4 collective-permute-start.4
  100.7 2.1 %shard_map.118 = bf16[256,768]{1,0:T(8,128)(2,1)} custom-call(bf16[256,768]{1,0:T(8,128)(2,1)S(1)} %bitcast.18, bf16[256,768]{1,0:T(8,128)(2,1)S(1)} %bitcast.22, bf16[256,2304]{1,0:T(8,128)(2,1)S(1)} %shard_map.117.dqkv_ref.d_ref, bf16[768,2304]{1,0:T(8,128)(2,1)S(1)} %copy-done), custom_call_target="tpu_custom_call" | custom-call | flops 905969664 | bytes 5898240 | tf_op jit(solution)/shard_map/pallas_call | solution.py:255
  104.8 5.2 %shard_map.119 = (bf16[4,96,768]{2,1,0:T(8,128)(2,1)}, bf16[4,96,768]{2,1,0:T(8,128)(2,1)}, bf16[4,96,768]{2,1,0:T(8,128)(2,1)}, bf16[4,96,768]{2,1,0:T(8,128)(2,1)}) custom-call(s32[4]{0:T(128)} %pad_add_fusion.pos_ref, bf16[2,384,256]{2,1,0:T(8,128)(2,1)} %get-tuple-element.66.l_ref, bf16[2,384,256]{2,1,0:T(8,128)(2,1)} %copy-done.16, ...), custom_call_target="tpu_custom_call" | custom-call | flops 1207959552 | bytes 6291472 | tf_op jit(solution)/shard_map/pallas_call | solution.py:255
  110.5 2.5 %collective-permute-start.6 = (bf16[4,96,768]{2,1,0:T(8,128)(2,1)}, bf16[4,96,768]{2,1,0:T(8,128)(2,1)}, u32[]{:S(2)}, u32[]{:S(2)}) collective-permute-start(bf16[4,96,768]{2,1,0:T(8,128)(2,1)} %get-tuple-element.74), channel_id=1, source_target_pairs={{0,128},{64,192},{128,0},{192,64},{8,136},{72,200},{136,8},{200,72... | collective-permute-start | bytes 1769480 | tf_op jit(solution)/shard_map/ppermute | solution.py:303
  113.7 2.5 %collective-permute-start.8 = (bf16[4,96,768]{2,1,0:T(8,128)(2,1)}, bf16[4,96,768]{2,1,0:T(8,128)(2,1)}, u32[]{:S(2)}, u32[]{:S(2)}) collective-permute-start(bf16[4,96,768]{2,1,0:T(8,128)(2,1)} %get-tuple-element.76), channel_id=1, source_target_pairs={{0,192},{64,0},{128,64},{192,128},{8,200},{72,8},{136,72},{200,136... | collective-permute-start | bytes 1769480 | tf_op jit(solution)/shard_map/ppermute | solution.py:303
  116.2 7.5 %all-to-all-start.4 = ((bf16[32,8,768]{2,1,0:T(8,128)(2,1)}), bf16[32,8,768]{2,1,0:T(8,128)(2,1)S(1)}, u32[]{:S(2)}, u32[]{:S(2)}) async-start(bf16[32,8,768]{2,1,0:T(8,128)(2,1)} %bitcast.13), calls=%async_computation.4 | async-start | bytes 786432 | tf_op jit(solution)/shard_map/all_to_all | solution.py:275
  123.7 4.8 %collective-permute-done.7.refs_2_ = bf16[4,96,768]{2,1,0:T(8,128)(2,1)} collective-permute-done((bf16[4,96,768]{2,1,0:T(8,128)(2,1)}, bf16[4,96,768]{2,1,0:T(8,128)(2,1)}, u32[]{:S(2)}, u32[]{:S(2)}) %collective-permute-start.7) | collective-permute-done | bytes 589856 | tf_op jit(solution)/shard_map/ppermute | solution.py:303
  128.5 2.0 %shard_map.120 = (bf16[96,1536]{1,0:T(8,128)(2,1)S(1)}, bf16[96,1536]{1,0:T(8,128)(2,1)S(1)}, bf16[96,1536]{1,0:T(8,128)(2,1)S(1)}, bf16[96,1536]{1,0:T(8,128)(2,1)S(1)}) custom-call(s32[4]{0:T(128)S(1)} %copy-done.8, bf16[4,4,96,768]{3,2,1,0:T(8,128)(2,1)S(1)} %all-to-all-done.3.s_ref, bf16[4,96,768]{2,1,0:T(8,128)(2,1)S(1)} %copy-done.6, ...), custom_call_target="tpu_custom_call" | custom-call | tf_op jit(solution)/shard_map/pallas_call | solution.py:255
  130.5 2.0 %collective-permute-start.9 = (bf16[96,1536]{1,0:T(8,128)(2,1)S(1)}, bf16[96,1536]{1,0:T(8,128)(2,1)S(1)}, u32[]{:S(2)}, u32[]{:S(2)}) collective-permute-start(bf16[96,1536]{1,0:T(8,128)(2,1)S(1)} %get-tuple-element.78), channel_id=1, source_target_pairs={{1,129},{65,193},{129,1},{193,65},{9,137},{73,201},{137,9},{201,73... | collective-permute-start | bytes 884744 | tf_op jit(solution)/shard_map/ppermute | solution.py:303
  132.5 1.8 %collective-permute-start.10 = (bf16[96,1536]{1,0:T(8,128)(2,1)S(1)}, bf16[96,1536]{1,0:T(8,128)(2,1)S(1)}, u32[]{:S(2)}, u32[]{:S(2)}) collective-permute-start(bf16[96,1536]{1,0:T(8,128)(2,1)S(1)} %get-tuple-element.79), channel_id=1, source_target_pairs={{1,65},{65,129},{129,193},{193,1},{9,73},{73,137},{137,201},{201,9... | collective-permute-start | bytes 884744 | tf_op jit(solution)/shard_map/ppermute | solution.py:303
  134.5 4.7 %collective-permute-done.9.refs_1_ = bf16[96,1536]{1,0:T(8,128)(2,1)S(1)} collective-permute-done((bf16[96,1536]{1,0:T(8,128)(2,1)S(1)}, bf16[96,1536]{1,0:T(8,128)(2,1)S(1)}, u32[]{:S(2)}, u32[]{:S(2)}) %collective-permute-start.9) | collective-permute-done | bytes 294944 | tf_op jit(solution)/shard_map/ppermute | solution.py:303
  139.2 2.9 %collective-permute-done.10.refs_2_ = bf16[96,1536]{1,0:T(8,128)(2,1)S(1)} collective-permute-done((bf16[96,1536]{1,0:T(8,128)(2,1)S(1)}, bf16[96,1536]{1,0:T(8,128)(2,1)S(1)}, u32[]{:S(2)}, u32[]{:S(2)}) %collective-permute-start.10) | collective-permute-done | bytes 294944 | tf_op jit(solution)/shard_map/ppermute | solution.py:303
  142.4 16.4 %all_to_all.63.got_ref = bf16[4,24,1536]{2,1,0:T(8,128)(2,1)S(1)} all-to-all(bf16[4,24,1536]{2,1,0:T(8,128)(2,1)S(1)} %bitcast.24), channel_id=1, replica_groups=mesh['x'=4,'zl'=2,'y'=4,'zh'=4,'c'=2] {'zh'}, dimensions={0} | all-to-all | bytes 589824 | tf_op jit(solution)/shard_map/all_to_all | solution.py:275
  159.7 4.5 %all-to-all-start.6 = ((bf16[8,24,1536]{2,1,0:T(8,128)(2,1)}), bf16[8,24,1536]{2,1,0:T(8,128)(2,1)S(1)}, u32[]{:S(2)}, u32[]{:S(2)}) async-start(bf16[8,24,1536]{2,1,0:T(8,128)(2,1)} %shard_map.123), calls=%async_computation.6 | async-start | bytes 1179648 | tf_op jit(solution)/shard_map/all_to_all | solution.py:275
  165.3 8.2 %all-to-all-done.6.got_ref = bf16[8,24,1536]{2,1,0:T(8,128)(2,1)S(1)} async-done(((bf16[8,24,1536]{2,1,0:T(8,128)(2,1)}), bf16[8,24,1536]{2,1,0:T(8,128)(2,1)S(1)}, u32[]{:S(2)}, u32[]{:S(2)}) %all-to-all-start.6) | async-done | bytes 589856 | tf_op jit(solution)/shard_map/all_to_all | solution.py:275
  (58 shorter events, 15.1 us)
Async XLA Ops:
  1.6 12.7 %copy-start.10 = (bf16[1,2,128,768]{3,2,1,0:T(8,128)(2,1)S(1)}, bf16[1,2,128,768]{3,2,1,0:T(8,128)(2,1)}, u32[]{:S(2)}) copy-start(bf16[1,2,128,768]{3,2,1,0:T(8,128)(2,1)} %param.7) | copy-start | bytes 1179652
  2.6 25.5 %all-to-all-start = ((bf16[32,8,768]{2,1,0:T(8,128)(2,1)}), bf16[32,8,768]{2,1,0:T(8,128)(2,1)S(1)}, u32[]{:S(2)}, u32[]{:S(2)}) async-start(bf16[32,8,768]{2,1,0:T(8,128)(2,1)} %bitcast.1), calls=%async_computation | async-start | bytes 786432 | tf_op jit(solution)/shard_map/all_to_all | solution.py:275
  14.4 1.8 %collective-permute-start = (bf16[256,768]{1,0:T(8,128)(2,1)S(1)}, bf16[256,768]{1,0:T(8,128)(2,1)S(1)}, u32[]{:S(2)}, u32[]{:S(2)}) collective-permute-start(bf16[256,768]{1,0:T(8,128)(2,1)S(1)} %bitcast.29), channel_id=1, source_target_pairs={{0,1},{1,0},{2,3},{3,2},{4,5},{5,4},{6,7},{7,6},{8,9},{9,8},{10,11... | collective-permute-start | bytes 1179656 | tf_op jit(solution)/shard_map/ppermute | solution.py:308
  16.2 29.8 %copy-start.12 = (bf16[256,768]{1,0:T(8,128)(2,1)}, bf16[256,768]{1,0:T(8,128)(2,1)S(1)}, u32[]{:S(2)}) copy-start(bf16[256,768]{1,0:T(8,128)(2,1)S(1)} %collective-permute-done.g2_ref) | copy-start | bytes 1179652
  36.2 20.2 %all-to-all-start.1 = ((bf16[32,8,768]{2,1,0:T(8,128)(2,1)}), bf16[32,8,768]{2,1,0:T(8,128)(2,1)S(1)}, u32[]{:S(2)}, u32[]{:S(2)}) async-start(bf16[32,8,768]{2,1,0:T(8,128)(2,1)} %bitcast.32), calls=%async_computation.1 | async-start | bytes 786432 | tf_op jit(solution)/shard_map/all_to_all | solution.py:275
  46.0 2.8 %collective-permute-start.1 = (bf16[2,384,256]{2,1,0:T(8,128)(2,1)}, bf16[2,384,256]{2,1,0:T(8,128)(2,1)S(1)}, u32[]{:S(2)}, u32[]{:S(2)}) collective-permute-start(bf16[2,384,256]{2,1,0:T(8,128)(2,1)} %get-tuple-element.51), channel_id=1, source_target_pairs={{0,1},{1,0},{2,3},{3,2},{4,5},{5,4},{6,7},{7,6},{8,9},{9,8},{10,11... | collective-permute-start | bytes 1179656 | tf_op jit(solution)/shard_map/ppermute | solution.py:308
  48.8 20.4 %copy-start.16 = (bf16[2,384,256]{2,1,0:T(8,128)(2,1)}, bf16[2,384,256]{2,1,0:T(8,128)(2,1)S(1)}, u32[]{:S(2)}) copy-start(bf16[2,384,256]{2,1,0:T(8,128)(2,1)S(1)} %collective-permute-done.1.l2_ref) | copy-start | bytes 1179652
  67.8 12.1 %collective-permute-start.3 = (bf16[256,2304]{1,0:T(8,128)(2,1)}, bf16[256,2304]{1,0:T(8,128)(2,1)S(1)}, u32[]{:S(2)}, u32[]{:S(2)}) collective-permute-start(bf16[256,2304]{1,0:T(8,128)(2,1)} %get-tuple-element.60.d_ref), channel_id=1, source_target_pairs={{0,1},{1,0},{2,3},{3,2},{4,5},{5,4},{6,7},{7,6},{8,9},{9,8},{10,11... | collective-permute-start | bytes 3538952 | tf_op jit(solution)/shard_map/ppermute | solution.py:308
  69.2 18.4 %all-to-all-start.2 = ((bf16[32,8,768]{2,1,0:T(8,128)(2,1)}), bf16[32,8,768]{2,1,0:T(8,128)(2,1)S(1)}, u32[]{:S(2)}, u32[]{:S(2)}) async-start(bf16[32,8,768]{2,1,0:T(8,128)(2,1)} %bitcast.33), calls=%async_computation.2 | async-start | bytes 786432 | tf_op jit(solution)/shard_map/all_to_all | solution.py:275
  77.0 2.9 %collective-permute-start.2 = (bf16[2,384,256]{2,1,0:T(8,128)(2,1)}, bf16[2,384,256]{2,1,0:T(8,128)(2,1)S(1)}, u32[]{:S(2)}, u32[]{:S(2)}) collective-permute-start(bf16[2,384,256]{2,1,0:T(8,128)(2,1)} %get-tuple-element.59), channel_id=1, source_target_pairs={{0,1},{1,0},{2,3},{3,2},{4,5},{5,4},{6,7},{7,6},{8,9},{9,8},{10,11... | collective-permute-start | bytes 1179656 | tf_op jit(solution)/shard_map/ppermute | solution.py:308
  79.9 1.2 copy-start.11
  87.6 13.1 %copy-start.3 = (bf16[32,8,768]{2,1,0:T(8,128)(2,1)}, bf16[32,8,768]{2,1,0:T(8,128)(2,1)S(1)}, u32[]{:S(2)}) copy-start(bf16[32,8,768]{2,1,0:T(8,128)(2,1)S(1)} %all-to-all-done.2) | copy-start | bytes 1179652
  87.6 22.9 %all-to-all-start.3 = ((bf16[4,4,96,768]{3,2,1,0:T(8,128)(2,1)}), bf16[4,4,96,768]{3,2,1,0:T(8,128)(2,1)S(1)}, u32[]{:S(2)}, u32[]{:S(2)}) async-start(bf16[4,4,96,768]{3,2,1,0:T(8,128)(2,1)} %shard_map.116), calls=%async_computation.3 | async-start | bytes 4718592 | tf_op jit(solution)/shard_map/all_to_all | solution.py:296
  92.6 1.3 copy-start.4
  93.8 1.3 copy-start.9
  95.1 5.6 %copy-start = (bf16[768,2304]{1,0:T(8,128)(2,1)S(1)}, bf16[768,2304]{1,0:T(8,128)(2,1)}, u32[]{:S(2)}) copy-start(bf16[768,2304]{1,0:T(8,128)(2,1)} %wq_ref.5) | copy-start | bytes 10616836
  95.1 5.6 %copy-start.2 = (bf16[32,8,768]{2,1,0:T(8,128)(2,1)S(1)}, bf16[32,8,768]{2,1,0:T(8,128)(2,1)}, u32[]{:S(2)}) copy-start(bf16[32,8,768]{2,1,0:T(8,128)(2,1)} %copy-done.1) | copy-start | bytes 1179652
  99.2 3.6 %copy-start.5 = (bf16[256,2304]{1,0:T(8,128)(2,1)}, bf16[256,2304]{1,0:T(8,128)(2,1)S(1)}, u32[]{:S(2)}) copy-start(bf16[256,2304]{1,0:T(8,128)(2,1)S(1)} %shard_map.117.dqkv_ref.d_ref) | copy-start | bytes 3538948
  99.2 4.4 %collective-permute-start.4 = (bf16[256,2304]{1,0:T(8,128)(2,1)S(1)}, bf16[256,2304]{1,0:T(8,128)(2,1)S(1)}, u32[]{:S(2)}, u32[]{:S(2)}) collective-permute-start(bf16[256,2304]{1,0:T(8,128)(2,1)S(1)} %shard_map.117.dqkv_ref.d_ref), channel_id=1, source_target_pairs={{0,1},{1,0},{2,3},{3,2},{4,5},{5,4},{6,7},{7,6},{8,9},{9,8},{10,11... | collective-permute-start | bytes 3538952 | tf_op jit(solution)/shard_map/ppermute | solution.py:308
  100.6 3.0 %collective-permute-start.5 = (bf16[256,768]{1,0:T(8,128)(2,1)S(1)}, bf16[256,768]{1,0:T(8,128)(2,1)S(1)}, u32[]{:S(2)}, u32[]{:S(2)}) collective-permute-start(bf16[256,768]{1,0:T(8,128)(2,1)S(1)} %bitcast.21), channel_id=1, source_target_pairs={{0,1},{1,0},{2,3},{3,2},{4,5},{5,4},{6,7},{7,6},{8,9},{9,8},{10,11... | collective-permute-start | bytes 1179656 | tf_op jit(solution)/shard_map/ppermute | solution.py:308
  103.6 1.2 copy-start.17
  103.6 1.1 copy-start.15
  104.8 23.7 %copy-start.8 = (s32[4]{0:T(128)S(1)}, s32[4]{0:T(128)}, u32[]{:S(2)}) copy-start(s32[4]{0:T(128)} %pad_add_fusion.pos_ref) | copy-start | bytes 52
  110.0 18.5 %copy-start.6 = (bf16[4,96,768]{2,1,0:T(8,128)(2,1)S(1)}, bf16[4,96,768]{2,1,0:T(8,128)(2,1)}, u32[]{:S(2)}) copy-start(bf16[4,96,768]{2,1,0:T(8,128)(2,1)} %get-tuple-element.73.refs_0_) | copy-start | bytes 1769476
  110.5 13.3 %collective-permute-start.6 = (bf16[4,96,768]{2,1,0:T(8,128)(2,1)}, bf16[4,96,768]{2,1,0:T(8,128)(2,1)}, u32[]{:S(2)}, u32[]{:S(2)}) collective-permute-start(bf16[4,96,768]{2,1,0:T(8,128)(2,1)} %get-tuple-element.74), channel_id=1, source_target_pairs={{0,128},{64,192},{128,0},{192,64},{8,136},{72,200},{136,8},{200,72... | collective-permute-start | bytes 1769480 | tf_op jit(solution)/shard_map/ppermute | solution.py:303
  113.0 15.5 %collective-permute-start.7 = (bf16[4,96,768]{2,1,0:T(8,128)(2,1)}, bf16[4,96,768]{2,1,0:T(8,128)(2,1)}, u32[]{:S(2)}, u32[]{:S(2)}) collective-permute-start(bf16[4,96,768]{2,1,0:T(8,128)(2,1)} %get-tuple-element.75), channel_id=1, source_target_pairs={{0,64},{64,128},{128,192},{192,0},{8,72},{72,136},{136,200},{200,8... | collective-permute-start | bytes 1769480 | tf_op jit(solution)/shard_map/ppermute | solution.py:303
  113.7 14.8 %collective-permute-start.8 = (bf16[4,96,768]{2,1,0:T(8,128)(2,1)}, bf16[4,96,768]{2,1,0:T(8,128)(2,1)}, u32[]{:S(2)}, u32[]{:S(2)}) collective-permute-start(bf16[4,96,768]{2,1,0:T(8,128)(2,1)} %get-tuple-element.76), channel_id=1, source_target_pairs={{0,192},{64,0},{128,64},{192,128},{8,200},{72,8},{136,72},{200,136... | collective-permute-start | bytes 1769480 | tf_op jit(solution)/shard_map/ppermute | solution.py:303
  116.2 26.2 %all-to-all-start.4 = ((bf16[32,8,768]{2,1,0:T(8,128)(2,1)}), bf16[32,8,768]{2,1,0:T(8,128)(2,1)S(1)}, u32[]{:S(2)}, u32[]{:S(2)}) async-start(bf16[32,8,768]{2,1,0:T(8,128)(2,1)} %bitcast.13), calls=%async_computation.4 | async-start | bytes 786432 | tf_op jit(solution)/shard_map/all_to_all | solution.py:275
  130.5 8.7 %collective-permute-start.9 = (bf16[96,1536]{1,0:T(8,128)(2,1)S(1)}, bf16[96,1536]{1,0:T(8,128)(2,1)S(1)}, u32[]{:S(2)}, u32[]{:S(2)}) collective-permute-start(bf16[96,1536]{1,0:T(8,128)(2,1)S(1)} %get-tuple-element.78), channel_id=1, source_target_pairs={{1,129},{65,193},{129,1},{193,65},{9,137},{73,201},{137,9},{201,73... | collective-permute-start | bytes 884744 | tf_op jit(solution)/shard_map/ppermute | solution.py:303
  132.5 9.6 %collective-permute-start.10 = (bf16[96,1536]{1,0:T(8,128)(2,1)S(1)}, bf16[96,1536]{1,0:T(8,128)(2,1)S(1)}, u32[]{:S(2)}, u32[]{:S(2)}) collective-permute-start(bf16[96,1536]{1,0:T(8,128)(2,1)S(1)} %get-tuple-element.79), channel_id=1, source_target_pairs={{1,65},{65,129},{129,193},{193,1},{9,73},{73,137},{137,201},{201,9... | collective-permute-start | bytes 884744 | tf_op jit(solution)/shard_map/ppermute | solution.py:303
  134.3 7.9 %collective-permute-start.11 = (bf16[96,1536]{1,0:T(8,128)(2,1)S(1)}, bf16[96,1536]{1,0:T(8,128)(2,1)S(1)}, u32[]{:S(2)}, u32[]{:S(2)}) collective-permute-start(bf16[96,1536]{1,0:T(8,128)(2,1)S(1)} %get-tuple-element.80), channel_id=1, source_target_pairs={{1,193},{65,1},{129,65},{193,129},{9,201},{73,9},{137,73},{201,137... | collective-permute-start | bytes 884744 | tf_op jit(solution)/shard_map/ppermute | solution.py:303
  159.7 13.8 %all-to-all-start.6 = ((bf16[8,24,1536]{2,1,0:T(8,128)(2,1)}), bf16[8,24,1536]{2,1,0:T(8,128)(2,1)S(1)}, u32[]{:S(2)}, u32[]{:S(2)}) async-start(bf16[8,24,1536]{2,1,0:T(8,128)(2,1)} %shard_map.123), calls=%async_computation.6 | async-start | bytes 1179648 | tf_op jit(solution)/shard_map/all_to_all | solution.py:275
  (4 other events, 3.2 us)
